TPU v7x, 32 devices: a whole 2x2x4 slice. The times are simulated.
32 devices in a mesh: dp: 8 (over y, x, core), section: 4 (over z).
Axes of the slice: x: 2, y: 2, z: 4, core: 2. Of those that a mesh axis runs over, the one named last changes fastest.
Arguments:
- clean_lat: float32 [8, 16, 256, 8], P('dp', None, 'section'), may hold values from -6 to 6
- noise_lat: float32 [8, 16, 256, 8], P('dp', None, 'section'), may hold values from -6 to 6
- column_ids: int32 [8, 256], P('dp'), may hold values from 0 to 4, as said below
- timesteps: int32 [8, 4], P('dp'), may hold values from 0 to 999
- clap_emb: float32 [8, 4, 512], P('dp'), may hold values from -6 to 6
- conv_w: float32 [2, 2304, 256], P(None, 'dp'), may hold values from -0.125 to 0.125
- proj_w: float32 [256, 2048], P(None, 'dp')
- film_w: float32 [512, 512], P(None, 'dp'), may hold values from -0.25 to 0.25
- skip_w: float32 [512, 256], P(None, 'dp'), may hold values from -0.25 to 0.25
- down_w: float32 [1024, 256], P('dp'), may hold values from -0.1875 to 0.1875
- stem_w: float32 [72, 256], P(None, 'dp'), may hold values from -0.75 to 0.75
- head_w: float32 [2304, 8], P('dp'), may hold values from -0.125 to 0.125
- gains: float32 [8, 256], P(None, 'dp'), may hold values from 0.5 to 1.5
- conv_m: float32 [2, 2304, 256], P(None, 'dp'), may hold values from -7.6293945e-06 to 7.6293945e-06
- proj_m: float32 [256, 2048], P(None, 'dp'), may hold values from -7.6293945e-06 to 7.6293945e-06
- film_m: float32 [512, 512], P(None, 'dp'), may hold values from -7.6293945e-06 to 7.6293945e-06
- skip_m: float32 [512, 256], P(None, 'dp'), may hold values from -7.6293945e-06 to 7.6293945e-06
- down_m: float32 [1024, 256], P('dp'), may hold values from -7.6293945e-06 to 7.6293945e-06
- stem_m: float32 [72, 256], P(None, 'dp'), may hold values from -7.6293945e-06 to 7.6293945e-06
- head_m: float32 [2304, 8], P('dp'), may hold values from -7.6293945e-06 to 7.6293945e-06
- gains_m: float32 [8, 256], P(None, 'dp'), may hold values from -9.1552734e-05 to 9.1552734e-05
- conv_v: float32 [2, 2304, 256], P(None, 'dp'), may hold values from 1.6679121e-13 to 6.6716484e-13
- proj_v: float32 [256, 2048], P(None, 'dp'), may hold values from 1.6679121e-13 to 6.6716484e-13
- film_v: float32 [512, 512], P(None, 'dp'), may hold values from 1.6679121e-13 to 6.6716484e-13
- skip_v: float32 [512, 256], P(None, 'dp'), may hold values from 1.6679121e-13 to 6.6716484e-13
- down_v: float32 [1024, 256], P('dp'), may hold values from 1.6679121e-13 to 6.6716484e-13
- stem_v: float32 [72, 256], P(None, 'dp'), may hold values from 1.6679121e-13 to 6.6716484e-13
- head_v: float32 [2304, 8], P('dp'), may hold values from 1.6679121e-13 to 6.6716484e-13
- gains_v: float32 [8, 256], P(None, 'dp'), may hold values from 1.667912e-11 to 6.671648e-11
Outputs:
- conv_new: float32 [2, 2304, 256], P(None, 'dp')
- proj_new: float32 [256, 2048], P(None, 'dp')
- film_new: float32 [512, 512], P(None, 'dp')
- skip_new: float32 [512, 256], P(None, 'dp')
- down_new: float32 [1024, 256], P('dp')
- stem_new: float32 [72, 256], P(None, 'dp')
- head_new: float32 [2304, 8], P('dp')
- gains_new: float32 [8, 256], P(None, 'dp')
- conv_m_new: float32 [2, 2304, 256], P(None, 'dp')
- proj_m_new: float32 [256, 2048], P(None, 'dp')
- film_m_new: float32 [512, 512], P(None, 'dp')
- skip_m_new: float32 [512, 256], P(None, 'dp')
- down_m_new: float32 [1024, 256], P('dp')
- stem_m_new: float32 [72, 256], P(None, 'dp')
- head_m_new: float32 [2304, 8], P('dp')
- gains_m_new: float32 [8, 256], P(None, 'dp')
- conv_v_new: float32 [2, 2304, 256], P(None, 'dp')
- proj_v_new: float32 [256, 2048], P(None, 'dp')
- film_v_new: float32 [512, 512], P(None, 'dp')
- skip_v_new: float32 [512, 256], P(None, 'dp')
- down_v_new: float32 [1024, 256], P('dp')
- stem_v_new: float32 [72, 256], P(None, 'dp')
- head_v_new: float32 [2304, 8], P('dp')
- gains_v_new: float32 [8, 256], P(None, 'dp')
- grad_norm: float32 [], replicated
- loss_sum: float32 [], replicated
- pix_count: float32 [], replicated
Inputs may be any that keep to these rules, and one draw needn't show every extreme that they name: `column_ids`: along a row the ids never fall: 4 clips of one or more columns in order, then one or more padding columns marked 4.
All inputs are finite; a program needn't handle non-finite values.
Results may differ from a plain program's by a relative error of at most 0.00095.
The roundings to bfloat16 on the way count: a program that leaves them out, or rounds other values in their place, can miss the bound.
Values may be sent and summed in bfloat16 or wider, within the bound.
A program may use at most 192 MiB of HBM per device.

v0:
```python
import math

import jax
import jax.numpy as jnp
from jax import lax
from jax.sharding import PartitionSpec as P

CIN = 8
C = 256
HEADS = 8
HD = 32
COND = 512
GROUPS = 32
CLIPS = 4
STEP = 10


EPS_NORM = 1e-05
CLIP_NORM = 0.02
RATE = 0.04
BETA_ONE = 0.9
BETA_TWO = 0.999
ADAM_EPS = 1e-08
DECAY = 0.1


def with_halo(cells, sides, width):
    for axis, dim in sides:
        count = lax.axis_size(axis)
        ends = count - 1
        head = lax.slice_in_dim(cells, 0, width, axis=dim)
        tail = lax.slice_in_dim(cells, cells.shape[dim] - width, cells.shape[dim], axis=dim)
        cells = jnp.concatenate(
            [
                lax.ppermute(tail, axis, [(i, (i + 1) % count) for i in range(ends)]),
                cells,
                lax.ppermute(head, axis, [((i + 1) % count, i) for i in range(ends)]),
            ],
            axis=dim,
        )
    return cells


def matmul(lhs_mat, rhs_mat):
    return jnp.dot(lhs_mat, rhs_mat, preferred_element_type=jnp.float32)


def left_product(lhs_mat, rhs_mat):
    return lax.dot_general(
        lhs_mat, rhs_mat, (((0,), (0,)), ((), ())), preferred_element_type=jnp.float32
    )


def exact(lhs_mat, rhs_mat):
    return jnp.dot(
        lhs_mat, rhs_mat, precision=lax.Precision.HIGHEST, preferred_element_type=jnp.float32
    )


def clip_terms(timesteps, clap_emb):
    half_cond = COND // 2
    frequency = jnp.exp(-math.log(10000.0) * jnp.arange(half_cond, dtype=jnp.float32) / half_cond)
    angles = timesteps.astype(jnp.float32)[:, None] * frequency[None]
    cond_vec = clap_emb + jnp.concatenate([jnp.sin(angles), jnp.cos(angles)], axis=1)
    theta_clip = 0.5 * math.pi * (timesteps.astype(jnp.float32) + 1.0) / 1001.0
    return (cond_vec, jnp.cos(theta_clip), jnp.sin(theta_clip))


def conv_forward(inputs, weight, masks_all):
    height, n_cols, n_in = inputs.shape
    widened = with_halo(inputs, (("section", 1),), 1)
    padded = jnp.pad(widened, ((1, 1), (0, 0), (0, 0)))
    taps = [
        padded[tap_row : tap_row + height, tap_col : tap_col + n_cols]
        * masks_all[tap_col][None, :, None]
        for tap_row in range(3)
        for tap_col in range(3)
    ]
    columns = jnp.concatenate(taps, axis=2).reshape(height * n_cols, 9 * n_in)
    return (columns, matmul(columns, weight))


def conv_backward(d_out, weight, masks_all):
    height, n_cols, n_out = d_out.shape
    widened = with_halo(d_out, (("section", 1),), 1)
    padded = jnp.pad(widened, ((1, 1), (0, 0), (0, 0)))
    taps = [
        padded[2 - tap_row : 2 - tap_row + height, 2 - tap_col : 2 - tap_col + n_cols]
        * masks_all[2 - tap_col][None, :, None]
        for tap_row in range(3)
        for tap_col in range(3)
    ]
    flipped = weight.reshape(9, -1, n_out).transpose(0, 2, 1).reshape(9 * n_out, -1)
    return matmul(jnp.concatenate(taps, axis=2).reshape(height * n_cols, 9 * n_out), flipped)


def group_forward(inputs, onehot, counts):
    per_group = inputs.shape[2] // GROUPS
    sum_one = exact(onehot.T, jnp.sum(inputs, axis=0)).reshape(-1, GROUPS, per_group).sum(axis=2)
    sum_two = (
        exact(onehot.T, jnp.sum(inputs * inputs, axis=0)).reshape(-1, GROUPS, per_group).sum(axis=2)
    )
    sum_one, sum_two = lax.psum((sum_one, sum_two), "section")
    mean_row = sum_one / counts
    inv_std = lax.rsqrt(sum_two / counts - mean_row * mean_row + EPS_NORM)
    mean_col = jnp.repeat(exact(onehot, mean_row), per_group, axis=1)
    std_col = jnp.repeat(exact(onehot, inv_std), per_group, axis=1)
    return ((inputs - mean_col[None]) * std_col[None], std_col)


def group_backward(d_out, normed, std_col, gain_row, onehot, counts):
    per_group = d_out.shape[2] // GROUPS
    scaled = d_out * gain_row
    sum_one = exact(onehot.T, jnp.sum(scaled, axis=0)).reshape(-1, GROUPS, per_group).sum(axis=2)
    sum_two = (
        exact(onehot.T, jnp.sum(scaled * normed, axis=0)).reshape(-1, GROUPS, per_group).sum(axis=2)
    )
    sum_one, sum_two = lax.psum((sum_one, sum_two), "section")
    mean_one = jnp.repeat(exact(onehot, sum_one / counts), per_group, axis=1)
    mean_two = jnp.repeat(exact(onehot, sum_two / counts), per_group, axis=1)
    d_in = std_col[None] * (scaled - mean_one[None] - normed * mean_two[None])
    return (d_in, jnp.sum(d_out * normed, axis=(0, 1)), jnp.sum(d_out, axis=(0, 1)))


def layer_forward(inputs, gain_row, bias_row):
    mean_row = jnp.mean(inputs, axis=1, keepdims=True)
    centered = inputs - mean_row
    inv_std = lax.rsqrt(jnp.mean(centered * centered, axis=1, keepdims=True) + EPS_NORM)
    normed = centered * inv_std
    return (normed * gain_row + bias_row, normed, inv_std)


def layer_backward(d_out, normed, inv_std, gain_row):
    scaled = d_out * gain_row
    d_in = inv_std * (
        scaled
        - jnp.mean(scaled, axis=1, keepdims=True)
        - normed * jnp.mean(scaled * normed, axis=1, keepdims=True)
    )
    return (d_in, jnp.sum(d_out * normed, axis=0), jnp.sum(d_out, axis=0))


def attention_forward(heads_x, pixel_ids):
    n_pix, n_heads, _ = heads_x.shape
    block_rows = min(512, n_pix)
    score_scale = HD ** (-0.5)
    key_rows = heads_x[..., HD : 2 * HD]
    val_rows = heads_x[..., 2 * HD :]

    def per_block(block_in):
        q_blk, i_blk = block_in
        scores = (
            jnp.einsum("bhd,rhd->hbr", q_blk, key_rows, preferred_element_type=jnp.float32)
            * score_scale
        )
        scores = jnp.where((i_blk[:, None] == pixel_ids[None, :])[None], scores, -1e30)
        row_max = jnp.max(scores, axis=2, keepdims=True)
        exp_rows = jnp.exp(scores - row_max)
        sum_rows = jnp.sum(exp_rows, axis=2, keepdims=True)
        prob_rows = (exp_rows / sum_rows).astype(jnp.bfloat16)
        out_blk = jnp.einsum(
            "hbr,rhd->bhd", prob_rows, val_rows, preferred_element_type=jnp.float32
        )
        return (out_blk.astype(jnp.bfloat16), (row_max + jnp.log(sum_rows))[:, :, 0].T)

    out_rows, log_total = lax.map(
        per_block,
        (heads_x[..., :HD].reshape(-1, block_rows, n_heads, HD), pixel_ids.reshape(-1, block_rows)),
    )
    return (out_rows.reshape(n_pix, n_heads, HD), log_total.reshape(n_pix, n_heads), heads_x)


def attention_backward(heads_x, log_total, d_heads, pixel_ids):
    n_pix, n_heads, _ = heads_x.shape
    block_rows = min(512, n_pix)
    score_scale = HD ** (-0.5)
    key_rows = heads_x[..., HD : 2 * HD]
    val_rows = heads_x[..., 2 * HD :]

    def per_block(running, block_in):
        d_key, d_value = running
        q_blk, d_blk, l_blk, i_blk = block_in
        scores = (
            jnp.einsum("bhd,rhd->hbr", q_blk, key_rows, preferred_element_type=jnp.float32)
            * score_scale
        )
        scores = jnp.where((i_blk[:, None] == pixel_ids[None, :])[None], scores, -1e30)
        prob_rows = jnp.exp(scores - l_blk.T[:, :, None])
        d_probs = jnp.einsum("bhd,rhd->hbr", d_blk, val_rows, preferred_element_type=jnp.float32)
        delta_row = jnp.sum(prob_rows * d_probs, axis=2, keepdims=True)
        d_scores = (prob_rows * (d_probs - delta_row)).astype(jnp.bfloat16)
        d_query = (
            jnp.einsum("hbr,rhd->bhd", d_scores, key_rows, preferred_element_type=jnp.float32)
            * score_scale
        )
        d_key = (
            d_key
            + jnp.einsum("hbr,bhd->rhd", d_scores, q_blk, preferred_element_type=jnp.float32)
            * score_scale
        )
        d_value = d_value + jnp.einsum(
            "hbr,bhd->rhd",
            prob_rows.astype(jnp.bfloat16),
            d_blk,
            preferred_element_type=jnp.float32,
        )
        return ((d_key, d_value), d_query)

    zero_acc = jnp.zeros((n_pix, n_heads, HD), jnp.float32)
    (d_key, d_value), d_query = lax.scan(
        per_block,
        (zero_acc, zero_acc),
        (
            heads_x[..., :HD].reshape(-1, block_rows, n_heads, HD),
            d_heads.reshape(-1, block_rows, n_heads, HD),
            log_total.reshape(-1, block_rows, n_heads),
            pixel_ids.reshape(-1, block_rows),
        ),
    )
    return jnp.concatenate([d_query.reshape(n_pix, n_heads, HD), d_key, d_value], axis=2)


def body(
    clean_lat,
    noise_lat,
    column_ids,
    timesteps,
    clap_emb,
    conv_w,
    proj_w,
    film_w,
    skip_w,
    down_w,
    stem_w,
    head_w,
    gains,
    conv_m,
    proj_m,
    film_m,
    skip_m,
    down_m,
    stem_m,
    head_m,
    gains_m,
    conv_v,
    proj_v,
    film_v,
    skip_v,
    down_v,
    stem_v,
    head_v,
    gains_v,
):
    bf16 = jnp.bfloat16
    masters = (conv_w, proj_w, film_w, skip_w, down_w, stem_w, head_w, gains)
    firsts = (conv_m, proj_m, film_m, skip_m, down_m, stem_m, head_m, gains_m)
    seconds = (conv_v, proj_v, film_v, skip_v, down_v, stem_v, head_v, gains_v)
    shard_dims = (1, 1, 1, 1, 0, 1, 0, 1)
    conv_b, proj_b, film_b, skip_b, down_b, stem_b, head_b, gain_b = (
        lax.all_gather(conv_w.astype(bf16), "dp", axis=1, tiled=True),
        lax.all_gather(proj_w.astype(bf16), "dp", axis=1, tiled=True),
        lax.all_gather(film_w.astype(bf16), "dp", axis=1, tiled=True),
        lax.all_gather(skip_w.astype(bf16), "dp", axis=1, tiled=True),
        lax.all_gather(down_w.astype(bf16), "dp", axis=0, tiled=True),
        lax.all_gather(stem_w.astype(bf16), "dp", axis=1, tiled=True),
        lax.all_gather(head_w.astype(bf16), "dp", axis=0, tiled=True),
        lax.all_gather(gains.astype(bf16), "dp", axis=1, tiled=True),
    )
    gain_f = gain_b.astype(jnp.float32)
    clean_row = clean_lat[0]
    noise_row = noise_lat[0]
    ids_row = column_ids[0]
    height, n_cols, _ = clean_row.shape
    n_pix = height * n_cols
    section_size = lax.axis_size("section")
    edge_pad = jnp.full((1,), -1, jnp.int32)
    ids_rim = lax.dynamic_slice_in_dim(
        jnp.concatenate([edge_pad, ids_row, edge_pad]),
        lax.axis_index("section") * n_cols,
        n_cols + 2,
    )
    own_ids = ids_rim[1 : n_cols + 1]
    masks_all = [(ids_rim[offset : offset + n_cols] == own_ids).astype(bf16) for offset in range(3)]
    labels = jnp.arange(CLIPS + 1)
    onehot = (own_ids[:, None] == labels[None, :]).astype(jnp.float32)
    full_onehot = (ids_row[:, None] == labels[None, :]).astype(jnp.float32)
    counts = jnp.maximum(jnp.sum(full_onehot, axis=0) * (height * (C // GROUPS)), 1.0)[:, None]
    clip_hot = onehot[:, :CLIPS]
    valid_cols = jnp.sum(clip_hot, axis=1)
    cond_vec, alpha_clip, sigma_clip = clip_terms(timesteps[0], clap_emb[0])
    alpha_col = exact(clip_hot, alpha_clip[:, None])[:, 0][None, :, None]
    sigma_col = exact(clip_hot, sigma_clip[:, None])[:, 0][None, :, None]
    noisy_in = alpha_col * clean_row + sigma_col * noise_row
    target = alpha_col * noise_row - sigma_col * clean_row
    stem_cols, stem = conv_forward(noisy_in.astype(bf16), stem_b, masks_all)
    stem = stem.reshape(height, n_cols, C)
    norm_one, std_one = group_forward(stem, onehot, counts)
    first_act, silu_one = jax.vjp(jax.nn.silu, norm_one * gain_f[0] + gain_f[1])
    cols_one, inner_out = conv_forward(first_act.astype(bf16), conv_b[0], masks_all)
    inner_out = inner_out.reshape(height, n_cols, C)
    cond_act = jax.nn.silu(cond_vec).astype(bf16)
    film_col = exact(clip_hot, matmul(cond_act, film_b))
    norm_two, std_two = group_forward(inner_out, onehot, counts)
    affine_two = norm_two * gain_f[2] + gain_f[3]
    second, silu_two = jax.vjp(
        jax.nn.silu, affine_two * (1.0 + film_col[None, :, :C]) + film_col[None, :, C:]
    )
    cols_two, branch = conv_forward(second.astype(bf16), conv_b[1], masks_all)
    stem_rows = stem.reshape(n_pix, C)
    joined = jnp.concatenate([stem_rows + branch, stem_rows], axis=1).astype(bf16)
    base_rows = matmul(joined, skip_b)
    ln_one, normed_one, lstd_one = layer_forward(base_rows, gain_f[4], gain_f[5])
    ln_one_b = ln_one.astype(bf16)
    qkv_rows = matmul(ln_one_b, proj_b[:, : 3 * C]).astype(bf16)
    pixel_ids = jnp.broadcast_to(
        ids_row.reshape(section_size, 1, n_cols), (section_size, height, n_cols)
    ).reshape(-1)
    out_heads, log_total, kept_heads = attention_forward(
        lax.all_to_all(
            qkv_rows.reshape(n_pix, section_size, HEADS // section_size, 3 * HD),
            "section",
            split_axis=1,
            concat_axis=0,
            tiled=True,
        )[:, 0],
        pixel_ids,
    )
    attended = lax.all_to_all(
        out_heads, "section", split_axis=0, concat_axis=1, tiled=True
    ).reshape(n_pix, C)
    mid_rows = base_rows + matmul(attended, proj_b[:, 3 * C : 4 * C])
    ln_two, normed_two, lstd_two = layer_forward(mid_rows, gain_f[6], gain_f[7])
    ln_two_b = ln_two.astype(bf16)
    hidden = matmul(ln_two_b, proj_b[:, 4 * C :])
    act_out, gelu_pull = jax.vjp(jax.nn.gelu, hidden)
    act_b = act_out.astype(bf16)
    top_rows = mid_rows + matmul(act_b, down_b)
    head_cols, pred = conv_forward(
        top_rows.reshape(height, n_cols, C).astype(bf16), head_b, masks_all
    )
    residue = pred.reshape(height, n_cols, CIN) - target
    local_loss = jnp.sum(valid_cols[None, :, None] * residue * residue)
    local_count = jnp.sum(valid_cols) * (height * CIN)
    loss_sum, pix_count = lax.psum((local_loss, local_count), ("dp", "section"))
    d_pred = (2.0 * valid_cols[None, :, None] * residue / pix_count).astype(bf16)
    g_head = left_product(head_cols, d_pred.reshape(n_pix, CIN))
    d_top = conv_backward(d_pred, head_b, masks_all)
    d_top_b = d_top.astype(bf16)
    g_down = left_product(act_b, d_top_b)
    d_hidden = gelu_pull(matmul(d_top_b, down_b.T))[0].astype(bf16)
    g_up = left_product(ln_two_b, d_hidden)
    d_ln_two, g_ln2_g, g_ln2_b = layer_backward(
        matmul(d_hidden, proj_b[:, 4 * C :].T), normed_two, lstd_two, gain_f[6]
    )
    d_mid = d_top + d_ln_two
    d_mid_b = d_mid.astype(bf16)
    g_out = left_product(attended, d_mid_b)
    d_att = matmul(d_mid_b, proj_b[:, 3 * C : 4 * C].T).astype(bf16)
    d_heads = lax.all_to_all(
        d_att.reshape(n_pix, HEADS, HD), "section", split_axis=1, concat_axis=0, tiled=True
    )
    d_qkv_heads = attention_backward(kept_heads, log_total, d_heads, pixel_ids).astype(bf16)
    d_qkv = lax.all_to_all(d_qkv_heads, "section", split_axis=0, concat_axis=1, tiled=True).reshape(
        n_pix, 3 * C
    )
    g_qkv = left_product(ln_one_b, d_qkv)
    d_ln_one, g_ln1_g, g_ln1_b = layer_backward(
        matmul(d_qkv, proj_b[:, : 3 * C].T), normed_one, lstd_one, gain_f[4]
    )
    d_base = (d_mid + d_ln_one).astype(bf16)
    g_skip = left_product(joined, d_base)
    d_joined = matmul(d_base, skip_b.T)
    d_branch = d_joined[:, :C].astype(bf16)
    g_conv_two = left_product(cols_two, d_branch)
    d_second = conv_backward(d_branch.reshape(height, n_cols, C), conv_b[1], masks_all).reshape(
        height, n_cols, C
    )
    d_pre_two = silu_two(d_second)[0]
    d_scale = jnp.sum(d_pre_two * affine_two, axis=0)
    d_shift = jnp.sum(d_pre_two, axis=0)
    d_film = exact(clip_hot.T, jnp.concatenate([d_scale, d_shift], axis=1))
    g_film = exact(cond_act.astype(jnp.float32).T, d_film)
    d_inner, g_gn2_g, g_gn2_b = group_backward(
        d_pre_two * (1.0 + film_col[None, :, :C]), norm_two, std_two, gain_f[2], onehot, counts
    )
    d_inner_b = d_inner.astype(bf16)
    g_conv_one = left_product(cols_one, d_inner_b.reshape(n_pix, C))
    d_first = conv_backward(d_inner_b, conv_b[0], masks_all).reshape(height, n_cols, C)
    d_stem_gn, g_gn1_g, g_gn1_b = group_backward(
        silu_one(d_first)[0], norm_one, std_one, gain_f[0], onehot, counts
    )
    d_stem = (d_stem_gn.reshape(n_pix, C) + d_joined[:, :C] + d_joined[:, C:]).astype(bf16)
    g_stem = left_product(stem_cols, d_stem)
    g_conv = jnp.stack([g_conv_one, g_conv_two])
    g_proj = jnp.concatenate([g_qkv, g_out, g_up], axis=1)
    g_gains = jnp.stack([g_gn1_g, g_gn1_b, g_gn2_g, g_gn2_b, g_ln1_g, g_ln1_b, g_ln2_g, g_ln2_b])
    totals = lax.psum(
        (g_conv, g_proj, g_film, g_skip, g_down, g_stem, g_head, g_gains), ("dp", "section")
    )
    squares = sum((jnp.sum(item * item) for item in totals))
    dp_size = lax.axis_size("dp")
    dp_place = lax.axis_index("dp")
    shards = tuple(
        (
            lax.dynamic_slice_in_dim(
                item, dp_place * (item.shape[dim] // dp_size), item.shape[dim] // dp_size, dim
            )
            for item, dim in zip(totals, shard_dims)
        )
    )
    grad_norm = jnp.sqrt(squares)
    factor = jnp.minimum(1.0, CLIP_NORM / grad_norm)
    new_w, new_m, new_v = ([], [], [])
    for weight, grad_one, m_old, v_old in zip(masters, shards, firsts, seconds):
        grad_one = grad_one * factor
        m_new = BETA_ONE * m_old + (1.0 - BETA_ONE) * grad_one
        v_new = BETA_TWO * v_old + (1.0 - BETA_TWO) * grad_one * grad_one
        step_dir = (
            m_new / (1.0 - BETA_ONE**STEP) / (jnp.sqrt(v_new / (1.0 - BETA_TWO**STEP)) + ADAM_EPS)
        )
        new_w.append(weight - RATE * (step_dir + DECAY * weight))
        new_m.append(m_new)
        new_v.append(v_new)
    return (
        new_w[0],
        new_w[1],
        new_w[2],
        new_w[3],
        new_w[4],
        new_w[5],
        new_w[6],
        new_w[7],
        new_m[0],
        new_m[1],
        new_m[2],
        new_m[3],
        new_m[4],
        new_m[5],
        new_m[6],
        new_m[7],
        new_v[0],
        new_v[1],
        new_v[2],
        new_v[3],
        new_v[4],
        new_v[5],
        new_v[6],
        new_v[7],
        grad_norm,
        loss_sum,
        pix_count,
    )


def solution(mesh):
    return jax.shard_map(
        body,
        mesh=mesh,
        in_specs=(
            P("dp", None, "section", None),
            P("dp", None, "section", None),
            P("dp", None),
            P("dp", None),
            P("dp", None, None),
            P(None, "dp", None),
            P(None, "dp"),
            P(None, "dp"),
            P(None, "dp"),
            P("dp", None),
            P(None, "dp"),
            P("dp", None),
            P(None, "dp"),
            P(None, "dp", None),
            P(None, "dp"),
            P(None, "dp"),
            P(None, "dp"),
            P("dp", None),
            P(None, "dp"),
            P("dp", None),
            P(None, "dp"),
            P(None, "dp", None),
            P(None, "dp"),
            P(None, "dp"),
            P(None, "dp"),
            P("dp", None),
            P(None, "dp"),
            P("dp", None),
            P(None, "dp"),
        ),
        out_specs=(
            P(None, "dp", None),
            P(None, "dp"),
            P(None, "dp"),
            P(None, "dp"),
            P("dp", None),
            P(None, "dp"),
            P("dp", None),
            P(None, "dp"),
            P(None, "dp", None),
            P(None, "dp"),
            P(None, "dp"),
            P(None, "dp"),
            P("dp", None),
            P(None, "dp"),
            P("dp", None),
            P(None, "dp"),
            P(None, "dp", None),
            P(None, "dp"),
            P(None, "dp"),
            P(None, "dp"),
            P("dp", None),
            P(None, "dp"),
            P("dp", None),
            P(None, "dp"),
            P(),
            P(),
            P(),
        ),
        check_vma=False,
    )
```

profile of v0, /device:TPU:0, one launch (start us, length us, event | category | flops | bytes accessed | tf_op | source)
XLA Modules:
  0.0 1284.2 jit_solution(16529872938991114728)
XLA Ops:
  56.8 13.0 %all-reduce.12 = (f32[5,32]{1,0:T(8,128)S(1)}, f32[5,32]{1,0:T(8,128)S(1)}) all-reduce(f32[5,32]{1,0:T(8,128)S(1)} %convolution_reduce_fusion.6, f32[5,32]{1,0:T(8,128)S(1)} %convolution_reduce_fusion.7), channel_id=1, replica_groups=mesh['dp'=8,'section'=4] {'section'}, use_global_device_ids=true, to_apply=%region_6.7 | all-reduce | flops 320 | bytes 2560 | tf_op jit(solution)/shard_map/psum | solution.py:103
  133.7 35.5 %all-to-all-done = bf16[1024,4,2,96]{0,3,2,1:T(8,128)(2,1)S(1)} async-done(((bf16[1024,4,2,96]{0,3,2,1:T(8,128)(2,1)}), bf16[1024,4,2,96]{0,3,2,1:T(8,128)(2,1)S(1)}, u32[]{:S(2)}, u32[]{:S(2)}) %all-to-all-start) | async-done | bytes 1572896 | tf_op jit(solution)/shard_map/all_to_all | solution.py:319
  175.4 138.4 %while.28 = (s32[]{:T(128)}, bf16[8,512,2,32]{1,3,2,0:T(8,128)(2,1)S(1)}, f32[8,512,2]{1,2,0:T(2,128)}, s32[8,512]{1,0:T(8,128)}, bf16[8,512,2,32]{1,3,2,0:T(8,1...) while((s32[]{:T(128)}, ...), condition=%wide.region_19.20_spmd.clone, body=%wide.region_16.19_spmd.clone.sunk | while | flops 589331456 | bytes 60005492 | solution.py:166
  323.9 39.8 %psum.130 = f32[]{:T(128)} all-reduce(f32[]{:T(128)S(6)} %mul.1194), channel_id=1, replica_groups=mesh['dp'=8,'section'=4] {'dp','section'}, use_global_device_ids=true, to_apply=%region_23.24 | all-reduce | flops 1 | bytes 8 | tf_op jit(solution)/shard_map/psum | solution.py:344
  433.6 13.8 %all-to-all-done.2 = bf16[1024,8,32]{0,2,1:T(8,128)(2,1)S(1)} async-done(((bf16[1024,8,32]{0,2,1:T(8,128)(2,1)}), bf16[1024,8,32]{0,2,1:T(8,128)(2,1)S(1)}, u32[]{:S(2)}, u32[]{:S(2)}) %all-to-all-start.2) | async-done | bytes 524320 | tf_op jit(solution)/shard_map/all_to_all | solution.py:359
  448.9 448.6 %while.29 = (s32[]{:T(128)}, f32[4096,2,32]{0,2,1:T(8,128)S(1)}, f32[4096,2,32]{0,2,1:T(8,128)}, bf16[8,512,2,32]{1,3,2,0:T(8,128)(2,1)}, bf16[8,512,2,32]{1,3,2...) while((s32[]{:T(128)}, f32[4096,2,32]{0,2,1:T(8,128)S(1)}, ...), condition=%wide.region_28.29_spmd.clone, body=%wide.region_26.28_spmd.clone.sunk | while | flops 1408531456 | bytes 215977200 | solution.py:210
  470.3 15.6 %multiply_reduce_fusion.28 = (f32[2,512]{1,0:T(2,128)S(1)}, f32[2,512,4096]{2,1,0:T(8,128)}) fusion(f32[2,512,4096]{2,1,0:T(8,128)} %copy-done, f32[2,512]{1,0:T(2,128)S(1)} %dynamic-slice_bitcast_fusion.2, pred[512,4096]{1,0:T(8,128)(4,1)} %broadcast_compare_fusion.5, bf16[4096,2,32]{0,2,1:T(8,128)(2,1)} %get-tuple-element.809, ...), kind=kOutput, calls=%fused_computation.21.clone.1 | convolution fusion | flops 289405952 | bytes 36249604 | tf_op jit(solution)/shard_map/while/body/eval_jaxpr/bhd,rhd->hbr/dot_general | solution.py:189
  485.9 12.4 multiply_convert_fusion.8
  526.4 15.6 %multiply_reduce_fusion.28 = (f32[2,512]{1,0:T(2,128)S(1)}, f32[2,512,4096]{2,1,0:T(8,128)}) fusion(f32[2,512,4096]{2,1,0:T(8,128)} %copy-done, f32[2,512]{1,0:T(2,128)S(1)} %dynamic-slice_bitcast_fusion.2, pred[512,4096]{1,0:T(8,128)(4,1)} %broadcast_compare_fusion.5, bf16[4096,2,32]{0,2,1:T(8,128)(2,1)} %get-tuple-element.809, ...), kind=kOutput, calls=%fused_computation.21.clone.1 | convolution fusion | flops 289405952 | bytes 36249604 | tf_op jit(solution)/shard_map/while/body/eval_jaxpr/bhd,rhd->hbr/dot_general | solution.py:189
  541.9 12.4 multiply_convert_fusion.8
  582.4 15.6 %multiply_reduce_fusion.28 = (f32[2,512]{1,0:T(2,128)S(1)}, f32[2,512,4096]{2,1,0:T(8,128)}) fusion(f32[2,512,4096]{2,1,0:T(8,128)} %copy-done, f32[2,512]{1,0:T(2,128)S(1)} %dynamic-slice_bitcast_fusion.2, pred[512,4096]{1,0:T(8,128)(4,1)} %broadcast_compare_fusion.5, bf16[4096,2,32]{0,2,1:T(8,128)(2,1)} %get-tuple-element.809, ...), kind=kOutput, calls=%fused_computation.21.clone.1 | convolution fusion | flops 289405952 | bytes 36249604 | tf_op jit(solution)/shard_map/while/body/eval_jaxpr/bhd,rhd->hbr/dot_general | solution.py:189
  598.0 12.4 multiply_convert_fusion.8
  638.4 15.6 %multiply_reduce_fusion.28 = (f32[2,512]{1,0:T(2,128)S(1)}, f32[2,512,4096]{2,1,0:T(8,128)}) fusion(f32[2,512,4096]{2,1,0:T(8,128)} %copy-done, f32[2,512]{1,0:T(2,128)S(1)} %dynamic-slice_bitcast_fusion.2, pred[512,4096]{1,0:T(8,128)(4,1)} %broadcast_compare_fusion.5, bf16[4096,2,32]{0,2,1:T(8,128)(2,1)} %get-tuple-element.809, ...), kind=kOutput, calls=%fused_computation.21.clone.1 | convolution fusion | flops 289405952 | bytes 36249604 | tf_op jit(solution)/shard_map/while/body/eval_jaxpr/bhd,rhd->hbr/dot_general | solution.py:189
  654.0 12.4 multiply_convert_fusion.8
  694.5 15.6 %multiply_reduce_fusion.28 = (f32[2,512]{1,0:T(2,128)S(1)}, f32[2,512,4096]{2,1,0:T(8,128)}) fusion(f32[2,512,4096]{2,1,0:T(8,128)} %copy-done, f32[2,512]{1,0:T(2,128)S(1)} %dynamic-slice_bitcast_fusion.2, pred[512,4096]{1,0:T(8,128)(4,1)} %broadcast_compare_fusion.5, bf16[4096,2,32]{0,2,1:T(8,128)(2,1)} %get-tuple-element.809, ...), kind=kOutput, calls=%fused_computation.21.clone.1 | convolution fusion | flops 289405952 | bytes 36249604 | tf_op jit(solution)/shard_map/while/body/eval_jaxpr/bhd,rhd->hbr/dot_general | solution.py:189
  710.1 12.4 multiply_convert_fusion.8
  750.5 15.6 %multiply_reduce_fusion.28 = (f32[2,512]{1,0:T(2,128)S(1)}, f32[2,512,4096]{2,1,0:T(8,128)}) fusion(f32[2,512,4096]{2,1,0:T(8,128)} %copy-done, f32[2,512]{1,0:T(2,128)S(1)} %dynamic-slice_bitcast_fusion.2, pred[512,4096]{1,0:T(8,128)(4,1)} %broadcast_compare_fusion.5, bf16[4096,2,32]{0,2,1:T(8,128)(2,1)} %get-tuple-element.809, ...), kind=kOutput, calls=%fused_computation.21.clone.1 | convolution fusion | flops 289405952 | bytes 36249604 | tf_op jit(solution)/shard_map/while/body/eval_jaxpr/bhd,rhd->hbr/dot_general | solution.py:189
  766.1 12.4 multiply_convert_fusion.8
  806.5 15.6 %multiply_reduce_fusion.28 = (f32[2,512]{1,0:T(2,128)S(1)}, f32[2,512,4096]{2,1,0:T(8,128)}) fusion(f32[2,512,4096]{2,1,0:T(8,128)} %copy-done, f32[2,512]{1,0:T(2,128)S(1)} %dynamic-slice_bitcast_fusion.2, pred[512,4096]{1,0:T(8,128)(4,1)} %broadcast_compare_fusion.5, bf16[4096,2,32]{0,2,1:T(8,128)(2,1)} %get-tuple-element.809, ...), kind=kOutput, calls=%fused_computation.21.clone.1 | convolution fusion | flops 289405952 | bytes 36249604 | tf_op jit(solution)/shard_map/while/body/eval_jaxpr/bhd,rhd->hbr/dot_general | solution.py:189
  822.1 12.4 multiply_convert_fusion.8
  862.6 15.6 %multiply_reduce_fusion.28 = (f32[2,512]{1,0:T(2,128)S(1)}, f32[2,512,4096]{2,1,0:T(8,128)}) fusion(f32[2,512,4096]{2,1,0:T(8,128)} %copy-done, f32[2,512]{1,0:T(2,128)S(1)} %dynamic-slice_bitcast_fusion.2, pred[512,4096]{1,0:T(8,128)(4,1)} %broadcast_compare_fusion.5, bf16[4096,2,32]{0,2,1:T(8,128)(2,1)} %get-tuple-element.809, ...), kind=kOutput, calls=%fused_computation.21.clone.1 | convolution fusion | flops 289405952 | bytes 36249604 | tf_op jit(solution)/shard_map/while/body/eval_jaxpr/bhd,rhd->hbr/dot_general | solution.py:189
  925.8 30.6 %all-to-all-done.3 = bf16[4096,2,96]{2,1,0:T(2,128)(2,1)} async-done(((bf16[4096,2,96]{2,1,0:T(2,128)(2,1)}), bf16[4096,2,96]{2,1,0:T(2,128)(2,1)}, u32[]{:S(2)}, u32[]{:S(2)}) %all-to-all-start.3) | async-done | bytes 1572896 | tf_op jit(solution)/shard_map/all_to_all | solution.py:363
  1049.4 39.2 %all-reduce.7 = (f32[8,256]{1,0:T(8,128)S(1)}, f32[]{:T(128)}) all-reduce(f32[8,256]{1,0:T(8,128)S(1)} %stack.47, f32[]{:T(128)} %get-tuple-element.592), channel_id=1, replica_groups=mesh['dp'=8,'section'=4] {'dp','section'}, use_global_device_ids=true, to_apply=%region_67.68 | all-reduce | flops 2049 | bytes 16392 | tf_op jit(solution)/shard_map/psum | solution.py:397
  1089.2 154.4 %all-reduce.15.cloned.1.call-done = (f32[2,2304,256]{2,1,0:T(8,128)}, f32[256,2048]{1,0:T(8,128)}, f32[512,512]{0,1:T(8,128)}, f32[512,256]{0,1:T(8,128)}, f32[1...) async-done(((f32[2,2304,256]{2,1,0:T(8,128)}, f32[256,2048]{1,0:T(8,128)}, f32[512,512]{0,1:T(8,128)}, f32[512,256]{0,1:T(8,128)}, f32[1024,256]{1,0:T(8,128)}, ...) | async-done | bytes 9584656 | tf_op jit(solution)/shard_map/psum | solution.py:397
  (746 shorter events, 721.8 us)
Async XLA Ops:
  7.2 81.5 %all-gather.5.cloned.1.call-start = ((), (), s32[]{:S(2)}) async-start(), calls=%async_computation.4 | async-start | bytes 2654208 | tf_op jit(solution)/shard_map/all_gather | solution.py:260
  9.1 115.1 %all-gather.7.cloned.1.call-start = ((), (), s32[]{:S(2)}) async-start(), calls=%async_computation.5 | async-start | bytes 1179648 | tf_op jit(solution)/shard_map/all_gather | solution.py:261
  12.7 41.6 %collective-permute-start = (bf16[16,1,8]{1,2,0:T(8,128)(2,1)S(1)}, bf16[16,1,8]{1,2,0:T(8,128)(2,1)S(1)}, u32[]{:S(2)}, u32[]{:S(2)}) collective-permute-start(bf16[16,1,8]{1,2,0:T(8,128)(2,1)S(1)} %get-tuple-element.596), channel_id=1, source_target_pairs={{0,1},{1,2},{2,3},{4,5},{5,6},{6,7},{8,9},{9,10},{10,11},{12,13},{... | collective-permute-start | bytes 776 | tf_op jit(solution)/shard_map/ppermute | solution.py:35
  17.6 36.7 %collective-permute-start.1 = (bf16[16,1,8]{1,2,0:T(8,128)(2,1)S(1)}, bf16[16,1,8]{1,2,0:T(8,128)(2,1)S(1)}, u32[]{:S(2)}, u32[]{:S(2)}) collective-permute-start(bf16[16,1,8]{1,2,0:T(8,128)(2,1)S(1)} %get-tuple-element.597), channel_id=1, source_target_pairs={{1,0},{2,1},{3,2},{5,4},{6,5},{7,6},{9,8},{10,9},{11,10},{13,12},{... | collective-permute-start | bytes 776 | tf_op jit(solution)/shard_map/ppermute | solution.py:37
  22.1 98.4 %copy-start.66 = (bf16[64]{0:T(256)(128)(2,1)}, bf16[64]{0:T(256)(128)(2,1)S(1)}, u32[]{:S(2)}) copy-start(bf16[64]{0:T(256)(128)(2,1)S(1)} %get-tuple-element.609) | copy-start | bytes 388
  22.1 98.8 %copy-start.69 = (bf16[64]{0:T(256)(128)(2,1)}, bf16[64]{0:T(256)(128)(2,1)S(1)}, u32[]{:S(2)}) copy-start(bf16[64]{0:T(256)(128)(2,1)S(1)} %get-tuple-element.608) | copy-start | bytes 388
  71.0 2.7 collective-permute-start.2
  72.3 5.6 collective-permute-start.3
  104.3 13.8 %collective-permute-start.4 = (bf16[16,1,256]{2,1,0:T(2,128)(2,1)S(1)}, bf16[16,1,256]{2,1,0:T(2,128)(2,1)S(1)}, u32[]{:S(2)}, u32[]{:S(2)}) collective-permute-start(bf16[16,1,256]{2,1,0:T(2,128)(2,1)S(1)} %get-tuple-element.586), channel_id=1, source_target_pairs={{0,1},{1,2},{2,3},{4,5},{5,6},{6,7},{8,9},{9,10},{10,11},{12,13},{... | collective-permute-start | bytes 24584 | tf_op jit(solution)/shard_map/ppermute | solution.py:35
  107.3 10.8 collective-permute-start.5
  127.3 41.9 %all-to-all-start = ((bf16[1024,4,2,96]{0,3,2,1:T(8,128)(2,1)}), bf16[1024,4,2,96]{0,3,2,1:T(8,128)(2,1)S(1)}, u32[]{:S(2)}, u32[]{:S(2)}) async-start(bf16[1024,4,2,96]{0,3,2,1:T(8,128)(2,1)} %bitcast.334), calls=%async_computation | async-start | bytes 3145728 | tf_op jit(solution)/shard_map/all_to_all | solution.py:319
  319.0 56.7 %all-to-all-start.1 = ((bf16[4,2,32768]{2,1,0:T(2,128)(2,1)}), bf16[4,2,32768]{2,1,0:T(2,128)(2,1)S(1)}, u32[]{:S(2)}, u32[]{:S(2)}) async-start(bf16[4,2,32768]{2,1,0:T(2,128)(2,1)} %reshape.361), calls=%async_computation.1 | async-start | bytes 1048576 | tf_op jit(solution)/shard_map/all_to_all | solution.py:328
  387.2 13.1 %collective-permute-start.6 = (bf16[16,1,256]{2,1,0:T(2,128)(2,1)S(1)}, bf16[16,1,256]{2,1,0:T(2,128)(2,1)S(1)}, u32[]{:S(2)}, u32[]{:S(2)}) collective-permute-start(bf16[16,1,256]{2,1,0:T(2,128)(2,1)S(1)} %get-tuple-element.584), channel_id=1, source_target_pairs={{0,1},{1,2},{2,3},{4,5},{5,6},{6,7},{8,9},{9,10},{10,11},{12,13},{... | collective-permute-start | bytes 24584 | tf_op jit(solution)/shard_map/ppermute | solution.py:35
  390.7 9.7 collective-permute-start.7
  408.6 6.1 collective-permute-start.8
  413.1 5.8 collective-permute-start.9
  430.1 17.3 %all-to-all-start.2 = ((bf16[1024,8,32]{0,2,1:T(8,128)(2,1)}), bf16[1024,8,32]{0,2,1:T(8,128)(2,1)S(1)}, u32[]{:S(2)}, u32[]{:S(2)}) async-start(bf16[1024,8,32]{0,2,1:T(8,128)(2,1)} %bitcast.49), calls=%async_computation.2 | async-start | bytes 1048576 | tf_op jit(solution)/shard_map/all_to_all | solution.py:359
  904.0 52.3 %all-to-all-start.3 = ((bf16[4096,2,96]{2,1,0:T(2,128)(2,1)}), bf16[4096,2,96]{2,1,0:T(2,128)(2,1)}, u32[]{:S(2)}, u32[]{:S(2)}) async-start(bf16[4096,2,96]{2,1,0:T(2,128)(2,1)} %copy.425), calls=%async_computation.3 | async-start | bytes 4194304 | tf_op jit(solution)/shard_map/all_to_all | solution.py:363
  908.6 335.0 %all-reduce.15.cloned.1.call-start = ((), (), s32[]{:S(2)}) async-start(), calls=%async_computation.6 | async-start | bytes 19283968 | tf_op jit(solution)/shard_map/psum | solution.py:397
  973.2 5.6 collective-permute-start.10
  974.7 5.6 collective-permute-start.11
  1010.8 7.2 collective-permute-start.12
  1012.1 5.9 collective-permute-start.13
  1088.6 158.2 %copy-start.100 = (f32[8,256]{1,0:T(8,128)}, f32[8,256]{1,0:T(8,128)S(1)}, u32[]{:S(2)}) copy-start(f32[8,256]{1,0:T(8,128)S(1)} %get-tuple-element.530) | copy-start | bytes 24580
  (151 other events, 2719.0 us)
Sparse Core Ops, SparseCore 0:
  10.5 32.4 all-gather.4
  45.4 23.5 all-gather.6
  1048.8 194.7 all-reduce.14
where the time goes:
time: 1300 us; the launch traced here: 1280 us
  matrix products  421 us (32%)
  waiting for transfers between devices  244 us (19%)
  other arithmetic  242 us (19%)
  blocking collectives  182 us (14%)
  local copies, waits for them, and re-layouts  125 us (10%)
  starting transfers between devices  45.3 us (3%)
  between operations  23.7 us (2%)
    psum x1, waiting for transfers between devices, body(): lax.psum((g_conv, g_proj, g_film, g_skip, g_down, g_stem, g_head, g_gains...  154 us
    dot_general x8, matrix products, per_block(): jnp.einsum('bhd,rhd->hbr', d_blk, val_rows, preferred_element_type=jnp.fl...  125 us
    convert_element_type x8, other arithmetic, per_block(): d_scores = (prob_rows * (d_probs - delta_row)).astype(jnp.bfloat16)  98.8 us
    dot_general x16, matrix products, per_block(): jnp.einsum('bhd,rhd->hbr', q_blk, key_rows, preferred_element_type=jnp.fl...  68.3 us
    dot_general x8, matrix products, per_block(): jnp.einsum('hbr,bhd->rhd', prob_rows.astype(jnp.bfloat16), d_blk, preferr...  63 us
    while x32, local copies, waits for them, and re-layouts  46 us
    psum x1, blocking collectives, body(): loss_sum, pix_count = lax.psum((local_loss, local_count), ('dp', 'section'))  39.8 us
    psum x1, blocking collectives, body(): lax.psum((g_conv, g_proj, g_film, g_skip, g_down, g_stem, g_head, g_gains...  39.2 us
  transfers between devices with their start and end apart: 21, of which 9 were waited for; matrix products, arithmetic and copies ran while one was open for 5% of the time, Pallas kernels for 0%

commit v1 on v0

--- a/solution.py
+++ b/solution.py
@@ -1,8 +1,11 @@
+import functools
 import math
 
 import jax
 import jax.numpy as jnp
 from jax import lax
+from jax.experimental import pallas as pl
+from jax.experimental.pallas import tpu as pltpu
 from jax.sharding import PartitionSpec as P
 
 CIN = 8
@@ -140,84 +143,205 @@
     return (d_in, jnp.sum(d_out * normed, axis=0), jnp.sum(d_out, axis=0))
 
 
+BIG = 1e30
+LOG2E = 1.4426950408889634
+SCALE = HD**-0.5 * LOG2E
+VMEM_LIMIT = 56 << 20
+NN = (((1,), (0,)), ((), ()))
+NT = (((1,), (1,)), ((), ()))
+
+
+def mxu(lhs_mat, rhs_mat, dims=NN):
+    return lax.dot_general(lhs_mat, rhs_mat, dims, preferred_element_type=jnp.float32)
+
+
+def picker(rows, first, copies):
+    row = lax.broadcasted_iota(jnp.int32, (rows, 128), 0) - first
+    col = lax.broadcasted_iota(jnp.int32, (rows, 128), 1)
+    hit = (row >= 0) & (row < HD) & (col < HD * copies) & ((col & (HD - 1)) == row)
+    return hit.astype(jnp.bfloat16)
+
+
+def picker_t(lanes, first):
+    row = lax.broadcasted_iota(jnp.int32, (HD, lanes), 0)
+    col = lax.broadcasted_iota(jnp.int32, (HD, lanes), 1) - first
+    return (col == row).astype(jnp.bfloat16)
+
+
+def split_three(value):
+    high = value.astype(jnp.bfloat16).astype(jnp.float32)
+    rest = value - high
+    mid = rest.astype(jnp.bfloat16).astype(jnp.float32)
+    return high, mid, rest - mid
+
+
+def put(lane, first, parts):
+    total = jnp.where(lane == first, parts[0], 0.0)
+    for step, part in enumerate(parts[1:]):
+        total = total + jnp.where(lane == first + 1 + step, part, 0.0)
+    return total
+
+
+def forward_kernel(heads, bq, bk, x_ref, ids_ref, out_ref, lse_ref, kaug, vt):
+    n_pix, lanes = x_ref.shape
+    step = pl.program_id(0)
+
+    @pl.when(step == 0)
+    def _():
+        for head in range(heads):
+            pick_k = picker(lanes, 3 * HD * head + HD, 1)
+            pick_v = picker_t(lanes, 3 * HD * head + 2 * HD)
+            for start in range(0, n_pix, 512):
+                rows = x_ref[start : start + 512, :]
+                lane = lax.broadcasted_iota(jnp.int32, (512, 128), 1)
+                same = (lane - HD == ids_ref[start : start + 512, :]).astype(jnp.float32)
+                kaug[head, start : start + 512, :] = (mxu(rows, pick_k) + same).astype(jnp.bfloat16)
+                vt[head, :, start : start + 512] = mxu(pick_v, rows, NT).astype(jnp.bfloat16)
+
+    block = pl.ds(pl.multiple_of(step * bq, bq), bq)
+    own = x_ref[block, :]
+    own_ids = ids_ref[block, :]
+    lane = lax.broadcasted_iota(jnp.int32, (bq, 128), 1)
+    other = (lane >= HD) & (lane < HD + CLIPS + 1) & (lane - HD != own_ids)
+    tops, stats = [], []
+    for head in range(heads):
+        query = (mxu(own, picker(lanes, 3 * HD * head, 1)) + jnp.where(other, -BIG, 0.0)).astype(
+            jnp.bfloat16
+        )
+        total = jnp.zeros((8, bq), jnp.float32)
+        acc = jnp.zeros((HD, bq), jnp.float32)
+        row_max = jnp.full((1, bq), -jnp.inf, jnp.float32)
+        for start in range(0, n_pix, bk):
+            scores = mxu(kaug[head, start : start + bk, :], query, NT)
+            new_max = jnp.maximum(row_max, jnp.max(scores, axis=0, keepdims=True) * SCALE)
+            probs = jnp.exp2(scores * SCALE - new_max)
+            decay = jnp.exp2(row_max - new_max)
+            total = total * decay + jnp.sum(probs.reshape(bk // 8, 8, bq), axis=0)
+            acc = acc * decay + mxu(vt[head, :, start : start + bk], probs.astype(jnp.bfloat16))
+            row_max = new_max
+        total = jnp.sum(total, axis=0, keepdims=True)
+        tops.append(acc / total)
+        stats.append(jnp.broadcast_to(row_max + jnp.log2(total), (8, bq)))
+    out_ref[...] = jnp.concatenate(tops, axis=0).T.astype(jnp.bfloat16)
+    lse_ref[...] = jnp.concatenate(stats, axis=0).T
+
+
 def attention_forward(heads_x, pixel_ids):
-    n_pix, n_heads, _ = heads_x.shape
-    block_rows = min(512, n_pix)
-    score_scale = HD ** (-0.5)
-    key_rows = heads_x[..., HD : 2 * HD]
-    val_rows = heads_x[..., 2 * HD :]
-
-    def per_block(block_in):
-        q_blk, i_blk = block_in
-        scores = (
-            jnp.einsum("bhd,rhd->hbr", q_blk, key_rows, preferred_element_type=jnp.float32)
-            * score_scale
-        )
-        scores = jnp.where((i_blk[:, None] == pixel_ids[None, :])[None], scores, -1e30)
-        row_max = jnp.max(scores, axis=2, keepdims=True)
-        exp_rows = jnp.exp(scores - row_max)
-        sum_rows = jnp.sum(exp_rows, axis=2, keepdims=True)
-        prob_rows = (exp_rows / sum_rows).astype(jnp.bfloat16)
-        out_blk = jnp.einsum(
-            "hbr,rhd->bhd", prob_rows, val_rows, preferred_element_type=jnp.float32
-        )
-        return (out_blk.astype(jnp.bfloat16), (row_max + jnp.log(sum_rows))[:, :, 0].T)
-
-    out_rows, log_total = lax.map(
-        per_block,
-        (heads_x[..., :HD].reshape(-1, block_rows, n_heads, HD), pixel_ids.reshape(-1, block_rows)),
-    )
-    return (out_rows.reshape(n_pix, n_heads, HD), log_total.reshape(n_pix, n_heads), heads_x)
-
-
-def attention_backward(heads_x, log_total, d_heads, pixel_ids):
-    n_pix, n_heads, _ = heads_x.shape
-    block_rows = min(512, n_pix)
-    score_scale = HD ** (-0.5)
-    key_rows = heads_x[..., HD : 2 * HD]
-    val_rows = heads_x[..., 2 * HD :]
-
-    def per_block(running, block_in):
-        d_key, d_value = running
-        q_blk, d_blk, l_blk, i_blk = block_in
-        scores = (
-            jnp.einsum("bhd,rhd->hbr", q_blk, key_rows, preferred_element_type=jnp.float32)
-            * score_scale
-        )
-        scores = jnp.where((i_blk[:, None] == pixel_ids[None, :])[None], scores, -1e30)
-        prob_rows = jnp.exp(scores - l_blk.T[:, :, None])
-        d_probs = jnp.einsum("bhd,rhd->hbr", d_blk, val_rows, preferred_element_type=jnp.float32)
-        delta_row = jnp.sum(prob_rows * d_probs, axis=2, keepdims=True)
-        d_scores = (prob_rows * (d_probs - delta_row)).astype(jnp.bfloat16)
-        d_query = (
-            jnp.einsum("hbr,rhd->bhd", d_scores, key_rows, preferred_element_type=jnp.float32)
-            * score_scale
-        )
-        d_key = (
-            d_key
-            + jnp.einsum("hbr,bhd->rhd", d_scores, q_blk, preferred_element_type=jnp.float32)
-            * score_scale
-        )
-        d_value = d_value + jnp.einsum(
-            "hbr,bhd->rhd",
-            prob_rows.astype(jnp.bfloat16),
-            d_blk,
-            preferred_element_type=jnp.float32,
-        )
-        return ((d_key, d_value), d_query)
-
-    zero_acc = jnp.zeros((n_pix, n_heads, HD), jnp.float32)
-    (d_key, d_value), d_query = lax.scan(
-        per_block,
-        (zero_acc, zero_acc),
-        (
-            heads_x[..., :HD].reshape(-1, block_rows, n_heads, HD),
-            d_heads.reshape(-1, block_rows, n_heads, HD),
-            log_total.reshape(-1, block_rows, n_heads),
-            pixel_ids.reshape(-1, block_rows),
-        ),
-    )
-    return jnp.concatenate([d_query.reshape(n_pix, n_heads, HD), d_key, d_value], axis=2)
+    n_pix, lanes = heads_x.shape
+    heads = lanes // (3 * HD)
+    bq, bk = min(2048, n_pix), min(512, n_pix)
+    return pl.pallas_call(
+        functools.partial(forward_kernel, heads, bq, bk),
+        grid=(n_pix // bq,),
+        in_specs=[
+            pl.BlockSpec((n_pix, lanes), lambda i: (0, 0)),
+            pl.BlockSpec((n_pix, 1), lambda i: (0, 0)),
+        ],
+        out_specs=[
+            pl.BlockSpec((bq, heads * HD), lambda i: (i, 0)),
+            pl.BlockSpec((bq, heads * 8), lambda i: (i, 0)),
+        ],
+        out_shape=[
+            jax.ShapeDtypeStruct((n_pix, heads * HD), jnp.bfloat16),
+            jax.ShapeDtypeStruct((n_pix, heads * 8), jnp.float32),
+        ],
+        scratch_shapes=[
+            pltpu.VMEM((heads, n_pix, 128), jnp.bfloat16),
+            pltpu.VMEM((heads, HD, n_pix), jnp.bfloat16),
+        ],
+        compiler_params=pltpu.CompilerParams(vmem_limit_bytes=VMEM_LIMIT),
+    )(heads_x, pixel_ids)
+
+
+def backward_kernel(
+    heads, bq, bk, x_ref, ids_ref, do_ref, o_ref, lse_ref, out_ref, qaug, kaug, vaug, daug, kt, dqt
+):
+    n_pix, lanes = x_ref.shape
+    step = pl.program_id(0)
+
+    @pl.when(step == 0)
+    def _():
+        dqt[...] = jnp.zeros_like(dqt)
+        for head in range(heads):
+            base = 3 * HD * head
+            pick_q, pick_k = picker(lanes, base, 3), picker(lanes, base + HD, 3)
+            pick_v = picker(lanes, base + 2 * HD, 1)
+            pick_d = picker(heads * HD, HD * head, 1)
+            pick_kt = picker_t(lanes, base + HD)
+
+            def prepare(part, carry):
+                rows = pl.ds(pl.multiple_of(part * 512, 512), 512)
+                cells, ids = x_ref[rows, :], ids_ref[rows, :]
+                lane = lax.broadcasted_iota(jnp.int32, (512, 128), 1)
+                ones = ((lane - 96 == ids) | ((lane >= 104) & (lane < 107))).astype(jnp.float32)
+                kaug[head, rows, :] = (mxu(cells, pick_k) + ones).astype(jnp.bfloat16)
+                ones = ((lane >= HD) & (lane < HD + 3)).astype(jnp.float32)
+                vaug[head, rows, :] = (mxu(cells, pick_v) + ones).astype(jnp.bfloat16)
+                one, two, three = split_three(mxu(cells, pick_q) * SCALE)
+                query = jnp.where(lane < HD, one, jnp.where(lane < 2 * HD, two, three))
+                other = (lane >= 96) & (lane < 96 + CLIPS + 1) & (lane - 96 != ids)
+                query = query + jnp.where(other, -BIG, 0.0)
+                lse = lse_ref[rows, 8 * head : 8 * head + 1]
+                query = query + put(lane, 104, split_three(-lse))
+                qaug[head, rows, :] = query.astype(jnp.bfloat16)
+                d_out, out = mxu(do_ref[rows, :], pick_d), mxu(o_ref[rows, :], pick_d)
+                delta = jnp.sum(d_out * out, axis=1, keepdims=True)
+                d_out = d_out + put(lane, HD, split_three(-delta))
+                daug[head, rows, :] = d_out.astype(jnp.bfloat16)
+                return carry
+
+            lax.fori_loop(0, n_pix // 512, prepare, 0)
+            for start in range(0, n_pix, 512):
+                kt[head, :, start : start + 512] = mxu(
+                    pick_kt, x_ref[start : start + 512, :], NT
+                ).astype(jnp.bfloat16)
+
+    rows = pl.ds(pl.multiple_of(step * bk, bk), bk)
+    for head in range(heads):
+        key, value, key_t = kaug[head, rows, :], vaug[head, rows, :], kt[head, :, rows]
+        d_value = jnp.zeros((bk, 128), jnp.float32)
+        d_key = jnp.zeros((bk, 128), jnp.float32)
+        for start in range(0, n_pix, bq):
+            query = qaug[head, start : start + bq, :]
+            d_out = daug[head, start : start + bq, :]
+            probs = jnp.exp2(mxu(key, query, NT))
+            d_scores = (probs * mxu(value, d_out, NT)).astype(jnp.bfloat16)
+            d_value = d_value + mxu(probs.astype(jnp.bfloat16), d_out)
+            d_key = d_key + mxu(d_scores, query)
+            dqt[head, :, start : start + bq] += mxu(key_t, d_scores)
+        base = 3 * HD * head
+        d_key = (d_key[:, :HD] + d_key[:, HD : 2 * HD] + d_key[:, 2 * HD : 3 * HD]) * (1.0 / LOG2E)
+        out_ref[rows, base + HD : base + 2 * HD] = d_key.astype(jnp.bfloat16)
+        out_ref[rows, base + 2 * HD : base + 3 * HD] = d_value[:, :HD].astype(jnp.bfloat16)
+
+    @pl.when(step == pl.num_programs(0) - 1)
+    def _():
+        for head in range(heads):
+            for start in range(0, n_pix, 512):
+                d_query = dqt[head, :, start : start + 512] * (HD**-0.5)
+                out_ref[start : start + 512, 3 * HD * head : 3 * HD * head + HD] = (
+                    d_query.T.astype(jnp.bfloat16)
+                )
+
+
+def attention_backward(heads_x, log_total, d_heads, out_heads, pixel_ids):
+    n_pix, lanes = heads_x.shape
+    heads = lanes // (3 * HD)
+    bq, bk = min(1024, n_pix), min(1024, n_pix)
+    operands = (heads_x, pixel_ids, d_heads, out_heads, log_total)
+    return pl.pallas_call(
+        functools.partial(backward_kernel, heads, bq, bk),
+        grid=(n_pix // bk,),
+        in_specs=[pl.BlockSpec(item.shape, lambda i: (0, 0)) for item in operands],
+        out_specs=pl.BlockSpec((n_pix, lanes), lambda i: (0, 0)),
+        out_shape=jax.ShapeDtypeStruct((n_pix, lanes), jnp.bfloat16),
+        scratch_shapes=[pltpu.VMEM((heads, n_pix, 128), jnp.bfloat16)] * 4
+        + [
+            pltpu.VMEM((heads, HD, n_pix), jnp.bfloat16),
+            pltpu.VMEM((heads, HD, n_pix), jnp.float32),
+        ],
+        compiler_params=pltpu.CompilerParams(vmem_limit_bytes=VMEM_LIMIT),
+    )(*operands)
 
 
 def body(
@@ -315,16 +439,15 @@
     pixel_ids = jnp.broadcast_to(
         ids_row.reshape(section_size, 1, n_cols), (section_size, height, n_cols)
     ).reshape(-1)
-    out_heads, log_total, kept_heads = attention_forward(
-        lax.all_to_all(
-            qkv_rows.reshape(n_pix, section_size, HEADS // section_size, 3 * HD),
-            "section",
-            split_axis=1,
-            concat_axis=0,
-            tiled=True,
-        )[:, 0],
-        pixel_ids,
-    )
+    kept_heads = lax.all_to_all(
+        qkv_rows.reshape(n_pix, section_size, HEADS // section_size, 3 * HD),
+        "section",
+        split_axis=1,
+        concat_axis=0,
+        tiled=True,
+    ).reshape(section_size * n_pix, -1)
+    pixel_ids = pixel_ids[:, None]
+    out_heads, log_total = attention_forward(kept_heads, pixel_ids)
     attended = lax.all_to_all(
         out_heads, "section", split_axis=0, concat_axis=1, tiled=True
     ).reshape(n_pix, C)
@@ -357,9 +480,9 @@
     g_out = left_product(attended, d_mid_b)
     d_att = matmul(d_mid_b, proj_b[:, 3 * C : 4 * C].T).astype(bf16)
     d_heads = lax.all_to_all(
-        d_att.reshape(n_pix, HEADS, HD), "section", split_axis=1, concat_axis=0, tiled=True
-    )
-    d_qkv_heads = attention_backward(kept_heads, log_total, d_heads, pixel_ids).astype(bf16)
+        d_att, "section", split_axis=1, concat_axis=0, tiled=True
+    )
+    d_qkv_heads = attention_backward(kept_heads, log_total, d_heads, out_heads, pixel_ids)
     d_qkv = lax.all_to_all(d_qkv_heads, "section", split_axis=0, concat_axis=1, tiled=True).reshape(
         n_pix, 3 * C
     )

time: 1300 us -> 853 us (0.66)
  matrix products: 421 us -> 72.9 us
  other arithmetic: 242 us -> 68.8 us
  Pallas kernels: 0 us -> 162 us
  local copies, waits for them, and re-layouts: 125 us -> 58.6 us
  waiting for transfers between devices: 244 us -> 216 us
  blocking collectives: 182 us -> 200 us
    dot_general x56 -> x0, matrix products: 349 us -> none  [the longest x8 125 us: per_block(): jnp.einsum('bhd,rhd->hbr', d_blk, val_rows, preferred_element_type=jnp.fl...]
    pallas_call x0 -> x2, Pallas kernels: none -> 162 us  [the longest x1 98.9 us: attention_backward(): pl.pallas_call(functools.partial(backward_kernel, heads, bq, bk), grid=(n...]
    convert_element_type x8 -> x0, other arithmetic: 98.8 us -> none  [per_block(): d_scores = (prob_rows * (d_probs - delta_row)).astype(jnp.bfloat16)]
    while x32 -> x0, local copies, waits for them, and re-layouts: 46 us -> none
    reduce_sum x8 -> x0, other arithmetic: 37.1 us -> none  [per_block(): sum_rows = jnp.sum(exp_rows, axis=2, keepdims=True)]
    eq x16 -> x0, other arithmetic: 32 us -> none  [per_block(): i_blk[:, None] == pixel_ids[None, :]]
    all_to_all x0 -> x1, blocking collectives: none -> 16.9 us  [body(): lax.all_to_all(d_att, 'section', split_axis=1, concat_axis=0, tiled=True)]
    all_to_all x1 -> x0, waiting for transfers between devices: 13.8 us -> none  [body(): lax.all_to_all(d_att.reshape(n_pix, HEADS, HD), 'section', split_axis=1,...]
  transfers between devices with their start and end apart: 21 -> 20, of which waited for: 9 -> 7; matrix products, arithmetic and copies ran while one was open for 5% -> 8% of each run, Pallas kernels for 0% -> 0%
where the time goes in v1:
time: 853 us; the launch traced here: 843 us
  waiting for transfers between devices  216 us (25%)
  blocking collectives  200 us (23%)
  Pallas kernels  162 us (19%)
  matrix products  72.9 us (9%)
  other arithmetic  68.8 us (8%)
  local copies, waits for them, and re-layouts  58.6 us (7%)
  starting transfers between devices  41.6 us (5%)
  between operations  23.2 us (3%)
    psum x1, waiting for transfers between devices, body(): lax.psum((g_conv, g_proj, g_film, g_skip, g_down, g_stem, g_head, g_gains...  154 us
    pallas_call x1, Pallas kernels, attention_backward(): pl.pallas_call(functools.partial(backward_kernel, heads, bq, bk), grid=(n...  98.9 us
    pallas_call x1, Pallas kernels, attention_forward(): pl.pallas_call(functools.partial(forward_kernel, heads, bq, bk), grid=(n_...  63.6 us
    psum x1, blocking collectives, body(): loss_sum, pix_count = lax.psum((local_loss, local_count), ('dp', 'section'))  39.8 us
    psum x1, blocking collectives, body(): lax.psum((g_conv, g_proj, g_film, g_skip, g_down, g_stem, g_head, g_gains...  39.2 us
    dot_general x18, matrix products, matmul(): return jnp.dot(lhs_mat, rhs_mat, preferred_element_type=jnp.float32)  38 us
    all_to_all x1, waiting for transfers between devices, body(): lax.all_to_all(qkv_rows.reshape(n_pix, section_size, HEADS // section_siz...  33.1 us
    psum x2, blocking collectives, group_backward(): sum_one, sum_two = lax.psum((sum_one, sum_two), 'section')  23.8 us
  transfers between devices with their start and end apart: 20, of which 7 were waited for; matrix products, arithmetic and copies ran while one was open for 8% of the time, Pallas kernels for 0%

profile of v1, /device:TPU:0, one launch (start us, length us, event | category | flops | bytes accessed | tf_op | source)
XLA Modules:
  0.0 842.9 jit_solution(4340766888792313520)
XLA Ops:
  12.7 4.9 collective-permute-start
  23.5 8.9 %all-gather = bf16[8,32,8]{1,2,0:T(8,128)(2,1)S(1)} all-gather(bf16[1,32,8]{1,2,0:T(8,128)(2,1)S(1)} %convert_bitcast_fusion.1), channel_id=1, replica_groups=mesh['dp'=8,'section'=4] {'dp'}, dimensions={0}, use_global_device_ids=true | all-gather | bytes 4608 | tf_op jit(solution)/shard_map/all_gather | solution.py:391
  34.0 10.6 %all_gather.27 = bf16[512,512]{0,1:T(8,128)(2,1)S(1)} all-gather(bf16[512,64]{0,1:T(8,128)(2,1)S(1)} %convert_element_type.135), channel_id=1, replica_groups=mesh['dp'=8,'section'=4] {'dp'}, dimensions={1}, use_global_device_ids=true | all-gather | bytes 589824 | tf_op jit(solution)/shard_map/all_gather | solution.py:386
  46.0 8.3 all_gather.24
  57.5 13.0 %all-reduce.12 = (f32[5,32]{1,0:T(8,128)S(1)}, f32[5,32]{1,0:T(8,128)S(1)}) all-reduce(f32[5,32]{1,0:T(8,128)S(1)} %convolution_reduce_fusion.6, f32[5,32]{1,0:T(8,128)S(1)} %convolution_reduce_fusion.7), channel_id=1, replica_groups=mesh['dp'=8,'section'=4] {'section'}, use_global_device_ids=true, to_apply=%region_6.7 | all-reduce | flops 320 | bytes 2560 | tf_op jit(solution)/shard_map/psum | solution.py:106
  94.3 9.4 %all-reduce.11 = (f32[5,32]{1,0:T(8,128)S(1)}, f32[5,32]{1,0:T(8,128)S(1)}) all-reduce(f32[5,32]{1,0:T(8,128)S(1)} %convolution_reduce_fusion.5, f32[5,32]{1,0:T(8,128)S(1)} %convolution_reduce_fusion.4), channel_id=1, replica_groups=mesh['dp'=8,'section'=4] {'section'}, use_global_device_ids=true, to_apply=%region_9.10 | all-reduce | flops 320 | bytes 2560 | tf_op jit(solution)/shard_map/psum | solution.py:106
  109.2 9.5 %all_gather.28 = bf16[512,256]{0,1:T(8,128)(2,1)S(1)} all-gather(bf16[512,32]{0,1:T(8,128)(2,1)S(1)} %convert_element_type.137), channel_id=1, replica_groups=mesh['dp'=8,'section'=4] {'dp'}, dimensions={1}, use_global_device_ids=true | all-gather | bytes 294912 | tf_op jit(solution)/shard_map/all_gather | solution.py:387
  128.4 4.3 all-to-all-start
  137.4 33.1 %all-to-all-done = bf16[1024,4,2,96]{0,3,2,1:T(8,128)(2,1)} async-done(((bf16[1024,4,2,96]{0,3,2,1:T(8,128)(2,1)}), bf16[1024,4,2,96]{0,3,2,1:T(8,128)(2,1)}, u32[]{:S(2)}, u32[]{:S(2)}) %all-to-all-start) | async-done | bytes 1572896 | tf_op jit(solution)/shard_map/all_to_all | solution.py:442
  170.5 6.1 copy.317
  181.0 63.6 %shard_map.484 = (bf16[4096,64]{1,0:T(8,128)(2,1)}, f32[4096,16]{1,0:T(8,128)}) custom-call(bf16[4096,192]{1,0:T(8,128)(2,1)} %reshape.258.x_ref, s32[4096,1]{1,0:T(8,128)} %broadcast_in_dim_reshape.3.ids_ref), custom_call_target="tpu_custom_call" | custom-call | tf_op jit(solution)/shard_map/pallas_call | solution.py:233
  251.8 39.8 %psum.130 = f32[]{:T(128)} all-reduce(f32[]{:T(128)S(6)} %mul.1170), channel_id=1, replica_groups=mesh['dp'=8,'section'=4] {'dp','section'}, use_global_device_ids=true, to_apply=%region_19.20 | all-reduce | flops 1 | bytes 8 | tf_op jit(solution)/shard_map/psum | solution.py:467
  291.7 11.8 %all_gather.30 = bf16[1024,256]{1,0:T(8,128)(2,1)} all-gather(bf16[128,256]{1,0:T(8,128)(2,1)S(1)} %convert_element_type.143), channel_id=1, replica_groups=mesh['dp'=8,'section'=4] {'dp'}, dimensions={0}, use_global_device_ids=true | all-gather | bytes 589824 | tf_op jit(solution)/shard_map/all_gather | solution.py:388
  315.0 8.3 all-gather.1
  332.4 4.5 collective-permute-start.8
  345.0 5.4 fusion.6
  353.2 16.9 %all_to_all.72 = bf16[1024,4,64]{0,2,1:T(8,128)(2,1)} all-to-all(bf16[1024,4,64]{0,2,1:T(8,128)(2,1)S(1)} %bitcast.236), channel_id=1, replica_groups=mesh['dp'=8,'section'=4] {'section'}, dimensions={1} | all-to-all | bytes 1048576 | tf_op jit(solution)/shard_map/all_to_all | solution.py:482
  372.5 98.9 %shard_map.485 = bf16[4096,192]{1,0:T(8,128)(2,1)} custom-call(bf16[4096,192]{1,0:T(8,128)(2,1)} %reshape.258.x_ref, s32[4096,1]{1,0:T(8,128)} %broadcast_in_dim_reshape.3.ids_ref, bf16[4096,64]{1,0:T(8,128)(2,1)} %bitcast.234, bf16[4096,64]{1,0:T(8,128)(2,1)} %get-tuple-element.29.o_ref, f32[4096,16]{1,0:T(8,128)} %get-tuple-element.30.lse_ref), custom_call_target="tpu_custom_call" | custom-call | tf_op jit(solution)/shard_map/pallas_call | solution.py:332
  475.4 4.4 all-to-all-start.3
  497.3 18.6 %all-to-all-done.3 = bf16[4,1024,192]{1,2,0:T(8,128)(2,1)} async-done(((bf16[4,1024,192]{1,2,0:T(8,128)(2,1)}), bf16[4,1024,192]{1,2,0:T(8,128)(2,1)}, u32[]{:S(2)}, u32[]{:S(2)}) %all-to-all-start.3) | async-done | bytes 1572896 | tf_op jit(solution)/shard_map/all_to_all | solution.py:486
  545.7 12.3 %all-reduce.10 = (f32[5,32]{1,0:T(8,128)S(1)}, f32[5,32]{1,0:T(8,128)}) all-reduce(f32[5,32]{1,0:T(8,128)S(1)} %convolution_reduce_fusion.2, f32[5,32]{1,0:T(8,128)S(1)} %convolution_reduce_fusion.3), channel_id=1, replica_groups=mesh['dp'=8,'section'=4] {'section'}, use_global_device_ids=true, to_apply=%region_29.30 | all-reduce | flops 320 | bytes 2560 | tf_op jit(solution)/shard_map/psum | solution.py:121
  588.0 11.5 %all-reduce.9 = (f32[5,32]{1,0:T(8,128)S(1)}, f32[5,32]{1,0:T(8,128)S(1)}) all-reduce(f32[5,32]{1,0:T(8,128)S(1)} %convolution_reduce_fusion, f32[5,32]{1,0:T(8,128)S(1)} %convolution_reduce_fusion.1), channel_id=1, replica_groups=mesh['dp'=8,'section'=4] {'section'}, use_global_device_ids=true, to_apply=%region_47.48 | all-reduce | flops 320 | bytes 2560 | tf_op jit(solution)/shard_map/psum | solution.py:121
  608.2 39.2 %all-reduce.7 = (f32[8,256]{1,0:T(8,128)S(1)}, f32[]{:T(128)}) all-reduce(f32[8,256]{1,0:T(8,128)S(1)} %stack.47, f32[]{:T(128)} %get-tuple-element.218), channel_id=1, replica_groups=mesh['dp'=8,'section'=4] {'dp','section'}, use_global_device_ids=true, to_apply=%region_60.61 | all-reduce | flops 2049 | bytes 16392 | tf_op jit(solution)/shard_map/psum | solution.py:520
  648.0 154.3 %all-reduce.15.cloned.1.call-done = (f32[2,2304,256]{2,1,0:T(8,128)}, f32[256,2048]{1,0:T(8,128)}, f32[512,512]{0,1:T(8,128)}, f32[512,256]{0,1:T(8,128)}, f32[1...) async-done(((f32[2,2304,256]{2,1,0:T(8,128)}, f32[256,2048]{1,0:T(8,128)}, f32[512,512]{0,1:T(8,128)}, f32[512,256]{0,1:T(8,128)}, f32[1024,256]{1,0:T(8,128)}, ...) | async-done | bytes 9584656 | tf_op jit(solution)/shard_map/psum | solution.py:520
  (488 shorter events, 221.9 us)
Async XLA Ops:
  7.2 82.1 %all-gather.5.cloned.1.call-start = ((), (), s32[]{:S(2)}) async-start(), calls=%async_computation.4 | async-start | bytes 2654208 | tf_op jit(solution)/shard_map/all_gather | solution.py:384
  9.1 116.2 %all-gather.7.cloned.1.call-start = ((), (), s32[]{:S(2)}) async-start(), calls=%async_computation.5 | async-start | bytes 1179648 | tf_op jit(solution)/shard_map/all_gather | solution.py:385
  12.7 41.6 %collective-permute-start = (bf16[16,1,8]{1,2,0:T(8,128)(2,1)S(1)}, bf16[16,1,8]{1,2,0:T(8,128)(2,1)S(1)}, u32[]{:S(2)}, u32[]{:S(2)}) collective-permute-start(bf16[16,1,8]{1,2,0:T(8,128)(2,1)S(1)} %get-tuple-element.222), channel_id=1, source_target_pairs={{0,1},{1,2},{2,3},{4,5},{5,6},{6,7},{8,9},{9,10},{10,11},{12,13},{... | collective-permute-start | bytes 776 | tf_op jit(solution)/shard_map/ppermute | solution.py:38
  17.6 36.7 %collective-permute-start.1 = (bf16[16,1,8]{1,2,0:T(8,128)(2,1)S(1)}, bf16[16,1,8]{1,2,0:T(8,128)(2,1)S(1)}, u32[]{:S(2)}, u32[]{:S(2)}) collective-permute-start(bf16[16,1,8]{1,2,0:T(8,128)(2,1)S(1)} %get-tuple-element.223), channel_id=1, source_target_pairs={{1,0},{2,1},{3,2},{5,4},{6,5},{7,6},{9,8},{10,9},{11,10},{13,12},{... | collective-permute-start | bytes 776 | tf_op jit(solution)/shard_map/ppermute | solution.py:40
  71.7 2.7 collective-permute-start.2
  73.0 5.6 collective-permute-start.3
  104.9 13.8 %collective-permute-start.4 = (bf16[16,1,256]{2,1,0:T(2,128)(2,1)S(1)}, bf16[16,1,256]{2,1,0:T(2,128)(2,1)S(1)}, u32[]{:S(2)}, u32[]{:S(2)}) collective-permute-start(bf16[16,1,256]{2,1,0:T(2,128)(2,1)S(1)} %get-tuple-element.212), channel_id=1, source_target_pairs={{0,1},{1,2},{2,3},{4,5},{5,6},{6,7},{8,9},{9,10},{10,11},{12,13},{... | collective-permute-start | bytes 24584 | tf_op jit(solution)/shard_map/ppermute | solution.py:38
  107.9 10.8 %collective-permute-start.5 = (bf16[16,1,256]{2,1,0:T(2,128)(2,1)S(1)}, bf16[16,1,256]{2,1,0:T(2,128)(2,1)S(1)}, u32[]{:S(2)}, u32[]{:S(2)}) collective-permute-start(bf16[16,1,256]{2,1,0:T(2,128)(2,1)S(1)} %get-tuple-element.213), channel_id=1, source_target_pairs={{1,0},{2,1},{3,2},{5,4},{6,5},{7,6},{9,8},{10,9},{11,10},{13,12},{... | collective-permute-start | bytes 24584 | tf_op jit(solution)/shard_map/ppermute | solution.py:40
  124.6 180.8 %copy-start.1 = (f32[1024,256]{1,0:T(8,128)}, f32[1024,256]{1,0:T(8,128)S(1)}, u32[]{:S(2)}) copy-start(f32[1024,256]{1,0:T(8,128)S(1)} %get-tuple-element.240) | copy-start | bytes 3145732
  128.4 42.2 %all-to-all-start = ((bf16[1024,4,2,96]{0,3,2,1:T(8,128)(2,1)}), bf16[1024,4,2,96]{0,3,2,1:T(8,128)(2,1)}, u32[]{:S(2)}, u32[]{:S(2)}) async-start(bf16[1024,4,2,96]{0,3,2,1:T(8,128)(2,1)} %bitcast.228), calls=%async_computation | async-start | bytes 3145728 | tf_op jit(solution)/shard_map/all_to_all | solution.py:442
  181.0 110.7 %copy-start.38 = (f32[128,256]{1,0:T(8,128)S(1)}, f32[128,256]{1,0:T(8,128)}, u32[]{:S(2)}) copy-start(f32[128,256]{1,0:T(8,128)} %param.38) | copy-start | bytes 393220
  181.0 123.0 %copy-start.58 = (f32[288,8]{0,1:T(8,128)S(1)}, f32[288,8]{0,1:T(8,128)}, u32[]{:S(2)}) copy-start(f32[288,8]{0,1:T(8,128)} %param.40) | copy-start | bytes 27652
  246.9 57.7 %all-to-all-start.1 = ((bf16[4,1024,64]{1,2,0:T(8,128)(2,1)}), bf16[4,1024,64]{1,2,0:T(8,128)(2,1)S(1)}, u32[]{:S(2)}, u32[]{:S(2)}) async-start(bf16[4,1024,64]{1,2,0:T(8,128)(2,1)} %copy.285), calls=%async_computation.1 | async-start | bytes 1048576 | tf_op jit(solution)/shard_map/all_to_all | solution.py:451
  310.2 13.8 %collective-permute-start.6 = (bf16[16,1,256]{2,1,0:T(2,128)(2,1)S(1)}, bf16[16,1,256]{2,1,0:T(2,128)(2,1)S(1)}, u32[]{:S(2)}, u32[]{:S(2)}) collective-permute-start(bf16[16,1,256]{2,1,0:T(2,128)(2,1)S(1)} %get-tuple-element.210), channel_id=1, source_target_pairs={{0,1},{1,2},{2,3},{4,5},{5,6},{6,7},{8,9},{9,10},{10,11},{12,13},{... | collective-permute-start | bytes 24584 | tf_op jit(solution)/shard_map/ppermute | solution.py:38
  313.7 10.3 %collective-permute-start.7 = (bf16[16,1,256]{2,1,0:T(2,128)(2,1)S(1)}, bf16[16,1,256]{2,1,0:T(2,128)(2,1)S(1)}, u32[]{:S(2)}, u32[]{:S(2)}) collective-permute-start(bf16[16,1,256]{2,1,0:T(2,128)(2,1)S(1)} %get-tuple-element.211), channel_id=1, source_target_pairs={{1,0},{2,1},{3,2},{5,4},{6,5},{7,6},{9,8},{10,9},{11,10},{13,12},{... | collective-permute-start | bytes 24584 | tf_op jit(solution)/shard_map/ppermute | solution.py:40
  332.4 6.6 collective-permute-start.8
  336.9 5.8 collective-permute-start.9
  475.4 40.5 %all-to-all-start.3 = ((bf16[4,1024,192]{1,2,0:T(8,128)(2,1)}), bf16[4,1024,192]{1,2,0:T(8,128)(2,1)}, u32[]{:S(2)}, u32[]{:S(2)}) async-start(bf16[4,1024,192]{1,2,0:T(8,128)(2,1)} %copy.293), calls=%async_computation.3 | async-start | bytes 3145728 | tf_op jit(solution)/shard_map/all_to_all | solution.py:486
  479.7 322.6 %all-reduce.15.cloned.1.call-start = ((), (), s32[]{:S(2)}) async-start(), calls=%async_computation.6 | async-start | bytes 19283968 | tf_op jit(solution)/shard_map/psum | solution.py:520
  526.2 5.6 collective-permute-start.10
  527.6 5.6 collective-permute-start.11
  569.7 7.1 collective-permute-start.12
  571.0 5.8 collective-permute-start.13
  647.4 162.1 %copy-start.67 = (f32[8,256]{1,0:T(8,128)}, f32[8,256]{1,0:T(8,128)S(1)}, u32[]{:S(2)}) copy-start(f32[8,256]{1,0:T(8,128)S(1)} %get-tuple-element.163) | copy-start | bytes 24580
  (107 other events, 1696.1 us)
Sparse Core Ops, SparseCore 0:
  10.5 32.4 all-gather.4
  45.4 23.5 all-gather.6
  607.5 194.7 all-reduce.14

commit v2 on v1

--- a/solution.py
+++ b/solution.py
@@ -20,6 +20,7 @@
 
 EPS_NORM = 1e-05
 CLIP_NORM = 0.02
+DP = ("a", "b")
 RATE = 0.04
 BETA_ONE = 0.9
 BETA_TWO = 0.999
@@ -71,7 +72,7 @@
 
 def conv_forward(inputs, weight, masks_all):
     height, n_cols, n_in = inputs.shape
-    widened = with_halo(inputs, (("section", 1),), 1)
+    widened = with_halo(inputs, (("s", 1),), 1)
     padded = jnp.pad(widened, ((1, 1), (0, 0), (0, 0)))
     taps = [
         padded[tap_row : tap_row + height, tap_col : tap_col + n_cols]
@@ -85,7 +86,7 @@
 
 def conv_backward(d_out, weight, masks_all):
     height, n_cols, n_out = d_out.shape
-    widened = with_halo(d_out, (("section", 1),), 1)
+    widened = with_halo(d_out, (("s", 1),), 1)
     padded = jnp.pad(widened, ((1, 1), (0, 0), (0, 0)))
     taps = [
         padded[2 - tap_row : 2 - tap_row + height, 2 - tap_col : 2 - tap_col + n_cols]
@@ -103,7 +104,7 @@
     sum_two = (
         exact(onehot.T, jnp.sum(inputs * inputs, axis=0)).reshape(-1, GROUPS, per_group).sum(axis=2)
     )
-    sum_one, sum_two = lax.psum((sum_one, sum_two), "section")
+    sum_one, sum_two = lax.psum((sum_one, sum_two), "s")
     mean_row = sum_one / counts
     inv_std = lax.rsqrt(sum_two / counts - mean_row * mean_row + EPS_NORM)
     mean_col = jnp.repeat(exact(onehot, mean_row), per_group, axis=1)
@@ -118,7 +119,7 @@
     sum_two = (
         exact(onehot.T, jnp.sum(scaled * normed, axis=0)).reshape(-1, GROUPS, per_group).sum(axis=2)
     )
-    sum_one, sum_two = lax.psum((sum_one, sum_two), "section")
+    sum_one, sum_two = lax.psum((sum_one, sum_two), "s")
     mean_one = jnp.repeat(exact(onehot, sum_one / counts), per_group, axis=1)
     mean_two = jnp.repeat(exact(onehot, sum_two / counts), per_group, axis=1)
     d_in = std_col[None] * (scaled - mean_one[None] - normed * mean_two[None])
@@ -342,6 +343,230 @@
         ],
         compiler_params=pltpu.CompilerParams(vmem_limit_bytes=VMEM_LIMIT),
     )(*operands)
+
+
+MESH = pl.DeviceIdType.MESH
+
+
+def round_up(count, unit):
+    return -(-count // unit) * unit
+
+
+def greet(peers):
+    barrier = pltpu.get_barrier_semaphore()
+    for peer in peers:
+        pl.semaphore_signal(barrier, inc=1, device_id=peer, device_id_type=MESH)
+    pl.semaphore_wait(barrier, len(peers))
+
+
+def push(src, dst, sems, slot, peer):
+    copy = pltpu.make_async_remote_copy(
+        src_ref=src,
+        dst_ref=dst,
+        send_sem=sems.at[0, slot],
+        recv_sem=sems.at[1, slot],
+        device_id=peer,
+        device_id_type=MESH,
+    )
+    copy.start()
+    return copy
+
+
+def reduce_kernel(n_a, n_x, n_s, chunks, square_rows, *refs):
+    n_in = sum(len(parts) for parts in chunks)
+    n_chunk = len(chunks)
+    ins = refs[:n_in]
+    outs = refs[n_in : n_in + n_chunk]
+    norm_ref = refs[n_in + n_chunk]
+    scratch = list(refs[n_in + n_chunk + 1 :])
+    halves = scratch[:n_in]
+    accs, one_bufs, two_bufs, bit_bufs = (
+        scratch[n_in + i * n_chunk : n_in + (i + 1) * n_chunk] for i in range(4)
+    )
+    squares, sems = scratch[n_in + 4 * n_chunk :]
+    bits = n_s.bit_length() - 1
+    my_a, my_b, my_s = lax.axis_index("a"), lax.axis_index("b"), lax.axis_index("s")
+    core, my_x = lax.rem(my_b, 2), lax.div(my_b, 2)
+    n_b = 2 * n_x
+    n_d = n_a * n_b
+
+    def dp_peer(off):
+        place = lax.rem(my_a * n_b + my_b + off, n_d)
+        return {"a": lax.div(place, n_b), "b": lax.rem(place, n_b)}
+
+    def s_peer(bit):
+        flipped = my_s + (1 << bit) - 2 * (1 << bit) * lax.rem(lax.div(my_s, 1 << bit), 2)
+        return {"s": flipped}
+
+    greet([dp_peer(off) for off in range(1, n_d)] + [s_peer(bit) for bit in range(bits)])
+    slots = iter(range(sems.shape[1]))
+
+    first_in = []
+    at = 0
+    for parts in chunks:
+        first_in.append(at)
+        at += len(parts)
+
+    def core_send(c):
+        copies = []
+        for i in range(first_in[c], first_in[c] + len(chunks[c])):
+            copies.append(
+                push(ins[i].at[:, 1 - core], halves[i], sems, next(slots), {"b": my_b + 1 - 2 * core})
+            )
+        return copies
+
+    def core_sum(c):
+        acc = accs[c]
+        row = 0
+        for i in range(first_in[c], first_in[c] + len(chunks[c])):
+            rows, lanes = ins[i].shape[2:]
+            for lane in range(0, lanes, 256):
+                for j in range(n_a * n_x):
+                    acc[j // n_x, j % n_x, row : row + rows] = (
+                        ins[i][j, core, :, lane : lane + 256] + halves[i][j, :, lane : lane + 256]
+                    )
+                row += rows
+        if row < acc.shape[2]:
+            for j in range(n_a * n_x):
+                acc[j // n_x, j % n_x, row:] = jnp.zeros((acc.shape[2] - row, 256), jnp.float32)
+
+    def plane_send(c, stage):
+        over_x = (c + stage) % 2 == 0
+        buf = (one_bufs, two_bufs)[stage][c]
+        copies = []
+        for off in range(1, n_x if over_x else n_a):
+            if over_x:
+                there = lax.rem(my_x + off, n_x)
+                src = accs[c].at[:, there] if stage == 0 else accs[c].at[my_a, there]
+                peer = {"b": 2 * there + core}
+            else:
+                there = lax.rem(my_a + off, n_a)
+                src = accs[c].at[there] if stage == 0 else accs[c].at[there, my_x]
+                peer = {"a": there}
+            copies.append(push(src, buf.at[off - 1], sems, next(slots), peer))
+        return copies
+
+    def plane_sum(c, stage):
+        over_x = (c + stage) % 2 == 0
+        buf = (one_bufs, two_bufs)[stage][c]
+        for off in range(1, n_x if over_x else n_a):
+            if stage == 1:
+                accs[c][my_a, my_x] += buf[off - 1]
+            elif over_x:
+                for j in range(n_a):
+                    accs[c][j, my_x] += buf[off - 1, j]
+            else:
+                for j in range(n_x):
+                    accs[c][my_a, j] += buf[off - 1, j]
+
+    def span(c, level):
+        length = accs[c].shape[2]
+        start = 0
+        for bit in range(level):
+            length //= 2
+            start = start + lax.rem(lax.div(my_s, 1 << bit), 2) * length
+        return start, length
+
+    def s_send(c, bit):
+        start, length = span(c, bit)
+        length //= 2
+        mine = lax.rem(lax.div(my_s, 1 << bit), 2)
+        rows = pl.ds(pl.multiple_of(start + (1 - mine) * length, 8), length)
+        return [
+            push(
+                accs[c].at[my_a, my_x, rows],
+                bit_bufs[c].at[bit, pl.ds(0, length)],
+                sems,
+                next(slots),
+                s_peer(bit),
+            )
+        ]
+
+    def s_sum(c, bit):
+        start, length = span(c, bit + 1)
+        rows = pl.ds(pl.multiple_of(start, 8), length)
+        total = accs[c][my_a, my_x, rows] + bit_bufs[c][bit, :length]
+        if bit == bits - 1:
+            outs[c][rows] = total
+        else:
+            accs[c][my_a, my_x, rows] = total
+
+    def up_send(c, bit):
+        start, length = span(c, bit + 1)
+        rows = pl.ds(pl.multiple_of(start, 8), length)
+        return [push(outs[c].at[rows], outs[c].at[rows], sems, next(slots), s_peer(bit))]
+
+    steps = [(core_send, core_sum, ())]
+    steps += [(plane_send, plane_sum, (stage,)) for stage in range(2)]
+    steps += [(s_send, s_sum, (bit,)) for bit in range(bits)]
+    steps += [(up_send, None, (bit,)) for bit in reversed(range(bits))]
+    flying = [None] * n_chunk
+    for tick in range(n_chunk + len(steps)):
+        for c in range(n_chunk):
+            at = tick - c
+            if at < 0 or at > len(steps):
+                continue
+            if at > 0:
+                for copy in flying[c]:
+                    copy.wait()
+                if steps[at - 1][1] is not None:
+                    steps[at - 1][1](c, *steps[at - 1][2])
+            if at < len(steps):
+                flying[c] = steps[at][0](c, *steps[at][2])
+
+    lane = lax.broadcasted_iota(jnp.int32, (8, 256), 1)
+    total = jnp.zeros((8, 256), jnp.float32)
+    for c in range(n_chunk):
+        rows = square_rows[c]
+        total = total + jnp.sum((outs[c][:rows] * outs[c][:rows]).reshape(rows // 8, 8, 256), axis=0)
+    total = jnp.sum(jnp.sum(total, axis=0, keepdims=True), axis=1, keepdims=True)
+    last = square_rows[-1]
+    squares[my_a * n_b + my_b] = jnp.where(lane == 1, total, outs[-1][last : last + 8])
+    copies = []
+    for off in range(1, n_d):
+        place = squares.at[my_a * n_b + my_b]
+        copies.append(push(place, place, sems, next(slots), dp_peer(off)))
+    for copy in copies:
+        copy.wait()
+    total = squares[0]
+    for place in range(1, n_d):
+        total = total + squares[place]
+    norm_ref[...] = total
+
+
+def reduce_grads(chunks, square_rows, collective_id):
+    n_a, n_b, n_s = lax.axis_size("a"), lax.axis_size("b"), lax.axis_size("s")
+    n_x = n_b // 2
+    bits = n_s.bit_length() - 1
+    flat = [item for parts in chunks for item in parts]
+    heights = [
+        round_up(sum(item.shape[2] * item.shape[3] // 256 for item in parts), 8 * n_s)
+        for parts in chunks
+    ]
+    f32 = jnp.float32
+    one_shapes, two_shapes = [], []
+    for c, rows in enumerate(heights):
+        one_shapes.append((n_x - 1, n_a, rows, 256) if c % 2 == 0 else (n_a - 1, n_x, rows, 256))
+        two_shapes.append((n_a - 1, rows, 256) if c % 2 == 0 else (n_x - 1, rows, 256))
+    scratch = [(item.shape[0], *item.shape[2:]) for item in flat]
+    scratch += [(n_a, n_x, rows, 256) for rows in heights]
+    scratch += one_shapes + two_shapes
+    scratch += [(bits, rows // 2, 256) for rows in heights]
+    scratch += [(n_a * n_b, 8, 256)]
+    n_copy = len(flat) + len(chunks) * (n_x - 1 + n_a - 1 + 2 * bits) + n_a * n_b - 1
+    out = pl.pallas_call(
+        functools.partial(reduce_kernel, n_a, n_x, n_s, [[None] * len(parts) for parts in chunks], square_rows),
+        in_specs=[pl.BlockSpec(memory_space=pltpu.VMEM)] * len(flat),
+        out_specs=[pl.BlockSpec(memory_space=pltpu.VMEM)] * (len(chunks) + 1),
+        out_shape=[jax.ShapeDtypeStruct((rows, 256), f32) for rows in heights]
+        + [jax.ShapeDtypeStruct((8, 256), f32)],
+        scratch_shapes=[pltpu.VMEM(shape, f32) for shape in scratch]
+        + [pltpu.SemaphoreType.DMA((2, n_copy))],
+        compiler_params=pltpu.CompilerParams(
+            collective_id=collective_id, has_side_effects=True, vmem_limit_bytes=VMEM_LIMIT
+        ),
+    )(*flat)
+    return out[:-1], out[-1]
 
 
 def body(
@@ -381,14 +606,14 @@
     seconds = (conv_v, proj_v, film_v, skip_v, down_v, stem_v, head_v, gains_v)
     shard_dims = (1, 1, 1, 1, 0, 1, 0, 1)
     conv_b, proj_b, film_b, skip_b, down_b, stem_b, head_b, gain_b = (
-        lax.all_gather(conv_w.astype(bf16), "dp", axis=1, tiled=True),
-        lax.all_gather(proj_w.astype(bf16), "dp", axis=1, tiled=True),
-        lax.all_gather(film_w.astype(bf16), "dp", axis=1, tiled=True),
-        lax.all_gather(skip_w.astype(bf16), "dp", axis=1, tiled=True),
-        lax.all_gather(down_w.astype(bf16), "dp", axis=0, tiled=True),
-        lax.all_gather(stem_w.astype(bf16), "dp", axis=1, tiled=True),
-        lax.all_gather(head_w.astype(bf16), "dp", axis=0, tiled=True),
-        lax.all_gather(gains.astype(bf16), "dp", axis=1, tiled=True),
+        lax.all_gather(conv_w.astype(bf16), DP, axis=1, tiled=True),
+        lax.all_gather(proj_w.astype(bf16), DP, axis=1, tiled=True),
+        lax.all_gather(film_w.astype(bf16), DP, axis=1, tiled=True),
+        lax.all_gather(skip_w.astype(bf16), DP, axis=1, tiled=True),
+        lax.all_gather(down_w.astype(bf16), DP, axis=0, tiled=True),
+        lax.all_gather(stem_w.astype(bf16), DP, axis=1, tiled=True),
+        lax.all_gather(head_w.astype(bf16), DP, axis=0, tiled=True),
+        lax.all_gather(gains.astype(bf16), DP, axis=1, tiled=True),
     )
     gain_f = gain_b.astype(jnp.float32)
     clean_row = clean_lat[0]
@@ -396,11 +621,11 @@
     ids_row = column_ids[0]
     height, n_cols, _ = clean_row.shape
     n_pix = height * n_cols
-    section_size = lax.axis_size("section")
+    section_size = lax.axis_size("s")
     edge_pad = jnp.full((1,), -1, jnp.int32)
     ids_rim = lax.dynamic_slice_in_dim(
         jnp.concatenate([edge_pad, ids_row, edge_pad]),
-        lax.axis_index("section") * n_cols,
+        lax.axis_index("s") * n_cols,
         n_cols + 2,
     )
     own_ids = ids_rim[1 : n_cols + 1]
@@ -410,6 +635,7 @@
     full_onehot = (ids_row[:, None] == labels[None, :]).astype(jnp.float32)
     counts = jnp.maximum(jnp.sum(full_onehot, axis=0) * (height * (C // GROUPS)), 1.0)[:, None]
     clip_hot = onehot[:, :CLIPS]
+    pix_count = lax.psum(jnp.sum(full_onehot[:, :CLIPS]) * (height * CIN), DP)
     valid_cols = jnp.sum(clip_hot, axis=1)
     cond_vec, alpha_clip, sigma_clip = clip_terms(timesteps[0], clap_emb[0])
     alpha_col = exact(clip_hot, alpha_clip[:, None])[:, 0][None, :, None]
@@ -441,7 +667,7 @@
     ).reshape(-1)
     kept_heads = lax.all_to_all(
         qkv_rows.reshape(n_pix, section_size, HEADS // section_size, 3 * HD),
-        "section",
+        "s",
         split_axis=1,
         concat_axis=0,
         tiled=True,
@@ -449,7 +675,7 @@
     pixel_ids = pixel_ids[:, None]
     out_heads, log_total = attention_forward(kept_heads, pixel_ids)
     attended = lax.all_to_all(
-        out_heads, "section", split_axis=0, concat_axis=1, tiled=True
+        out_heads, "s", split_axis=0, concat_axis=1, tiled=True
     ).reshape(n_pix, C)
     mid_rows = base_rows + matmul(attended, proj_b[:, 3 * C : 4 * C])
     ln_two, normed_two, lstd_two = layer_forward(mid_rows, gain_f[6], gain_f[7])
@@ -463,35 +689,33 @@
     )
     residue = pred.reshape(height, n_cols, CIN) - target
     local_loss = jnp.sum(valid_cols[None, :, None] * residue * residue)
-    local_count = jnp.sum(valid_cols) * (height * CIN)
-    loss_sum, pix_count = lax.psum((local_loss, local_count), ("dp", "section"))
     d_pred = (2.0 * valid_cols[None, :, None] * residue / pix_count).astype(bf16)
     g_head = left_product(head_cols, d_pred.reshape(n_pix, CIN))
     d_top = conv_backward(d_pred, head_b, masks_all)
     d_top_b = d_top.astype(bf16)
     g_down = left_product(act_b, d_top_b)
     d_hidden = gelu_pull(matmul(d_top_b, down_b.T))[0].astype(bf16)
-    g_up = left_product(ln_two_b, d_hidden)
+    g_up = left_product(d_hidden, ln_two_b)
     d_ln_two, g_ln2_g, g_ln2_b = layer_backward(
         matmul(d_hidden, proj_b[:, 4 * C :].T), normed_two, lstd_two, gain_f[6]
     )
     d_mid = d_top + d_ln_two
     d_mid_b = d_mid.astype(bf16)
-    g_out = left_product(attended, d_mid_b)
+    g_out = left_product(d_mid_b, attended)
     d_att = matmul(d_mid_b, proj_b[:, 3 * C : 4 * C].T).astype(bf16)
     d_heads = lax.all_to_all(
-        d_att, "section", split_axis=1, concat_axis=0, tiled=True
+        d_att, "s", split_axis=1, concat_axis=0, tiled=True
     )
     d_qkv_heads = attention_backward(kept_heads, log_total, d_heads, out_heads, pixel_ids)
-    d_qkv = lax.all_to_all(d_qkv_heads, "section", split_axis=0, concat_axis=1, tiled=True).reshape(
+    d_qkv = lax.all_to_all(d_qkv_heads, "s", split_axis=0, concat_axis=1, tiled=True).reshape(
         n_pix, 3 * C
     )
-    g_qkv = left_product(ln_one_b, d_qkv)
+    g_qkv = left_product(d_qkv, ln_one_b)
     d_ln_one, g_ln1_g, g_ln1_b = layer_backward(
         matmul(d_qkv, proj_b[:, : 3 * C].T), normed_one, lstd_one, gain_f[4]
     )
     d_base = (d_mid + d_ln_one).astype(bf16)
-    g_skip = left_product(joined, d_base)
+    g_skip = left_product(d_base, joined)
     d_joined = matmul(d_base, skip_b.T)
     d_branch = d_joined[:, :C].astype(bf16)
     g_conv_two = left_product(cols_two, d_branch)
@@ -502,7 +726,7 @@
     d_scale = jnp.sum(d_pre_two * affine_two, axis=0)
     d_shift = jnp.sum(d_pre_two, axis=0)
     d_film = exact(clip_hot.T, jnp.concatenate([d_scale, d_shift], axis=1))
-    g_film = exact(cond_act.astype(jnp.float32).T, d_film)
+    g_film = exact(d_film.T, cond_act.astype(jnp.float32))
     d_inner, g_gn2_g, g_gn2_b = group_backward(
         d_pre_two * (1.0 + film_col[None, :, :C]), norm_two, std_two, gain_f[2], onehot, counts
     )
@@ -514,25 +738,67 @@
     )
     d_stem = (d_stem_gn.reshape(n_pix, C) + d_joined[:, :C] + d_joined[:, C:]).astype(bf16)
     g_stem = left_product(stem_cols, d_stem)
-    g_conv = jnp.stack([g_conv_one, g_conv_two])
-    g_proj = jnp.concatenate([g_qkv, g_out, g_up], axis=1)
+    n_dp = lax.axis_size(DP)
+    pairs = n_dp // 2
+
+    def shards_of(item):
+        return item.reshape(pairs, 2, -1, item.shape[-1])
+
+    def small_rows(item):
+        flat = item.reshape(n_dp, -1)
+        flat = jnp.pad(flat, ((0, 0), (0, round_up(flat.shape[1], 256) - flat.shape[1])))
+        return flat.reshape(n_dp, -1, 256)
+
     g_gains = jnp.stack([g_gn1_g, g_gn1_b, g_gn2_g, g_gn2_b, g_ln1_g, g_ln1_b, g_ln2_g, g_ln2_b])
-    totals = lax.psum(
-        (g_conv, g_proj, g_film, g_skip, g_down, g_stem, g_head, g_gains), ("dp", "section")
-    )
-    squares = sum((jnp.sum(item * item) for item in totals))
-    dp_size = lax.axis_size("dp")
-    dp_place = lax.axis_index("dp")
-    shards = tuple(
-        (
-            lax.dynamic_slice_in_dim(
-                item, dp_place * (item.shape[dim] // dp_size), item.shape[dim] // dp_size, dim
-            )
-            for item, dim in zip(totals, shard_dims)
-        )
-    )
+    smalls = [
+        small_rows(g_head),
+        small_rows(g_stem.reshape(-1, n_dp, C // n_dp).transpose(1, 0, 2)),
+        small_rows(g_gains.reshape(-1, n_dp, C // n_dp).transpose(1, 0, 2)),
+    ]
+    small_at = [0]
+    for item in smalls:
+        small_at.append(small_at[-1] + item.shape[1])
+    small_end = round_up(small_at[-1], 8)
+    loss_rows = jnp.zeros((n_dp, 8 + small_end - small_at[-1], 256), jnp.float32)
+    smalls.append(loss_rows.at[0, -8, 0].set(local_loss))
+    small = jnp.concatenate(smalls, axis=1)
+    g_proj = jnp.concatenate([g_qkv, g_out, g_up], axis=0)
+    chunks = [
+        [shards_of(g_conv_one)],
+        [shards_of(g_conv_two)],
+        [shards_of(g_proj)],
+        [shards_of(g_film), shards_of(g_skip), shards_of(g_down), shards_of(small)],
+    ]
+    heights = [sum(item.shape[2] * item.shape[3] // 256 for item in parts) for parts in chunks]
+    heights[3] -= 8
+    shards, sums = reduce_grads(chunks, heights, 0)
+    squares, loss_sum = sums[0, 1], sums[0, 0]
     grad_norm = jnp.sqrt(squares)
     factor = jnp.minimum(1.0, CLIP_NORM / grad_norm)
+    conv_rows, film_cols = 9 * C // n_dp, 2 * C // n_dp
+    skip_cols, down_rows = C // n_dp, 4 * C // n_dp
+    last = shards[3]
+    film_end, skip_end = 2 * film_cols, 2 * film_cols + 2 * skip_cols
+    film_shard = jnp.concatenate([last[:film_cols], last[film_cols:film_end]], axis=1).T
+    skip_shard = jnp.concatenate(
+        [last[film_end : film_end + skip_cols], last[film_end + skip_cols : skip_end]], axis=1
+    ).T
+    small_shard = last[skip_end + down_rows :]
+
+    def small_part(index, like):
+        rows = small_shard[small_at[index] : small_at[index + 1]].reshape(-1)
+        return rows[: like.size].reshape(like.shape)
+
+    shards = (
+        jnp.stack([shards[0][:conv_rows], shards[1][:conv_rows]]),
+        shards[2][: proj_w.shape[1]].T,
+        film_shard,
+        skip_shard,
+        last[skip_end : skip_end + down_rows],
+        small_part(1, stem_w),
+        small_part(0, head_w),
+        small_part(2, gains),
+    )
     new_w, new_m, new_v = ([], [], [])
     for weight, grad_one, m_old, v_old in zip(masters, shards, firsts, seconds):
         grad_one = grad_one * factor
@@ -576,65 +842,67 @@
 
 
 def solution(mesh):
+    n_dp, n_s = mesh.shape["dp"], mesh.shape["section"]
+    blocks = jax.sharding.Mesh(mesh.devices.reshape(n_dp // n_s, n_s, n_s), ("a", "b", "s"))
     return jax.shard_map(
         body,
-        mesh=mesh,
+        mesh=blocks,
         in_specs=(
-            P("dp", None, "section", None),
-            P("dp", None, "section", None),
-            P("dp", None),
-            P("dp", None),
-            P("dp", None, None),
-            P(None, "dp", None),
-            P(None, "dp"),
-            P(None, "dp"),
-            P(None, "dp"),
-            P("dp", None),
-            P(None, "dp"),
-            P("dp", None),
-            P(None, "dp"),
-            P(None, "dp", None),
-            P(None, "dp"),
-            P(None, "dp"),
-            P(None, "dp"),
-            P("dp", None),
-            P(None, "dp"),
-            P("dp", None),
-            P(None, "dp"),
-            P(None, "dp", None),
-            P(None, "dp"),
-            P(None, "dp"),
-            P(None, "dp"),
-            P("dp", None),
-            P(None, "dp"),
-            P("dp", None),
-            P(None, "dp"),
+            P(DP, None, "s", None),
+            P(DP, None, "s", None),
+            P(DP, None),
+            P(DP, None),
+            P(DP, None, None),
+            P(None, DP, None),
+            P(None, DP),
+            P(None, DP),
+            P(None, DP),
+            P(DP, None),
+            P(None, DP),
+            P(DP, None),
+            P(None, DP),
+            P(None, DP, None),
+            P(None, DP),
+            P(None, DP),
+            P(None, DP),
+            P(DP, None),
+            P(None, DP),
+            P(DP, None),
+            P(None, DP),
+            P(None, DP, None),
+            P(None, DP),
+            P(None, DP),
+            P(None, DP),
+            P(DP, None),
+            P(None, DP),
+            P(DP, None),
+            P(None, DP),
         ),
         out_specs=(
-            P(None, "dp", None),
-            P(None, "dp"),
-            P(None, "dp"),
-            P(None, "dp"),
-            P("dp", None),
-            P(None, "dp"),
-            P("dp", None),
-            P(None, "dp"),
-            P(None, "dp", None),
-            P(None, "dp"),
-            P(None, "dp"),
-            P(None, "dp"),
-            P("dp", None),
-            P(None, "dp"),
-            P("dp", None),
-            P(None, "dp"),
-            P(None, "dp", None),
-            P(None, "dp"),
-            P(None, "dp"),
-            P(None, "dp"),
-            P("dp", None),
-            P(None, "dp"),
-            P("dp", None),
-            P(None, "dp"),
+            P(None, DP, None),
+            P(None, DP),
+            P(None, DP),
+            P(None, DP),
+            P(DP, None),
+            P(None, DP),
+            P(DP, None),
+            P(None, DP),
+            P(None, DP, None),
+            P(None, DP),
+            P(None, DP),
+            P(None, DP),
+            P(DP, None),
+            P(None, DP),
+            P(DP, None),
+            P(None, DP),
+            P(None, DP, None),
+            P(None, DP),
+            P(None, DP),
+            P(None, DP),
+            P(DP, None),
+            P(None, DP),
+            P(DP, None),
+            P(None, DP),
             P(),
             P(),
             P(),

time: 853 us -> 731 us (0.86)
  waiting for transfers between devices: 216 us -> 43 us
  Pallas kernels: 162 us -> 281 us
  blocking collectives: 200 us -> 117 us
  local copies, waits for them, and re-layouts: 58.6 us -> 88.6 us
  other arithmetic: 68.8 us -> 56.9 us
    psum x1 -> x0, waiting for transfers between devices: 154 us -> none  [body(): lax.psum((g_conv, g_proj, g_film, g_skip, g_down, g_stem, g_head, g_gains...]
    pallas_call x0 -> x1, Pallas kernels: none -> 118 us  [reduce_grads(): pl.pallas_call(functools.partial(reduce_kernel, n_a, n_x, n_s, [[None] *...]
    psum x6 -> x5, blocking collectives: 125 us -> 60.3 us  [the longest x2 25.2 us: group_backward(): sum_one, sum_two = lax.psum((sum_one, sum_two), 's')]
    all_to_all x1 -> x0, blocking collectives: 16.9 us -> none  [body(): lax.all_to_all(d_att, 'section', split_axis=1, concat_axis=0, tiled=True)]
    all_to_all x2 -> x3, waiting for transfers between devices: 18.6 us -> 1.89 us  [the longest x1 1.88 us: body(): lax.all_to_all(d_qkv_heads, 's', split_axis=0, concat_axis=1, tiled=True)]
    reduce_sum x8 -> x1, other arithmetic: 14.5 us -> 0.6 us  [body(): pix_count = lax.psum(jnp.sum(full_onehot[:, :CLIPS]) * (height * CIN), DP)]
    dot_general x0 -> x3, local copies, waits for them, and re-layouts: none -> 13.5 us  [left_product(): lax.dot_general(lhs_mat, rhs_mat, (((0,), (0,)), ((), ())), preferred_ele...]
    unnamed x243 -> x241, local copies, waits for them, and re-layouts: 10.7 us -> 19.6 us
  transfers between devices with their start and end apart: 20 -> 20, of which waited for: 7 -> 5; matrix products, arithmetic and copies ran while one was open for 8% -> 15% of each run, Pallas kernels for 0% -> 0%
where the time goes in v2:
time: 731 us; the launch traced here: 728 us
  Pallas kernels  281 us (38%)
  blocking collectives  117 us (16%)
  local copies, waits for them, and re-layouts  88.6 us (12%)
  matrix products  76.4 us (10%)
  other arithmetic  56.9 us (8%)
  starting transfers between devices  47.3 us (6%)
  waiting for transfers between devices  43 us (6%)
  between operations  18.9 us (3%)
    pallas_call x1, Pallas kernels, reduce_grads(): pl.pallas_call(functools.partial(reduce_kernel, n_a, n_x, n_s, [[None] *...  118 us
    pallas_call x1, Pallas kernels, attention_backward(): pl.pallas_call(functools.partial(backward_kernel, heads, bq, bk), grid=(n...  98.7 us
    pallas_call x1, Pallas kernels, attention_forward(): pl.pallas_call(functools.partial(forward_kernel, heads, bq, bk), grid=(n_...  63.6 us
    dot_general x18, matrix products, matmul(): return jnp.dot(lhs_mat, rhs_mat, preferred_element_type=jnp.float32)  38.9 us
    all_to_all x1, waiting for transfers between devices, body(): lax.all_to_all(qkv_rows.reshape(n_pix, section_size, HEADS // section_siz...  33 us
    dot_general x9, matrix products, left_product(): lax.dot_general(lhs_mat, rhs_mat, (((0,), (0,)), ((), ())), preferred_ele...  25.9 us
    psum x2, blocking collectives, group_backward(): sum_one, sum_two = lax.psum((sum_one, sum_two), 's')  25.2 us
    psum x2, blocking collectives, group_forward(): sum_one, sum_two = lax.psum((sum_one, sum_two), 's')  21.9 us
  transfers between devices with their start and end apart: 20, of which 5 were waited for; matrix products, arithmetic and copies ran while one was open for 15% of the time, Pallas kernels for 0%

profile of v2, /device:TPU:0, one launch (start us, length us, event | category | flops | bytes accessed | tf_op | source)
XLA Modules:
  0.0 728.4 jit_solution(727176918984907961)
XLA Ops:
  13.2 4.9 collective-permute-start
  24.1 8.9 %all-gather = bf16[8,32,8]{1,2,0:T(8,128)(2,1)S(1)} all-gather(bf16[1,32,8]{1,2,0:T(8,128)(2,1)S(1)} %convert_bitcast_fusion.1), channel_id=1, replica_groups=mesh['a'=2,'b'=4,'s'=4] {'a','b'}, dimensions={0}, use_global_device_ids=true | all-gather | bytes 4608 | tf_op jit(solution)/shard_map/all_gather | solution.py:616
  34.6 10.6 %all_gather.27 = bf16[512,512]{0,1:T(8,128)(2,1)S(1)} all-gather(bf16[512,64]{0,1:T(8,128)(2,1)S(1)} %convert_element_type.140), channel_id=1, replica_groups=mesh['a'=2,'b'=4,'s'=4] {'a','b'}, dimensions={1}, use_global_device_ids=true | all-gather | bytes 589824 | tf_op jit(solution)/shard_map/all_gather | solution.py:611
  46.6 8.3 %all_gather.24 = bf16[72,256]{0,1:T(8,128)(2,1)S(1)} all-gather(bf16[72,32]{0,1:T(8,128)(2,1)S(1)} %convert_element_type.133), channel_id=1, replica_groups=mesh['a'=2,'b'=4,'s'=4] {'a','b'}, dimensions={1}, use_global_device_ids=true | all-gather | bytes 41472 | tf_op jit(solution)/shard_map/all_gather | solution.py:614
  58.0 12.6 %all-reduce.11 = (f32[5,32]{1,0:T(8,128)S(1)}, f32[5,32]{1,0:T(8,128)S(1)}) all-reduce(f32[5,32]{1,0:T(8,128)S(1)} %convolution_reduce_fusion.6, f32[5,32]{1,0:T(8,128)S(1)} %convolution_reduce_fusion.7), channel_id=1, replica_groups=mesh['a'=2,'b'=4,'s'=4] {'s'}, use_global_device_ids=true, to_apply=%region_6.7 | all-reduce | flops 320 | bytes 2560 | tf_op jit(solution)/shard_map/psum | solution.py:107
  94.6 9.4 %all-reduce.10 = (f32[5,32]{1,0:T(8,128)S(1)}, f32[5,32]{1,0:T(8,128)S(1)}) all-reduce(f32[5,32]{1,0:T(8,128)S(1)} %convolution_reduce_fusion.5, f32[5,32]{1,0:T(8,128)S(1)} %convolution_reduce_fusion.4), channel_id=1, replica_groups=mesh['a'=2,'b'=4,'s'=4] {'s'}, use_global_device_ids=true, to_apply=%region_9.10 | all-reduce | flops 320 | bytes 2560 | tf_op jit(solution)/shard_map/psum | solution.py:107
  109.5 9.5 %all_gather.28 = bf16[512,256]{0,1:T(8,128)(2,1)S(1)} all-gather(bf16[512,32]{0,1:T(8,128)(2,1)S(1)} %convert_element_type.142), channel_id=1, replica_groups=mesh['a'=2,'b'=4,'s'=4] {'a','b'}, dimensions={1}, use_global_device_ids=true | all-gather | bytes 294912 | tf_op jit(solution)/shard_map/all_gather | solution.py:612
  137.8 33.0 %all-to-all-done = bf16[1024,4,2,96]{0,3,2,1:T(8,128)(2,1)} async-done(((bf16[1024,4,2,96]{0,3,2,1:T(8,128)(2,1)}), bf16[1024,4,2,96]{0,3,2,1:T(8,128)(2,1)}, u32[]{:S(2)}, u32[]{:S(2)}) %all-to-all-start) | async-done | bytes 1572896 | tf_op jit(solution)/shard_map/all_to_all | solution.py:668
  170.9 6.1 copy.363
  181.3 63.6 %shard_map.484 = (bf16[4096,64]{1,0:T(8,128)(2,1)}, f32[4096,16]{1,0:T(8,128)}) custom-call(bf16[4096,192]{1,0:T(8,128)(2,1)} %reshape.429.x_ref, s32[4096,1]{1,0:T(8,128)} %broadcast_in_dim_reshape.3.ids_ref), custom_call_target="tpu_custom_call" | custom-call | tf_op jit(solution)/shard_map/pallas_call | solution.py:234
  252.1 13.2 %psum.67 = f32[]{:T(128)} all-reduce(f32[]{:T(128)S(6)} %mul.1161), channel_id=1, replica_groups=mesh['a'=2,'b'=4,'s'=4] {'a','b'}, use_global_device_ids=true, to_apply=%region_19.20 | all-reduce | flops 1 | bytes 8 | tf_op jit(solution)/shard_map/psum | solution.py:638
  265.3 9.9 %all_gather.30 = bf16[1024,256]{1,0:T(8,128)(2,1)} all-gather(bf16[128,256]{1,0:T(8,128)(2,1)S(1)} %convert_element_type.148), channel_id=1, replica_groups=mesh['a'=2,'b'=4,'s'=4] {'a','b'}, dimensions={0}, use_global_device_ids=true | all-gather | bytes 589824 | tf_op jit(solution)/shard_map/all_gather | solution.py:613
  286.4 9.1 %all-gather.1 = bf16[8,288,8]{1,2,0:T(8,128)(2,1)S(1)} all-gather(bf16[1,288,8]{1,2,0:T(8,128)(2,1)S(1)} %convert_bitcast_fusion), channel_id=1, replica_groups=mesh['a'=2,'b'=4,'s'=4] {'a','b'}, dimensions={0}, use_global_device_ids=true | all-gather | bytes 41472 | tf_op jit(solution)/shard_map/all_gather | solution.py:615
  304.6 4.5 collective-permute-start.8
  317.2 5.5 fusion.6
  338.0 6.6 copy.305
  347.0 98.7 %shard_map.485 = bf16[4096,192]{1,0:T(8,128)(2,1)} custom-call(bf16[4096,192]{1,0:T(8,128)(2,1)} %reshape.429.x_ref, s32[4096,1]{1,0:T(8,128)} %broadcast_in_dim_reshape.3.ids_ref, bf16[4096,64]{1,0:T(8,128)(2,1)} %bitcast.296, bf16[4096,64]{1,0:T(8,128)(2,1)} %get-tuple-element.46.o_ref, f32[4096,16]{1,0:T(8,128)} %get-tuple-element.47.lse_ref), custom_call_target="tpu_custom_call" | custom-call | tf_op jit(solution)/shard_map/pallas_call | solution.py:333
  449.7 5.0 all-to-all-start.3
  462.7 6.7 copy.332
  469.4 6.1 convolution_bitcast_fusion
  519.2 13.7 %all-reduce.9 = (f32[5,32]{1,0:T(8,128)}, f32[5,32]{1,0:T(8,128)S(1)}) all-reduce(f32[5,32]{1,0:T(8,128)S(1)} %convolution_reduce_fusion.2, f32[5,32]{1,0:T(8,128)} %convolution_reduce_fusion.3), channel_id=1, replica_groups=mesh['a'=2,'b'=4,'s'=4] {'s'}, use_global_device_ids=true, to_apply=%region_29.30 | all-reduce | flops 320 | bytes 2560 | tf_op jit(solution)/shard_map/psum | solution.py:122
  542.1 5.3 fusion.225.refs_0_
  558.8 11.5 %all-reduce.8 = (f32[5,32]{1,0:T(8,128)S(1)}, f32[5,32]{1,0:T(8,128)S(1)}) all-reduce(f32[5,32]{1,0:T(8,128)S(1)} %convolution_reduce_fusion, f32[5,32]{1,0:T(8,128)S(1)} %convolution_reduce_fusion.1), channel_id=1, replica_groups=mesh['a'=2,'b'=4,'s'=4] {'s'}, use_global_device_ids=true, to_apply=%region_37.38 | all-reduce | flops 320 | bytes 2560 | tf_op jit(solution)/shard_map/psum | solution.py:122
  578.2 118.4 %shard_map.486 = (f32[288,256]{1,0:T(8,128)}, f32[288,256]{1,0:T(8,128)}, f32[256,256]{1,0:T(8,128)}, f32[352,256]{1,0:T(8,128)}, f32[8,256]{1,0:T(8,128)}) custom-call(f32[4,2,288,256]{3,2,1,0:T(8,128)} %fusion.225.refs_0_, f32[4,2,288,256]{3,2,1,0:T(8,128)} %fusion.61.refs_1_, f32[4,2,256,256]{3,2,1,0:T(8,128)} %bitcast.286, ...), custom_call_target="tpu_custom_call" | custom-call | tf_op jit(solution)/shard_map/pallas_call | solution.py:557
  (507 shorter events, 228.3 us)
Async XLA Ops:
  7.2 82.3 %all-gather.5.cloned.1.call-start = ((), (), s32[]{:S(2)}) async-start(), calls=%async_computation.4 | async-start | bytes 2654208 | tf_op jit(solution)/shard_map/all_gather | solution.py:609
  9.1 116.5 %all-gather.7.cloned.1.call-start = ((), (), s32[]{:S(2)}) async-start(), calls=%async_computation.5 | async-start | bytes 1179648 | tf_op jit(solution)/shard_map/all_gather | solution.py:610
  13.2 41.6 %collective-permute-start = (bf16[16,1,8]{1,2,0:T(8,128)(2,1)S(1)}, bf16[16,1,8]{1,2,0:T(8,128)(2,1)S(1)}, u32[]{:S(2)}, u32[]{:S(2)}) collective-permute-start(bf16[16,1,8]{1,2,0:T(8,128)(2,1)S(1)} %get-tuple-element.268), channel_id=1, source_target_pairs={{0,1},{1,2},{2,3},{4,5},{5,6},{6,7},{8,9},{9,10},{10,11},{12,13},{... | collective-permute-start | bytes 776 | tf_op jit(solution)/shard_map/ppermute | solution.py:39
  18.1 36.7 %collective-permute-start.1 = (bf16[16,1,8]{1,2,0:T(8,128)(2,1)S(1)}, bf16[16,1,8]{1,2,0:T(8,128)(2,1)S(1)}, u32[]{:S(2)}, u32[]{:S(2)}) collective-permute-start(bf16[16,1,8]{1,2,0:T(8,128)(2,1)S(1)} %get-tuple-element.269), channel_id=1, source_target_pairs={{1,0},{2,1},{3,2},{5,4},{6,5},{7,6},{9,8},{10,9},{11,10},{13,12},{... | collective-permute-start | bytes 776 | tf_op jit(solution)/shard_map/ppermute | solution.py:41
  71.8 2.7 collective-permute-start.2
  73.1 5.6 collective-permute-start.3
  105.2 13.8 %collective-permute-start.4 = (bf16[16,1,256]{2,1,0:T(2,128)(2,1)S(1)}, bf16[16,1,256]{2,1,0:T(2,128)(2,1)S(1)}, u32[]{:S(2)}, u32[]{:S(2)}) collective-permute-start(bf16[16,1,256]{2,1,0:T(2,128)(2,1)S(1)} %get-tuple-element.252), channel_id=1, source_target_pairs={{0,1},{1,2},{2,3},{4,5},{5,6},{6,7},{8,9},{9,10},{10,11},{12,13},{... | collective-permute-start | bytes 24584 | tf_op jit(solution)/shard_map/ppermute | solution.py:39
  108.2 10.8 %collective-permute-start.5 = (bf16[16,1,256]{2,1,0:T(2,128)(2,1)S(1)}, bf16[16,1,256]{2,1,0:T(2,128)(2,1)S(1)}, u32[]{:S(2)}, u32[]{:S(2)}) collective-permute-start(bf16[16,1,256]{2,1,0:T(2,128)(2,1)S(1)} %get-tuple-element.253), channel_id=1, source_target_pairs={{1,0},{2,1},{3,2},{5,4},{6,5},{7,6},{9,8},{10,9},{11,10},{13,12},{... | collective-permute-start | bytes 24584 | tf_op jit(solution)/shard_map/ppermute | solution.py:41
  124.9 151.7 %copy-start = (f32[1024,256]{1,0:T(8,128)}, f32[1024,256]{1,0:T(8,128)S(1)}, u32[]{:S(2)}) copy-start(f32[1024,256]{1,0:T(8,128)S(1)} %get-tuple-element.290) | copy-start | bytes 3145732
  128.7 42.2 %all-to-all-start = ((bf16[1024,4,2,96]{0,3,2,1:T(8,128)(2,1)}), bf16[1024,4,2,96]{0,3,2,1:T(8,128)(2,1)}, u32[]{:S(2)}, u32[]{:S(2)}) async-start(bf16[1024,4,2,96]{0,3,2,1:T(8,128)(2,1)} %bitcast.287), calls=%async_computation | async-start | bytes 3145728 | tf_op jit(solution)/shard_map/all_to_all | solution.py:668
  247.2 28.5 %all-to-all-start.1 = ((bf16[4,1024,64]{1,2,0:T(8,128)(2,1)}), bf16[4,1024,64]{1,2,0:T(8,128)(2,1)S(1)}, u32[]{:S(2)}, u32[]{:S(2)}) async-start(bf16[4,1024,64]{1,2,0:T(8,128)(2,1)} %copy.316), calls=%async_computation.1 | async-start | bytes 1048576 | tf_op jit(solution)/shard_map/all_to_all | solution.py:677
  281.5 14.7 %collective-permute-start.6 = (bf16[16,1,256]{2,1,0:T(2,128)(2,1)S(1)}, bf16[16,1,256]{2,1,0:T(2,128)(2,1)S(1)}, u32[]{:S(2)}, u32[]{:S(2)}) collective-permute-start(bf16[16,1,256]{2,1,0:T(2,128)(2,1)S(1)} %get-tuple-element.250), channel_id=1, source_target_pairs={{0,1},{1,2},{2,3},{4,5},{5,6},{6,7},{8,9},{9,10},{10,11},{12,13},{... | collective-permute-start | bytes 24584 | tf_op jit(solution)/shard_map/ppermute | solution.py:39
  285.1 11.1 %collective-permute-start.7 = (bf16[16,1,256]{2,1,0:T(2,128)(2,1)S(1)}, bf16[16,1,256]{2,1,0:T(2,128)(2,1)S(1)}, u32[]{:S(2)}, u32[]{:S(2)}) collective-permute-start(bf16[16,1,256]{2,1,0:T(2,128)(2,1)S(1)} %get-tuple-element.251), channel_id=1, source_target_pairs={{1,0},{2,1},{3,2},{5,4},{6,5},{7,6},{9,8},{10,9},{11,10},{13,12},{... | collective-permute-start | bytes 24584 | tf_op jit(solution)/shard_map/ppermute | solution.py:41
  304.6 6.6 collective-permute-start.8
  309.2 5.8 collective-permute-start.9
  326.3 18.4 %all-to-all-start.2 = ((bf16[1024,4,64]{0,2,1:T(8,128)(2,1)}), bf16[1024,4,64]{0,2,1:T(8,128)(2,1)}, u32[]{:S(2)}, u32[]{:S(2)}) async-start(bf16[1024,4,64]{0,2,1:T(8,128)(2,1)} %bitcast.298), calls=%async_computation.2 | async-start | bytes 1048576 | tf_op jit(solution)/shard_map/all_to_all | solution.py:706
  449.7 40.9 %all-to-all-start.3 = ((bf16[4,1024,192]{1,2,0:T(8,128)(2,1)}), bf16[4,1024,192]{1,2,0:T(8,128)(2,1)}, u32[]{:S(2)}, u32[]{:S(2)}) async-start(bf16[4,1024,192]{1,2,0:T(8,128)(2,1)} %copy.324), calls=%async_computation.3 | async-start | bytes 3145728 | tf_op jit(solution)/shard_map/all_to_all | solution.py:710
  498.5 10.5 %collective-permute-start.10 = (bf16[16,1,256]{2,1,0:T(2,128)(2,1)S(1)}, bf16[16,1,256]{2,1,0:T(2,128)(2,1)S(1)}, u32[]{:S(2)}, u32[]{:S(2)}) collective-permute-start(bf16[16,1,256]{2,1,0:T(2,128)(2,1)S(1)} %get-tuple-element.248), channel_id=1, source_target_pairs={{0,1},{1,2},{2,3},{4,5},{5,6},{6,7},{8,9},{9,10},{10,11},{12,13},{... | collective-permute-start | bytes 24584 | tf_op jit(solution)/shard_map/ppermute | solution.py:39
  500.5 8.5 %collective-permute-start.11 = (bf16[16,1,256]{2,1,0:T(2,128)(2,1)S(1)}, bf16[16,1,256]{2,1,0:T(2,128)(2,1)S(1)}, u32[]{:S(2)}, u32[]{:S(2)}) collective-permute-start(bf16[16,1,256]{2,1,0:T(2,128)(2,1)S(1)} %get-tuple-element.249), channel_id=1, source_target_pairs={{1,0},{2,1},{3,2},{5,4},{6,5},{7,6},{9,8},{10,9},{11,10},{13,12},{... | collective-permute-start | bytes 24584 | tf_op jit(solution)/shard_map/ppermute | solution.py:41
  538.2 12.3 %collective-permute-start.12 = (bf16[16,1,256]{2,1,0:T(2,128)(2,1)S(1)}, bf16[16,1,256]{2,1,0:T(2,128)(2,1)S(1)}, u32[]{:S(2)}, u32[]{:S(2)}) collective-permute-start(bf16[16,1,256]{2,1,0:T(2,128)(2,1)S(1)} %get-tuple-element.246), channel_id=1, source_target_pairs={{0,1},{1,2},{2,3},{4,5},{5,6},{6,7},{8,9},{9,10},{10,11},{12,13},{... | collective-permute-start | bytes 24584 | tf_op jit(solution)/shard_map/ppermute | solution.py:39
  539.5 11.0 %collective-permute-start.13 = (bf16[16,1,256]{2,1,0:T(2,128)(2,1)S(1)}, bf16[16,1,256]{2,1,0:T(2,128)(2,1)S(1)}, u32[]{:S(2)}, u32[]{:S(2)}) collective-permute-start(bf16[16,1,256]{2,1,0:T(2,128)(2,1)S(1)} %get-tuple-element.247), channel_id=1, source_target_pairs={{1,0},{2,1},{3,2},{5,4},{6,5},{7,6},{9,8},{10,9},{11,10},{13,12},{... | collective-permute-start | bytes 24584 | tf_op jit(solution)/shard_map/ppermute | solution.py:41
  578.2 127.3 %copy-start.25 = (f32[256,256]{0,1:T(8,128)S(1)}, f32[256,256]{0,1:T(8,128)}, u32[]{:S(2)}) copy-start(f32[256,256]{0,1:T(8,128)} %copy.347) | copy-start | bytes 786436
  578.2 127.3 %copy-start.26 = (f32[256,256]{0,1:T(8,128)S(1)}, f32[256,256]{0,1:T(8,128)}, u32[]{:S(2)}) copy-start(f32[256,256]{0,1:T(8,128)} %copy.344) | copy-start | bytes 786436
  578.2 127.3 %copy-start.27 = (f32[256,256]{0,1:T(8,128)S(1)}, f32[256,256]{0,1:T(8,128)}, u32[]{:S(2)}) copy-start(f32[256,256]{0,1:T(8,128)} %copy.345) | copy-start | bytes 786436
  (103 other events, 1731.1 us)
Sparse Core Ops, SparseCore 0:
  10.5 32.4 all-gather.4
  45.4 23.3 all-gather.6

commit v3 on v2

v3 whole, which is shorter than its diff:
```python
import functools
import math

import jax
import jax.numpy as jnp
from jax import lax
from jax.experimental import pallas as pl
from jax.experimental.pallas import tpu as pltpu
from jax.sharding import PartitionSpec as P

CIN = 8
C = 256
HEADS = 8
HD = 32
COND = 512
GROUPS = 32
CLIPS = 4
STEP = 10


EPS_NORM = 1e-05
CLIP_NORM = 0.02
DP = ("a", "b")
RATE = 0.04
BETA_ONE = 0.9
BETA_TWO = 0.999
ADAM_EPS = 1e-08
DECAY = 0.1


def matmul(lhs_mat, rhs_mat):
    return jnp.dot(lhs_mat, rhs_mat, preferred_element_type=jnp.float32)


def left_product(lhs_mat, rhs_mat):
    return lax.dot_general(
        lhs_mat, rhs_mat, (((0,), (0,)), ((), ())), preferred_element_type=jnp.float32
    )


def exact(lhs_mat, rhs_mat):
    return jnp.dot(
        lhs_mat, rhs_mat, precision=lax.Precision.HIGHEST, preferred_element_type=jnp.float32
    )


def contract(lhs_mat, rhs_mat, lhs_dim, rhs_dim):
    return lax.dot_general(
        lhs_mat, rhs_mat, (((lhs_dim,), (rhs_dim,)), ((), ())), preferred_element_type=jnp.float32
    )


def silu_pull(x, d_out):
    gate = jax.nn.sigmoid(x)
    return d_out * (gate + x * gate * (1.0 - gate))


def clip_terms(timesteps, clap_emb):
    half_cond = COND // 2
    frequency = jnp.exp(-math.log(10000.0) * jnp.arange(half_cond, dtype=jnp.float32) / half_cond)
    angles = timesteps.astype(jnp.float32)[:, None] * frequency[None]
    cond_vec = clap_emb + jnp.concatenate([jnp.sin(angles), jnp.cos(angles)], axis=1)
    theta_clip = 0.5 * math.pi * (timesteps.astype(jnp.float32) + 1.0) / 1001.0
    return (cond_vec, jnp.cos(theta_clip), jnp.sin(theta_clip))


def layer_forward(inputs, gain_row, bias_row):
    mean_row = jnp.mean(inputs, axis=1, keepdims=True)
    centered = inputs - mean_row
    inv_std = lax.rsqrt(jnp.mean(centered * centered, axis=1, keepdims=True) + EPS_NORM)
    normed = centered * inv_std
    return (normed * gain_row + bias_row, normed, inv_std)


def layer_backward(d_out, normed, inv_std, gain_row):
    scaled = d_out * gain_row
    d_in = inv_std * (
        scaled
        - jnp.mean(scaled, axis=1, keepdims=True)
        - normed * jnp.mean(scaled * normed, axis=1, keepdims=True)
    )
    return (d_in, jnp.sum(d_out * normed, axis=0), jnp.sum(d_out, axis=0))


BIG = 1e30
LOG2E = 1.4426950408889634
SCALE = HD**-0.5 * LOG2E
VMEM_LIMIT = 56 << 20
NN = (((1,), (0,)), ((), ()))
NT = (((1,), (1,)), ((), ()))


def mxu(lhs_mat, rhs_mat, dims=NN):
    return lax.dot_general(lhs_mat, rhs_mat, dims, preferred_element_type=jnp.float32)


def split_three(value):
    high = value.astype(jnp.bfloat16).astype(jnp.float32)
    rest = value - high
    mid = rest.astype(jnp.bfloat16).astype(jnp.float32)
    return high, mid, rest - mid


def rows_of(height, parts):
    row = lax.broadcasted_iota(jnp.int32, (height, parts[0].shape[1]), 0)
    total = jnp.zeros(row.shape, jnp.float32)
    for place, part in enumerate(parts):
        total = jnp.where(row == place, part, total)
    return total


def clip_rows(ids, hit, miss):
    return [jnp.where(ids == clip, hit, miss) for clip in range(CLIPS + 1)]


def forward_kernel(heads, bq, bk, x_ref, ids_ref, out_ref, lse_ref, keys):
    n_pix = x_ref.shape[1]
    step = pl.program_id(0)

    @pl.when(step == 0)
    def _():
        for head in range(heads):
            base = 3 * HD * head
            for start in range(0, n_pix, 512):
                cols = slice(start, start + 512)
                key = x_ref[base + HD : base + 2 * HD, cols].astype(jnp.float32)
                marks = rows_of(32, clip_rows(ids_ref[:, cols], 1.0, 0.0))
                stack = jnp.concatenate([key, marks, jnp.zeros((64, 512), jnp.float32)], axis=0)
                keys[head, cols, :] = stack.T.astype(jnp.bfloat16)

    block = pl.ds(pl.multiple_of(step * bq, bq), bq)
    marks = rows_of(32, clip_rows(ids_ref[:, block], 0.0, -BIG)).astype(jnp.bfloat16)
    for head in range(heads):
        base = 3 * HD * head
        query = jnp.concatenate([x_ref[base : base + HD, block], marks], axis=0)
        total = jnp.zeros((8, bq), jnp.float32)
        acc = jnp.zeros((HD, bq), jnp.float32)
        row_max = jnp.full((1, bq), -jnp.inf, jnp.float32)
        for start in range(0, n_pix, bk):
            scores = mxu(keys[head, start : start + bk, :64], query)
            new_max = jnp.maximum(row_max, jnp.max(scores, axis=0, keepdims=True) * SCALE)
            probs = jnp.exp2(scores * SCALE - new_max)
            decay = jnp.exp2(row_max - new_max)
            total = total * decay + jnp.sum(probs.reshape(bk // 8, 8, bq), axis=0)
            value = x_ref[base + 2 * HD : base + 3 * HD, start : start + bk]
            acc = acc * decay + mxu(value, probs.astype(jnp.bfloat16))
            row_max = new_max
        total = jnp.sum(total, axis=0, keepdims=True)
        out_ref[HD * head : HD * (head + 1), :] = (acc / total).astype(jnp.bfloat16)
        lse_ref[8 * head : 8 * (head + 1), :] = jnp.broadcast_to(row_max + jnp.log2(total), (8, bq))


def attention_forward(heads_x, pixel_ids):
    lanes, n_pix = heads_x.shape
    heads = lanes // (3 * HD)
    bq, bk = min(2048, n_pix), min(512, n_pix)
    return pl.pallas_call(
        functools.partial(forward_kernel, heads, bq, bk),
        grid=(n_pix // bq,),
        in_specs=[
            pl.BlockSpec((lanes, n_pix), lambda i: (0, 0)),
            pl.BlockSpec((1, n_pix), lambda i: (0, 0)),
        ],
        out_specs=[
            pl.BlockSpec((heads * HD, bq), lambda i: (0, i)),
            pl.BlockSpec((heads * 8, bq), lambda i: (0, i)),
        ],
        out_shape=[
            jax.ShapeDtypeStruct((heads * HD, n_pix), jnp.bfloat16),
            jax.ShapeDtypeStruct((heads * 8, n_pix), jnp.float32),
        ],
        scratch_shapes=[pltpu.VMEM((heads, n_pix, 128), jnp.bfloat16)],
        compiler_params=pltpu.CompilerParams(vmem_limit_bytes=VMEM_LIMIT),
    )(heads_x, pixel_ids)


def backward_kernel(
    heads, bq, bk, x_ref, ids_ref, do_ref, o_ref, lse_ref, out_ref,
    queries, keys, values, d_outs, d_query, query_rows, d_out_rows,
):
    n_pix = x_ref.shape[1]
    step = pl.program_id(0)

    @pl.when(step == 0)
    def _():
        d_query[...] = jnp.zeros_like(d_query)
        for head in range(heads):
            base = 3 * HD * head

            def prepare(part, carry):
                cols = pl.ds(pl.multiple_of(part * 512, 512), 512)
                ids = ids_ref[:, cols]
                one = jnp.ones((1, 512), jnp.float32)
                key = x_ref[base + HD : base + 2 * HD, cols].astype(jnp.float32)
                marks = rows_of(32, clip_rows(ids, 1.0, 0.0) + [one, one, one])
                stack = jnp.concatenate([key, key, key, marks], axis=0)
                keys[head, cols, :] = stack.T.astype(jnp.bfloat16)
                value = x_ref[base + 2 * HD : base + 3 * HD, cols].astype(jnp.float32)
                stack = jnp.concatenate(
                    [value, rows_of(32, [one, one, one]), jnp.zeros((64, 512), jnp.float32)], axis=0
                )
                values[head, cols, :] = stack.T.astype(jnp.bfloat16)
                query = x_ref[base : base + HD, cols].astype(jnp.float32) * SCALE
                lse = lse_ref[8 * head : 8 * head + 1, cols]
                marks = rows_of(32, clip_rows(ids, 0.0, -BIG) + list(split_three(-lse)))
                stack = jnp.concatenate([*split_three(query), marks], axis=0)
                queries[head, :, cols] = stack.astype(jnp.bfloat16)
                d_out = do_ref[HD * head : HD * (head + 1), cols].astype(jnp.float32)
                out = o_ref[HD * head : HD * (head + 1), cols].astype(jnp.float32)
                delta = jnp.sum(d_out * out, axis=0, keepdims=True)
                stack = jnp.concatenate([d_out, rows_of(32, split_three(-delta))], axis=0)
                d_outs[head, :, cols] = stack.astype(jnp.bfloat16)
                zero = jnp.zeros((96, 512), jnp.float32)
                query = x_ref[base : base + HD, cols].astype(jnp.float32)
                query_rows[head, cols, :] = jnp.concatenate([query, zero], 0).T.astype(jnp.bfloat16)
                d_out_rows[head, cols, :] = jnp.concatenate([d_out, zero], 0).T.astype(jnp.bfloat16)
                return carry

            lax.fori_loop(0, n_pix // 512, prepare, 0)

    block = pl.ds(pl.multiple_of(step * bk, bk), bk)
    for head in range(heads):
        base = 3 * HD * head
        key, value = keys[head, block, :], values[head, block, :64]
        key_t = x_ref[base + HD : base + 2 * HD, block]
        d_value = jnp.zeros((bk, 128), jnp.float32)
        d_key = jnp.zeros((bk, 128), jnp.float32)
        for start in range(0, n_pix, bq):
            cols = slice(start, start + bq)
            probs = jnp.exp2(mxu(key, queries[head, :, cols]))
            d_scores = (probs * mxu(value, d_outs[head, :, cols])).astype(jnp.bfloat16)
            probs = probs.astype(jnp.bfloat16)
            d_value += mxu(probs, d_out_rows[head, cols, :])
            d_key += mxu(d_scores, query_rows[head, cols, :])
            d_query[head, :, cols] += mxu(key_t, d_scores)
        d_key, d_value = d_key.T[:HD], d_value.T[:HD]
        out_ref[base + HD : base + 2 * HD, block] = (d_key * (HD**-0.5)).astype(jnp.bfloat16)
        out_ref[base + 2 * HD : base + 3 * HD, block] = d_value.astype(jnp.bfloat16)

    @pl.when(step == pl.num_programs(0) - 1)
    def _():
        for head in range(heads):
            base = 3 * HD * head
            out_ref[base : base + HD, :] = (d_query[head] * (HD**-0.5)).astype(jnp.bfloat16)


def attention_backward(heads_x, log_total, d_heads, out_heads, pixel_ids, bq=1024, bk=1024):
    lanes, n_pix = heads_x.shape
    heads = lanes // (3 * HD)
    bq, bk = min(bq, n_pix), min(bk, n_pix)
    operands = (heads_x, pixel_ids, d_heads, out_heads, log_total)
    return pl.pallas_call(
        functools.partial(backward_kernel, heads, bq, bk),
        grid=(n_pix // bk,),
        in_specs=[pl.BlockSpec(item.shape, lambda i: (0, 0)) for item in operands],
        out_specs=pl.BlockSpec((lanes, n_pix), lambda i: (0, 0)),
        out_shape=jax.ShapeDtypeStruct((lanes, n_pix), jnp.bfloat16),
        scratch_shapes=[
            pltpu.VMEM((heads, 128, n_pix), jnp.bfloat16),
            pltpu.VMEM((heads, n_pix, 128), jnp.bfloat16),
            pltpu.VMEM((heads, n_pix, 128), jnp.bfloat16),
            pltpu.VMEM((heads, 64, n_pix), jnp.bfloat16),
            pltpu.VMEM((heads, HD, n_pix), jnp.float32),
            pltpu.VMEM((heads, n_pix, 128), jnp.bfloat16),
            pltpu.VMEM((heads, n_pix, 128), jnp.bfloat16),
        ],
        compiler_params=pltpu.CompilerParams(vmem_limit_bytes=VMEM_LIMIT),
    )(*operands)


MESH = pl.DeviceIdType.MESH


def round_up(count, unit):
    return -(-count // unit) * unit


def greet(peers):
    barrier = pltpu.get_barrier_semaphore()
    for peer in peers:
        pl.semaphore_signal(barrier, inc=1, device_id=peer, device_id_type=MESH)
    pl.semaphore_wait(barrier, len(peers))


def push(src, dst, sems, slot, peer):
    copy = pltpu.make_async_remote_copy(
        src_ref=src,
        dst_ref=dst,
        send_sem=sems.at[0, slot],
        recv_sem=sems.at[1, slot],
        device_id=peer,
        device_id_type=MESH,
    )
    copy.start()
    return copy


def reduce_kernel(n_a, n_x, n_s, chunks, square_rows, *refs):
    n_in = sum(len(parts) for parts in chunks)
    n_chunk = len(chunks)
    ins = refs[:n_in]
    outs = refs[n_in : n_in + n_chunk]
    norm_ref = refs[n_in + n_chunk]
    scratch = list(refs[n_in + n_chunk + 1 :])
    halves = scratch[:n_in]
    accs = scratch[n_in : n_in + n_chunk]
    one_bufs = scratch[n_in + n_chunk : n_in + 3 * n_chunk]
    two_bufs = scratch[n_in + 3 * n_chunk : n_in + 5 * n_chunk]
    bit_bufs = scratch[n_in + 5 * n_chunk : n_in + 6 * n_chunk]
    squares, sems = scratch[n_in + 6 * n_chunk :]
    bits = n_s.bit_length() - 1
    my_a, my_b, my_s = lax.axis_index("a"), lax.axis_index("b"), lax.axis_index("s")
    core, my_x = lax.rem(my_b, 2), lax.div(my_b, 2)
    n_b = 2 * n_x
    n_d = n_a * n_b

    def dp_peer(off):
        place = lax.rem(my_a * n_b + my_b + off, n_d)
        return {"a": lax.div(place, n_b), "b": lax.rem(place, n_b)}

    def s_peer(bit):
        flipped = my_s + (1 << bit) - 2 * (1 << bit) * lax.rem(lax.div(my_s, 1 << bit), 2)
        return {"s": flipped}

    greet([dp_peer(off) for off in range(1, n_d)] + [s_peer(bit) for bit in range(bits)])
    slots = iter(range(sems.shape[1]))

    first_in = []
    at = 0
    for parts in chunks:
        first_in.append(at)
        at += len(parts)

    def core_send(c):
        copies = []
        for i in range(first_in[c], first_in[c] + len(chunks[c])):
            copies.append(
                push(ins[i].at[:, 1 - core], halves[i], sems, next(slots), {"b": my_b + 1 - 2 * core})
            )
        return copies

    def core_sum(c):
        acc = accs[c]
        row = 0
        for i in range(first_in[c], first_in[c] + len(chunks[c])):
            rows, lanes = ins[i].shape[2:]
            for lane in range(0, lanes, 256):
                for j in range(n_a * n_x):
                    acc[j // n_x, j % n_x, row : row + rows] = (
                        ins[i][j, core, :, lane : lane + 256] + halves[i][j, :, lane : lane + 256]
                    )
                row += rows
        if row < acc.shape[2]:
            for j in range(n_a * n_x):
                acc[j // n_x, j % n_x, row:] = jnp.zeros((acc.shape[2] - row, 256), jnp.float32)

    def plane_moves(c, stage):
        rows = accs[c].shape[2] // 2
        for half in range(2):
            over_x = (half + stage) % 2 == 0
            for off in range(1, n_x if over_x else n_a):
                yield half, over_x, off, pl.ds(half * rows, rows)

    def plane_buf(c, stage, half, off):
        return (one_bufs, two_bufs)[stage][2 * c + half].at[off - 1]

    def plane_send(c, stage):
        copies = []
        for half, over_x, off, rows in plane_moves(c, stage):
            acc = accs[c]
            if over_x:
                there = lax.rem(my_x + off, n_x)
                src = acc.at[:, there, rows] if stage == 0 else acc.at[my_a, there, rows]
                peer = {"b": 2 * there + core}
            else:
                there = lax.rem(my_a + off, n_a)
                src = acc.at[there, :, rows] if stage == 0 else acc.at[there, my_x, rows]
                peer = {"a": there}
            copies.append(push(src, plane_buf(c, stage, half, off), sems, next(slots), peer))
        return copies

    def plane_sum(c, stage):
        for half, over_x, off, rows in plane_moves(c, stage):
            buf = plane_buf(c, stage, half, off)
            if stage == 1:
                accs[c][my_a, my_x, rows] += buf[...]
            elif over_x:
                for j in range(n_a):
                    accs[c][j, my_x, rows] += buf[j]
            else:
                for j in range(n_x):
                    accs[c][my_a, j, rows] += buf[j]

    def span(c, level):
        length = accs[c].shape[2]
        start = 0
        for bit in range(level):
            length //= 2
            start = start + lax.rem(lax.div(my_s, 1 << bit), 2) * length
        return start, length

    def s_send(c, bit):
        start, length = span(c, bit)
        length //= 2
        mine = lax.rem(lax.div(my_s, 1 << bit), 2)
        rows = pl.ds(pl.multiple_of(start + (1 - mine) * length, 8), length)
        return [
            push(
                accs[c].at[my_a, my_x, rows],
                bit_bufs[c].at[bit, pl.ds(0, length)],
                sems,
                next(slots),
                s_peer(bit),
            )
        ]

    def s_sum(c, bit):
        start, length = span(c, bit + 1)
        rows = pl.ds(pl.multiple_of(start, 8), length)
        total = accs[c][my_a, my_x, rows] + bit_bufs[c][bit, :length]
        if bit == bits - 1:
            outs[c][rows] = total
        else:
            accs[c][my_a, my_x, rows] = total

    def up_send(c, bit):
        start, length = span(c, bit + 1)
        rows = pl.ds(pl.multiple_of(start, 8), length)
        return [push(outs[c].at[rows], outs[c].at[rows], sems, next(slots), s_peer(bit))]

    steps = [(core_send, core_sum, ())]
    steps += [(plane_send, plane_sum, (stage,)) for stage in range(2)]
    steps += [(s_send, s_sum, (bit,)) for bit in range(bits)]
    steps += [(up_send, None, (bit,)) for bit in reversed(range(bits))]
    flying = [None] * n_chunk
    for tick in range(n_chunk + len(steps)):
        for c in range(n_chunk):
            at = tick - c
            if at < 0 or at > len(steps):
                continue
            if at > 0:
                for copy in flying[c]:
                    copy.wait()
                if steps[at - 1][1] is not None:
                    steps[at - 1][1](c, *steps[at - 1][2])
            if at < len(steps):
                flying[c] = steps[at][0](c, *steps[at][2])

    lane = lax.broadcasted_iota(jnp.int32, (8, 256), 1)
    total = jnp.zeros((8, 256), jnp.float32)
    for c in range(n_chunk):
        rows = square_rows[c]
        total = total + jnp.sum((outs[c][:rows] * outs[c][:rows]).reshape(rows // 8, 8, 256), axis=0)
    total = jnp.sum(jnp.sum(total, axis=0, keepdims=True), axis=1, keepdims=True)
    last = square_rows[-1]
    squares[my_a * n_b + my_b] = jnp.where(lane == 1, total, outs[-1][last : last + 8])
    copies = []
    for off in range(1, n_d):
        place = squares.at[my_a * n_b + my_b]
        copies.append(push(place, place, sems, next(slots), dp_peer(off)))
    for copy in copies:
        copy.wait()
    total = squares[0]
    for place in range(1, n_d):
        total = total + squares[place]
    norm_ref[...] = total


def reduce_grads(chunks, square_rows, collective_id):
    n_a, n_b, n_s = lax.axis_size("a"), lax.axis_size("b"), lax.axis_size("s")
    n_x = n_b // 2
    bits = n_s.bit_length() - 1
    flat = [item for parts in chunks for item in parts]
    heights = [
        round_up(sum(item.shape[2] * item.shape[3] // 256 for item in parts), 16 * max(n_s // 2, 1))
        for parts in chunks
    ]
    f32 = jnp.float32
    one_shapes, two_shapes = [], []
    for rows in heights:
        half = rows // 2
        one_shapes += [(n_x - 1, n_a, half, 256), (n_a - 1, n_x, half, 256)]
        two_shapes += [(n_a - 1, half, 256), (n_x - 1, half, 256)]
    scratch = [(item.shape[0], *item.shape[2:]) for item in flat]
    scratch += [(n_a, n_x, rows, 256) for rows in heights]
    scratch += one_shapes + two_shapes
    scratch += [(bits, rows // 2, 256) for rows in heights]
    scratch += [(n_a * n_b, 8, 256)]
    n_copy = len(flat) + len(chunks) * 2 * (n_x - 1 + n_a - 1 + bits) + n_a * n_b - 1
    out = pl.pallas_call(
        functools.partial(reduce_kernel, n_a, n_x, n_s, [[None] * len(parts) for parts in chunks], square_rows),
        in_specs=[pl.BlockSpec(memory_space=pltpu.VMEM)] * len(flat),
        out_specs=[pl.BlockSpec(memory_space=pltpu.VMEM)] * (len(chunks) + 1),
        out_shape=[jax.ShapeDtypeStruct((rows, 256), f32) for rows in heights]
        + [jax.ShapeDtypeStruct((8, 256), f32)],
        scratch_shapes=[pltpu.VMEM(shape, f32) for shape in scratch]
        + [pltpu.SemaphoreType.DMA((2, n_copy))],
        compiler_params=pltpu.CompilerParams(
            collective_id=collective_id, has_side_effects=True, vmem_limit_bytes=VMEM_LIMIT
        ),
    )(*flat)
    return out[:-1], out[-1]


def exchange_kernel(n_b, has_stats, has_edges, *refs):
    refs = list(refs)
    take = lambda count: [refs.pop(0) for _ in range(count)]
    stats_in, edges_in = take(has_stats), take(2 * has_edges)
    stats_out, edges_out = take(has_stats), take(2 * has_edges)
    held = take(has_stats)
    (sems,) = refs
    me = lax.axis_index("b")
    peers = [{"b": lax.rem(me + off, n_b)} for off in range(1, n_b)]
    greet(peers)
    copies = []
    if has_edges:
        first, last = edges_in
        left, right = edges_out
        copies.append(push(last, left, sems, n_b - 1, {"b": lax.rem(me + 1, n_b)}))
        copies.append(push(first, right, sems, n_b, {"b": lax.rem(me + n_b - 1, n_b)}))
    if has_stats:
        held[0][me] = stats_in[0][...]
        for slot, peer in enumerate(peers):
            copies.append(push(stats_in[0], held[0].at[me], sems, slot, peer))
    for copy in copies:
        copy.wait()
    if has_stats:
        total = held[0][0]
        for place in range(1, n_b):
            total = total + held[0][place]
        stats_out[0][...] = total


def exchange(collective_id, stats=None, edges=None):
    n_b = lax.axis_size("b")
    operands = ([] if stats is None else [stats]) + ([] if edges is None else list(edges))
    shapes = [jax.ShapeDtypeStruct(item.shape, item.dtype) for item in operands]
    scratch = [] if stats is None else [pltpu.VMEM((n_b, *stats.shape), stats.dtype)]
    vmem = pl.BlockSpec(memory_space=pltpu.VMEM)
    return pl.pallas_call(
        functools.partial(exchange_kernel, n_b, int(stats is not None), int(edges is not None)),
        in_specs=[vmem] * len(operands),
        out_specs=[vmem] * len(operands),
        out_shape=shapes,
        scratch_shapes=scratch + [pltpu.SemaphoreType.DMA((2, n_b + 1))],
        compiler_params=pltpu.CompilerParams(collective_id=collective_id, has_side_effects=True),
    )(*operands)


def swap_kernel(n_b, spread, x_ref, out_ref, sems, own_sem):
    me = lax.axis_index("b")
    peers = [lax.rem(me + off, n_b) for off in range(1, n_b)]
    greet([{"b": peer} for peer in peers])
    rows = (x_ref if spread else out_ref).shape[0] // n_b
    cols = (out_ref if spread else x_ref).shape[1] // n_b

    def tall(ref, place):
        return ref.at[pl.ds(pl.multiple_of(place * rows, 16), rows)]

    def wide(ref, place):
        return ref.at[:, pl.ds(pl.multiple_of(place * cols, 128), cols)]

    source, target = (tall, wide) if spread else (wide, tall)
    copies = [
        push(source(x_ref, peer), target(out_ref, me), sems, slot, {"b": peer})
        for slot, peer in enumerate(peers)
    ]
    own = pltpu.make_async_copy(source(x_ref, me), target(out_ref, me), own_sem)
    own.start()
    for copy in copies:
        copy.wait()
    own.wait()


def swap(x, spread, collective_id):
    n_b = lax.axis_size("b")
    rows, cols = x.shape
    shape = (rows // n_b, cols * n_b) if spread else (rows * n_b, cols // n_b)
    return pl.pallas_call(
        functools.partial(swap_kernel, n_b, spread),
        in_specs=[pl.BlockSpec(memory_space=pl.ANY)],
        out_specs=pl.BlockSpec(memory_space=pl.ANY),
        out_shape=jax.ShapeDtypeStruct(shape, x.dtype),
        scratch_shapes=[pltpu.SemaphoreType.DMA((2, n_b - 1)), pltpu.SemaphoreType.DMA(())],
        compiler_params=pltpu.CompilerParams(collective_id=collective_id, has_side_effects=True),
    )(x)


def opening_kernel(n_a, n_b, n_gather, *refs):
    main, first, last = refs[:3]
    shards = refs[3 : 3 + n_gather]
    main_out, left, right = refs[3 + n_gather : 6 + n_gather]
    wholes = refs[6 + n_gather : 6 + 2 * n_gather]
    (sems,) = refs[6 + 2 * n_gather :]
    my_a, my_b, my_s = lax.axis_index("a"), lax.axis_index("b"), lax.axis_index("s")
    n_d = n_a * n_b
    place = my_a * n_b + my_b

    def at(b, s):
        return {"b": lax.rem(b + n_b, n_b), "s": lax.rem(s + n_b, n_b)}

    dp_peers = []
    for off in range(1, n_d):
        there = lax.rem(place + off, n_d)
        dp_peers.append({"a": lax.div(there, n_b), "b": lax.rem(there, n_b)})
    mirrored = my_b != my_s
    shift = jnp.where(mirrored, 0, 1)
    greet(
        dp_peers
        + [at(my_s + 1, my_b), at(my_s - 1, my_b), at(my_s, my_b + 1), at(my_s, my_b - 1)]
        + [at(my_s + shift, my_b + shift)]
    )

    @pl.when(mirrored)
    def _():
        push(main, main_out, sems, 0, at(my_s, my_b))

    @pl.when(jnp.logical_not(mirrored))
    def _():
        main_out[...] = main[...]

    copies = [
        push(last, left, sems, 1, at(my_s + 1, my_b)),
        push(first, right, sems, 2, at(my_s - 1, my_b)),
    ]
    slot = 3
    for shard, whole in zip(shards, wholes):
        rows = shard.shape[0]
        mine = pl.ds(pl.multiple_of(place * rows, 8), rows)
        for peer in dp_peers:
            copies.append(push(shard, whole.at[mine], sems, slot, peer))
            slot += 1
        whole[mine] = shard[...]
    for copy in copies:
        copy.wait()

    @pl.when(mirrored)
    def _():
        pltpu.make_async_remote_copy(
            src_ref=main,
            dst_ref=main_out,
            send_sem=sems.at[0, 0],
            recv_sem=sems.at[1, 0],
            device_id=at(my_s, my_b),
            device_id_type=MESH,
        ).wait()


def opening(main, first, last, shards, collective_id):
    n_a, n_b = lax.axis_size("a"), lax.axis_size("b")
    n_d = n_a * n_b
    operands = [main, first, last, *shards]
    shapes = [jax.ShapeDtypeStruct(item.shape, item.dtype) for item in operands[:3]]
    shapes += [jax.ShapeDtypeStruct((n_d * item.shape[0], item.shape[1]), item.dtype) for item in shards]
    vmem = pl.BlockSpec(memory_space=pltpu.VMEM)
    return pl.pallas_call(
        functools.partial(opening_kernel, n_a, n_b, len(shards)),
        in_specs=[vmem] * len(operands),
        out_specs=[vmem] * len(operands),
        out_shape=shapes,
        scratch_shapes=[pltpu.SemaphoreType.DMA((2, 3 + len(shards) * (n_d - 1)))],
        compiler_params=pltpu.CompilerParams(collective_id=collective_id, has_side_effects=True),
    )(*operands)


def conv_forward(widened, weight, masks_all):
    height, n_wide, n_in = widened.shape
    n_cols = n_wide - 2
    padded = jnp.pad(widened, ((1, 1), (0, 0), (0, 0)))
    taps = [
        padded[tap_row : tap_row + height, tap_col : tap_col + n_cols]
        * masks_all[tap_col][None, :, None]
        for tap_row in range(3)
        for tap_col in range(3)
    ]
    columns = jnp.concatenate(taps, axis=2).reshape(height * n_cols, 9 * n_in)
    return columns, weight(columns)


def conv_backward(widened, weight, masks_all):
    height, n_wide, n_out = widened.shape
    n_cols = n_wide - 2
    padded = jnp.pad(widened, ((1, 1), (0, 0), (0, 0)))
    taps = [
        padded[2 - tap_row : 2 - tap_row + height, 2 - tap_col : 2 - tap_col + n_cols]
        * masks_all[2 - tap_col][None, :, None]
        for tap_row in range(3)
        for tap_col in range(3)
    ]
    flipped = weight.reshape(9, -1, n_out).transpose(0, 2, 1).reshape(9 * n_out, -1)
    return matmul(jnp.concatenate(taps, axis=2).reshape(height * n_cols, 9 * n_out), flipped)


def group_sums(one, two, onehot):
    per_group = one.shape[2] // GROUPS

    def fold(item):
        return exact(onehot.T, jnp.sum(item, axis=0)).reshape(-1, GROUPS, per_group).sum(axis=2)

    sums = jnp.concatenate([fold(one), fold(two)], axis=1)
    return jnp.pad(sums, ((0, 8 - sums.shape[0]), (0, 128 - sums.shape[1])))


def group_rows(sums, counts):
    return sums[: CLIPS + 1, :GROUPS] / counts, sums[: CLIPS + 1, GROUPS : 2 * GROUPS] / counts


def per_column(onehot, values):
    return jnp.repeat(exact(onehot, values), C // GROUPS, axis=1)


def edges_of(item, width=1):
    count = item.shape[1]
    return item[:, :width].reshape(item.shape[0], -1), item[:, count - width :].reshape(
        item.shape[0], -1
    )


def widen(item, left, right):
    height, _, chans = item.shape
    left, right = (side.reshape(height, -1, chans) for side in (left, right))
    return jnp.concatenate([left, item, right], axis=1)


def group_forward(inputs, onehot, wide_hot, counts, collective_id):
    sums, left, right = exchange(
        collective_id, group_sums(inputs, inputs * inputs, onehot), edges_of(inputs)
    )
    mean_row, square_row = group_rows(sums, counts)
    inv_std = lax.rsqrt(square_row - mean_row * mean_row + EPS_NORM)
    mean_col, std_col = per_column(wide_hot, mean_row), per_column(wide_hot, inv_std)
    return (widen(inputs, left, right) - mean_col[None]) * std_col[None], std_col


def group_backward(d_out, normed, std_col, gain_row, onehot, wide_hot, counts, collective_id, wide):
    own = normed[:, 1:-1]
    scaled = d_out * gain_row
    sums = group_sums(scaled, scaled * own, onehot)
    if wide:
        sums, left, right = exchange(collective_id, sums, edges_of(scaled))
        scaled = widen(scaled, left, right)
        hot = wide_hot
    else:
        (sums,) = exchange(collective_id, sums)
        normed, std_col, hot = own, std_col[1:-1], onehot
    one_row, two_row = group_rows(sums, counts)
    mean_one, mean_two = per_column(hot, one_row), per_column(hot, two_row)
    d_in = std_col[None] * (scaled - mean_one[None] - normed * mean_two[None])
    return d_in, jnp.sum(d_out * own, axis=(0, 1)), jnp.sum(d_out, axis=(0, 1))


def body(
    clean_lat,
    noise_lat,
    column_ids,
    timesteps,
    clap_emb,
    conv_w,
    proj_w,
    film_w,
    skip_w,
    down_w,
    stem_w,
    head_w,
    gains,
    conv_m,
    proj_m,
    film_m,
    skip_m,
    down_m,
    stem_m,
    head_m,
    gains_m,
    conv_v,
    proj_v,
    film_v,
    skip_v,
    down_v,
    stem_v,
    head_v,
    gains_v,
):
    bf16, f32 = jnp.bfloat16, jnp.float32
    masters = (conv_w, proj_w, film_w, skip_w, down_w, stem_w, head_w, gains)
    firsts = (conv_m, proj_m, film_m, skip_m, down_m, stem_m, head_m, gains_m)
    seconds = (conv_v, proj_v, film_v, skip_v, down_v, stem_v, head_v, gains_v)
    n_dp, n_s = lax.axis_size(DP), lax.axis_size("s")
    conv_b = [lax.all_gather(conv_w[i].astype(bf16), DP, axis=0, tiled=True) for i in range(2)]
    head_size = head_w.size
    head_rows = round_up(round_up(head_size, 256) // 256, 16)
    head_flat = jnp.pad(head_w.reshape(-1), (0, head_rows * 256 - head_size)).reshape(-1, 256)
    late = jnp.concatenate([proj_w.T, down_w, head_flat], axis=0).astype(bf16)
    late = lax.all_gather(late, DP, axis=0, tiled=False)
    proj_cols, down_rows = proj_w.shape[1], down_w.shape[0]
    proj_t = late[:, :proj_cols].reshape(-1, C)
    down_b = late[:, proj_cols : proj_cols + down_rows].reshape(-1, C)
    head_b = late[:, proj_cols + down_rows :].reshape(n_dp, -1)[:, :head_size].reshape(-1, CIN)

    _, height, n_cols, _ = clean_lat.shape
    n_pix = height * n_cols
    wide = n_cols * CIN
    extra = jnp.concatenate(
        [column_ids[0].astype(f32), timesteps[0].astype(f32), clap_emb[0].reshape(-1)]
    )
    extra_rows = round_up(-(-extra.size // wide), 8)
    extra = jnp.pad(extra, (0, extra_rows * wide - extra.size)).reshape(-1, wide)
    both = jnp.concatenate([clean_lat[0], noise_lat[0]], axis=0)
    pack = jnp.concatenate([both.reshape(2 * height, wide), extra], axis=0)
    first, last = (
        jnp.pad(both[:, at], ((0, 0), (0, 128 - CIN))) for at in (0, n_cols - 1)
    )
    own_count = jnp.sum((column_ids < CLIPS).astype(f32)) * (height * CIN)
    stem_rows = stem_w.shape[0]
    front = jnp.concatenate([stem_w, gains], axis=0)
    front = jnp.pad(front, ((0, 128 - front.shape[0]), (0, 0))).T.astype(bf16)
    pack, left, right, film_t, skip_t, front, counts_all = opening(
        pack,
        first,
        last,
        [film_w.T.astype(bf16), skip_w.T.astype(bf16), front, jnp.full((8, 128), own_count)],
        0,
    )
    pix_count = jnp.sum(counts_all.reshape(n_dp, 8, 128)[:, 0, 0])
    stem_t = front[:, :stem_rows]
    gain_f = front[:, stem_rows : stem_rows + 8].T.astype(f32)
    both = pack[: 2 * height].reshape(2 * height, n_cols, CIN)
    both = jnp.concatenate([left[:, None, :CIN], both, right[:, None, :CIN]], axis=1)
    clean_row, noise_row = both[:height], both[height:]
    extra = pack[2 * height :].reshape(-1)
    row_cols = column_ids.shape[1]
    ids_row = extra[:row_cols].astype(jnp.int32)
    times = extra[row_cols : row_cols + CLIPS]
    emb = extra[row_cols + CLIPS : row_cols + CLIPS + CLIPS * COND].reshape(CLIPS, COND)

    edge_pad = jnp.full((2,), -1, jnp.int32)
    ids_rim = lax.dynamic_slice_in_dim(
        jnp.concatenate([edge_pad, ids_row, edge_pad]), lax.axis_index("b") * n_cols, n_cols + 4
    )
    own_ids, wide_ids = ids_rim[2:-2], ids_rim[1:-1]
    masks_all = [(ids_rim[1 + at : 1 + at + n_cols] == own_ids).astype(bf16) for at in range(3)]
    wide_masks = [(ids_rim[at : at + n_cols + 2] == wide_ids).astype(bf16) for at in range(3)]
    labels = jnp.arange(CLIPS + 1)
    wide_hot = (wide_ids[:, None] == labels[None, :]).astype(f32)
    onehot = wide_hot[1:-1]
    full_onehot = (ids_row[:, None] == labels[None, :]).astype(f32)
    counts = jnp.maximum(jnp.sum(full_onehot, axis=0) * (height * (C // GROUPS)), 1.0)[:, None]
    clip_hot = onehot[:, :CLIPS]
    wide_clips = wide_hot[:, :CLIPS]
    wide_valid = jnp.sum(wide_clips, axis=1)
    cond_vec, alpha_clip, sigma_clip = clip_terms(times, emb)
    alpha_col = exact(wide_clips, alpha_clip[:, None])[:, 0][None, :, None]
    sigma_col = exact(wide_clips, sigma_clip[:, None])[:, 0][None, :, None]
    noisy_in = alpha_col * clean_row + sigma_col * noise_row
    target = alpha_col * noise_row - sigma_col * clean_row
    stem_cols, stem = conv_forward(
        noisy_in.astype(bf16), lambda cols: mxu(cols, stem_t, NT), masks_all
    )
    stem = stem.reshape(height, n_cols, C)
    norm_one, std_one = group_forward(stem, onehot, wide_hot, counts, 1)
    act_one = norm_one * gain_f[0] + gain_f[1]
    first_act = jax.nn.silu(act_one).astype(bf16)
    cols_one, inner_out = conv_forward(first_act, lambda cols: matmul(cols, conv_b[0]), masks_all)
    inner_out = inner_out.reshape(height, n_cols, C)
    cond_act = jax.nn.silu(cond_vec).astype(bf16)
    film_col = exact(wide_clips, mxu(cond_act, film_t, NT))
    norm_two, std_two = group_forward(inner_out, onehot, wide_hot, counts, 2)
    affine_two = norm_two * gain_f[2] + gain_f[3]
    act_two = affine_two * (1.0 + film_col[None, :, :C]) + film_col[None, :, C:]
    second = jax.nn.silu(act_two).astype(bf16)
    cols_two, branch = conv_forward(second, lambda cols: matmul(cols, conv_b[1]), masks_all)
    stem_rows_f = stem.reshape(n_pix, C)
    joined = jnp.concatenate([stem_rows_f + branch, stem_rows_f], axis=1).astype(bf16)
    base_rows = mxu(joined, skip_t, NT)
    ln_one, normed_one, lstd_one = layer_forward(base_rows, gain_f[4], gain_f[5])
    ln_one_b = ln_one.astype(bf16)
    proj_qkv, proj_out, proj_up = proj_t[: 3 * C], proj_t[3 * C : 4 * C], proj_t[4 * C :]
    qkv_t = mxu(proj_qkv, ln_one_b, NT).astype(bf16)
    pixel_ids = jnp.broadcast_to(
        ids_row.reshape(n_s, 1, n_cols), (n_s, height, n_cols)
    ).reshape(1, -1)
    heads_x = swap(qkv_t, True, 3)
    out_heads, log_total = attention_forward(heads_x, pixel_ids)
    attended_t = swap(out_heads, False, 4)
    mid_rows = base_rows + contract(attended_t, proj_out, 0, 1)
    ln_two, normed_two, lstd_two = layer_forward(mid_rows, gain_f[6], gain_f[7])
    ln_two_b = ln_two.astype(bf16)
    hidden = mxu(ln_two_b, proj_up, NT)
    act_out, gelu_pull = jax.vjp(jax.nn.gelu, hidden)
    act_b = act_out.astype(bf16)
    top_rows = mid_rows + matmul(act_b, down_b)
    top_b = top_rows.reshape(height, n_cols, C).astype(bf16)
    left, right = exchange(5, None, edges_of(top_b, 2))
    head_cols, pred = conv_forward(
        widen(top_b, left, right), lambda cols: matmul(cols, head_b), wide_masks
    )
    residue = pred.reshape(height, n_cols + 2, CIN) - target
    weighted = wide_valid[None, :, None] * residue
    local_loss = jnp.sum((weighted * residue)[:, 1:-1])
    d_pred = (2.0 * weighted / pix_count).astype(bf16)
    d_own = jnp.pad(d_pred[:, 1:-1], ((0, 0), (1, 1), (0, 0)))
    g_head = left_product(head_cols, d_own.reshape(-1, CIN))
    d_top = conv_backward(d_pred, head_b, masks_all)
    d_top_b = d_top.astype(bf16)
    g_down = left_product(act_b, d_top_b)
    d_hidden = gelu_pull(matmul(d_top_b, down_b.T))[0].astype(bf16)
    g_up = left_product(d_hidden, ln_two_b)
    d_ln_two, g_ln2_g, g_ln2_b = layer_backward(
        matmul(d_hidden, proj_up), normed_two, lstd_two, gain_f[6]
    )
    d_mid = d_top + d_ln_two
    d_mid_b = d_mid.astype(bf16)
    g_out = contract(d_mid_b, attended_t, 0, 1)
    d_att_t = contract(proj_out, d_mid_b, 0, 1).astype(bf16)
    d_heads = swap(d_att_t, True, 6)
    d_heads_x = attention_backward(heads_x, log_total, d_heads, out_heads, pixel_ids)
    d_qkv_t = swap(d_heads_x, False, 7)
    g_qkv = matmul(d_qkv_t, ln_one_b)
    d_ln_one, g_ln1_g, g_ln1_b = layer_backward(
        contract(d_qkv_t, proj_qkv, 0, 0), normed_one, lstd_one, gain_f[4]
    )
    d_base = (d_mid + d_ln_one).astype(bf16)
    g_skip = left_product(d_base, joined)
    d_joined = matmul(d_base, skip_t)
    d_branch = d_joined[:, :C].astype(bf16)
    g_conv_two = left_product(cols_two, d_branch)
    d_branch = d_branch.reshape(height, n_cols, C)
    left, right = exchange(8, None, edges_of(d_branch))
    d_second = conv_backward(widen(d_branch, left, right), conv_b[1], masks_all).reshape(
        height, n_cols, C
    )
    d_pre_two = silu_pull(act_two[:, 1:-1], d_second)
    own_scale = film_col[1:-1, :C]
    d_scale = jnp.sum(d_pre_two * affine_two[:, 1:-1], axis=0)
    d_shift = jnp.sum(d_pre_two, axis=0)
    d_film = exact(clip_hot.T, jnp.concatenate([d_scale, d_shift], axis=1))
    g_film = exact(d_film.T, cond_act.astype(f32))
    d_inner, g_gn2_g, g_gn2_b = group_backward(
        d_pre_two * (1.0 + own_scale[None]),
        norm_two, std_two, gain_f[2], onehot, wide_hot, counts, 9, True,
    )
    d_inner_b = d_inner.astype(bf16)
    g_conv_one = left_product(cols_one, d_inner_b[:, 1:-1].reshape(n_pix, C))
    d_first = conv_backward(d_inner_b, conv_b[0], masks_all).reshape(height, n_cols, C)
    d_stem_gn, g_gn1_g, g_gn1_b = group_backward(
        silu_pull(act_one[:, 1:-1], d_first),
        norm_one, std_one, gain_f[0], onehot, wide_hot, counts, 10, False,
    )
    d_stem = (d_stem_gn.reshape(n_pix, C) + d_joined[:, :C] + d_joined[:, C:]).astype(bf16)
    g_stem = left_product(stem_cols, d_stem)
    pairs = n_dp // 2

    def shards_of(item):
        return item.reshape(pairs, 2, -1, item.shape[-1])

    def small_rows(item):
        flat = item.reshape(n_dp, -1)
        flat = jnp.pad(flat, ((0, 0), (0, round_up(flat.shape[1], 256) - flat.shape[1])))
        return flat.reshape(n_dp, -1, 256)

    g_gains = jnp.stack([g_gn1_g, g_gn1_b, g_gn2_g, g_gn2_b, g_ln1_g, g_ln1_b, g_ln2_g, g_ln2_b])
    smalls = [
        small_rows(g_head),
        small_rows(g_stem.reshape(-1, n_dp, C // n_dp).transpose(1, 0, 2)),
        small_rows(g_gains.reshape(-1, n_dp, C // n_dp).transpose(1, 0, 2)),
    ]
    small_at = [0]
    for item in smalls:
        small_at.append(small_at[-1] + item.shape[1])
    small_end = round_up(small_at[-1], 8)
    loss_rows = jnp.zeros((n_dp, 8 + small_end - small_at[-1], 256), jnp.float32)
    smalls.append(loss_rows.at[0, -8, 0].set(local_loss))
    small = jnp.concatenate(smalls, axis=1)
    g_proj = jnp.concatenate([g_qkv, g_out, g_up], axis=0)
    chunks = [
        [shards_of(g_conv_one)],
        [shards_of(g_conv_two)],
        [shards_of(g_proj)],
        [shards_of(g_film), shards_of(g_skip), shards_of(g_down), shards_of(small)],
    ]
    heights = [sum(item.shape[2] * item.shape[3] // 256 for item in parts) for parts in chunks]
    heights[3] -= 8
    shards, sums = reduce_grads(chunks, heights, 11)
    squares, loss_sum = sums[0, 1], sums[0, 0]
    grad_norm = jnp.sqrt(squares)
    factor = jnp.minimum(1.0, CLIP_NORM / grad_norm)
    conv_rows, film_cols = 9 * C // n_dp, 2 * C // n_dp
    skip_cols, down_rows = C // n_dp, 4 * C // n_dp
    last = shards[3]
    film_end, skip_end = 2 * film_cols, 2 * film_cols + 2 * skip_cols
    film_shard = jnp.concatenate([last[:film_cols], last[film_cols:film_end]], axis=1).T
    skip_shard = jnp.concatenate(
        [last[film_end : film_end + skip_cols], last[film_end + skip_cols : skip_end]], axis=1
    ).T
    small_shard = last[skip_end + down_rows :]

    def small_part(index, like):
        rows = small_shard[small_at[index] : small_at[index + 1]].reshape(-1)
        return rows[: like.size].reshape(like.shape)

    shards = (
        jnp.stack([shards[0][:conv_rows], shards[1][:conv_rows]]),
        shards[2][: proj_w.shape[1]].T,
        film_shard,
        skip_shard,
        last[skip_end : skip_end + down_rows],
        small_part(1, stem_w),
        small_part(0, head_w),
        small_part(2, gains),
    )
    new_w, new_m, new_v = ([], [], [])
    for weight, grad_one, m_old, v_old in zip(masters, shards, firsts, seconds):
        grad_one = grad_one * factor
        m_new = BETA_ONE * m_old + (1.0 - BETA_ONE) * grad_one
        v_new = BETA_TWO * v_old + (1.0 - BETA_TWO) * grad_one * grad_one
        step_dir = (
            m_new / (1.0 - BETA_ONE**STEP) / (jnp.sqrt(v_new / (1.0 - BETA_TWO**STEP)) + ADAM_EPS)
        )
        new_w.append(weight - RATE * (step_dir + DECAY * weight))
        new_m.append(m_new)
        new_v.append(v_new)
    return (
        new_w[0],
        new_w[1],
        new_w[2],
        new_w[3],
        new_w[4],
        new_w[5],
        new_w[6],
        new_w[7],
        new_m[0],
        new_m[1],
        new_m[2],
        new_m[3],
        new_m[4],
        new_m[5],
        new_m[6],
        new_m[7],
        new_v[0],
        new_v[1],
        new_v[2],
        new_v[3],
        new_v[4],
        new_v[5],
        new_v[6],
        new_v[7],
        grad_norm,
        loss_sum,
        pix_count,
    )


def solution(mesh):
    n_dp, n_s = mesh.shape["dp"], mesh.shape["section"]
    blocks = jax.sharding.Mesh(mesh.devices.reshape(n_dp // n_s, n_s, n_s), ("a", "b", "s"))
    return jax.shard_map(
        body,
        mesh=blocks,
        in_specs=(
            P(DP, None, "s", None),
            P(DP, None, "s", None),
            P(DP, None),
            P(DP, None),
            P(DP, None, None),
            P(None, DP, None),
            P(None, DP),
            P(None, DP),
            P(None, DP),
            P(DP, None),
            P(None, DP),
            P(DP, None),
            P(None, DP),
            P(None, DP, None),
            P(None, DP),
            P(None, DP),
            P(None, DP),
            P(DP, None),
            P(None, DP),
            P(DP, None),
            P(None, DP),
            P(None, DP, None),
            P(None, DP),
            P(None, DP),
            P(None, DP),
            P(DP, None),
            P(None, DP),
            P(DP, None),
            P(None, DP),
        ),
        out_specs=(
            P(None, DP, None),
            P(None, DP),
            P(None, DP),
            P(None, DP),
            P(DP, None),
            P(None, DP),
            P(DP, None),
            P(None, DP),
            P(None, DP, None),
            P(None, DP),
            P(None, DP),
            P(None, DP),
            P(DP, None),
            P(None, DP),
            P(DP, None),
            P(None, DP),
            P(None, DP, None),
            P(None, DP),
            P(None, DP),
            P(None, DP),
            P(DP, None),
            P(None, DP),
            P(DP, None),
            P(None, DP),
            P(),
            P(),
            P(),
        ),
        check_vma=False,
    )
```

time: 731 us -> 613 us (0.84); the launches traced: 728 us -> 602 us
  blocking collectives: 117 us -> 0 us
  Pallas kernels: 281 us -> 329 us
  starting transfers between devices: 47.3 us -> 0.12 us
  waiting for transfers between devices: 43 us -> 0.75 us
  local copies, waits for them, and re-layouts: 88.6 us -> 106 us
  matrix products: 76.4 us -> 85.7 us
    pallas_call x0 -> x11, Pallas kernels: none -> 109 us  [the longest x4 55.9 us: swap(): pl.pallas_call(functools.partial(swap_kernel, n_b, spread), in_specs=[pl....]
    psum x5 -> x0, blocking collectives: 60.3 us -> none  [the longest x2 25.2 us: group_backward(): sum_one, sum_two = lax.psum((sum_one, sum_two), 's')]
    all_gather x6 -> x0, blocking collectives: 56.3 us -> none  [the longest x1 10.6 us: body(): lax.all_gather(film_w.astype(bf16), DP, axis=1, tiled=True)]
    all_to_all x4 -> x0, waiting for transfers between devices: 34.9 us -> none  [the longest x1 33 us: body(): lax.all_to_all(qkv_rows.reshape(n_pix, section_size, HEADS // section_siz...]
    pallas_call x1, Pallas kernels: 118 us -> 84.1 us  [reduce_grads(): pl.pallas_call(functools.partial(reduce_kernel, n_a, n_x, n_s, [[None] *...]
    ppermute x14 -> x0, starting transfers between devices: 30.1 us -> none  [the longest x7 20.7 us: with_halo(): lax.ppermute(tail, axis, [(i, (i + 1) % count) for i in range(ends)])]
    all_to_all x4 -> x0, starting transfers between devices: 17.1 us -> none  [the longest x1 5.04 us: body(): lax.all_to_all(d_qkv_heads, 's', split_axis=0, concat_axis=1, tiled=True)]
    pallas_call x1, Pallas kernels: 63.6 us -> 47.8 us  [attention_forward(): pl.pallas_call(functools.partial(forward_kernel, heads, bq, bk), grid=(n_...]
  transfers between devices with their start and end apart: 20 -> 3, of which waited for: 5 -> 0; matrix products, arithmetic and copies ran while one was open for 15% -> 14% of each run, Pallas kernels for 0% -> 6%
where the time goes in v3:
time: 613 us; the launch traced here: 602 us
  Pallas kernels  329 us (54%)
  local copies, waits for them, and re-layouts  106 us (17%)
  matrix products  85.7 us (14%)
  other arithmetic  62 us (10%)
  between operations  18.4 us (3%)
    pallas_call x1, Pallas kernels, attention_backward(): pl.pallas_call(functools.partial(backward_kernel, heads, bq, bk), grid=(n...  88.2 us
    pallas_call x1, Pallas kernels, reduce_grads(): pl.pallas_call(functools.partial(reduce_kernel, n_a, n_x, n_s, [[None] *...  84.1 us
    pallas_call x4, Pallas kernels, swap(): pl.pallas_call(functools.partial(swap_kernel, n_b, spread), in_specs=[pl....  55.9 us
    pallas_call x1, Pallas kernels, attention_forward(): pl.pallas_call(functools.partial(forward_kernel, heads, bq, bk), grid=(n_...  47.8 us
    pallas_call x6, Pallas kernels, exchange(): pl.pallas_call(functools.partial(exchange_kernel, n_b, int(stats is not N...  32.1 us
    dot_general x11, matrix products, matmul(): return jnp.dot(lhs_mat, rhs_mat, preferred_element_type=jnp.float32)  26.8 us
    dot_general x7, matrix products, left_product(): lax.dot_general(lhs_mat, rhs_mat, (((0,), (0,)), ((), ())), preferred_ele...  26.3 us
    pallas_call x1, Pallas kernels, opening(): pl.pallas_call(functools.partial(opening_kernel, n_a, n_b, len(shards)),...  21 us
  transfers between devices with their start and end apart: 3, of which 0 were waited for; matrix products, arithmetic and copies ran while one was open for 14% of the time, Pallas kernels for 6%

profile of v3, /device:TPU:0, one launch (start us, length us, event | category | flops | bytes accessed | tf_op | source)
XLA Modules:
  0.0 601.7 jit_solution(9371540287336535058)
XLA Ops:
  26.6 21.0 %shard_map.484 = (f32[40,512]{1,0:T(8,128)}, f32[32,128]{1,0:T(8,128)}, f32[32,128]{1,0:T(8,128)}, bf16[512,512]{1,0:T(8,128)(2,1)}, bf16[256,512]{1,0:T(8,128)(...) custom-call(f32[40,512]{1,0:T(8,128)} %pad_maximum_fusion.11.refs_0_, f32[32,128]{1,0:T(8,128)} %pad.68.refs_1_, ...), custom_call_target="tpu_custom_call" | custom-call | tf_op jit(solution)/shard_map/pallas_call | solution.py:656
  60.7 6.5 %shard_map.485 = (f32[8,128]{1,0:T(8,128)}, f32[16,256]{1,0:T(8,128)}, f32[16,256]{1,0:T(8,128)}) custom-call(f32[8,128]{1,0:T(8,128)} %select_maximum_fusion.3.refs_0_, f32[16,256]{1,0:T(8,128)} %get-tuple-element.299.refs_1_, f32[16,256]{1,0:T(8,128)} %get-tuple-element.298.refs_2_), custom_call_target="tpu_custom_call" | custom-call | tf_op jit(solution)/shard_map/pallas_call | solution.py:540
  81.9 3.6 copy.400
  85.5 7.2 %copy.401 = bf16[2304,1024]{1,0:T(8,128)(2,1)} copy(bf16[2304,1024]{0,1:T(8,128)(2,1)} %bitcast.284) | data formatting | bytes 9437184 | tf_op jit(solution)/shard_map/dot_general | solution.py:36
  92.8 4.3 fusion.204
  100.3 5.7 shard_map.486
  120.7 6.7 %copy.431 = bf16[2304,1024]{1,0:T(8,128)(2,1)} copy(bf16[2304,1024]{0,1:T(8,128)(2,1)} %bitcast.282) | data formatting | bytes 9437184 | tf_op jit(solution)/shard_map/dot_general | solution.py:36
  127.4 3.8 fusion.8
  138.5 19.5 %shard_map.487.x_ref = bf16[192,4096]{1,0:T(8,128)(2,1)} custom-call(bf16[768,1024]{1,0:T(8,128)(2,1)} %convolution_convert_fusion.x_ref), custom_call_target="tpu_custom_call" | custom-call | tf_op jit(solution)/shard_map/pallas_call | solution.py:579
  158.0 47.8 %shard_map.488 = (bf16[64,4096]{1,0:T(8,128)(2,1)}, f32[16,4096]{1,0:T(8,128)}) custom-call(bf16[192,4096]{1,0:T(8,128)(2,1)} %shard_map.487.x_ref, s32[1,4096]{1,0:T(1,128)} %reshape.491.ids_ref), custom_call_target="tpu_custom_call" | custom-call | tf_op jit(solution)/shard_map/pallas_call | solution.py:157
  205.8 8.5 %shard_map.489 = bf16[256,1024]{1,0:T(8,128)(2,1)} custom-call(bf16[64,4096]{1,0:T(8,128)(2,1)} %get-tuple-element.78.x_ref.o_ref), custom_call_target="tpu_custom_call" | custom-call | tf_op jit(solution)/shard_map/pallas_call | solution.py:579
  223.1 4.9 shard_map.490
  245.6 4.9 fusion.82
  260.9 8.3 %shard_map.491.do_ref = bf16[64,4096]{1,0:T(8,128)(2,1)} custom-call(bf16[256,1024]{1,0:T(8,128)(2,1)} %convolution_convert_fusion.1.x_ref), custom_call_target="tpu_custom_call" | custom-call | tf_op jit(solution)/shard_map/pallas_call | solution.py:579
  269.2 88.2 %shard_map.492.x_ref = bf16[192,4096]{1,0:T(8,128)(2,1)} custom-call(bf16[192,4096]{1,0:T(8,128)(2,1)} %shard_map.487.x_ref, s32[1,4096]{1,0:T(1,128)} %reshape.491.ids_ref, bf16[64,4096]{1,0:T(8,128)(2,1)} %shard_map.491.do_ref, bf16[64,4096]{1,0:T(8,128)(2,1)} %get-tuple-element.78.x_ref.o_ref, f32[16,4096]{1,0:T(8,128)} %get-tuple-element.82.lse_ref), custom_call_target="tpu_custom_call" | custom-call | tf_op jit(solution)/shard_map/pallas_call | solution.py:252
  357.4 19.7 %shard_map.493 = bf16[768,1024]{1,0:T(8,128)(2,1)} custom-call(bf16[192,4096]{1,0:T(8,128)(2,1)} %shard_map.492.x_ref), custom_call_target="tpu_custom_call" | custom-call | tf_op jit(solution)/shard_map/pallas_call | solution.py:579
  385.7 4.8 shard_map.494
  405.3 5.3 shard_map.495
  421.1 3.6 multiply_reduce_fusion.4
  431.1 5.0 shard_map.496
  442.1 6.5 %convolution_bitcast_fusion = f32[2304,8]{1,0:T(8,128)} fusion(bf16[16,66,2304]{2,1,0:T(8,128)(2,1)} %copy-done, bf16[16,64,8]{1,2,0:T(8,128)(2,1)} %get-tuple-element.320), kind=kOutput, calls=%fused_computation.10 | convolution fusion | flops 38928384 | bytes 4956160 | tf_op jit(solution)/shard_map/dot_general | solution.py:36
  454.0 5.2 fusion.75.refs_1_
  477.2 5.2 fusion.230.refs_0_
  484.7 84.1 %shard_map.497 = (f32[288,256]{1,0:T(8,128)}, f32[288,256]{1,0:T(8,128)}, f32[256,256]{1,0:T(8,128)}, f32[352,256]{1,0:T(8,128)}, f32[8,256]{1,0:T(8,128)}) custom-call(f32[4,2,288,256]{3,2,1,0:T(8,128)} %fusion.230.refs_0_, f32[4,2,288,256]{3,2,1,0:T(8,128)} %fusion.75.refs_1_, f32[4,2,256,256]{3,2,1,0:T(8,128)} %bitcast.287, ...), custom_call_target="tpu_custom_call" | custom-call | tf_op jit(solution)/shard_map/pallas_call | solution.py:490
  (496 shorter events, 203.3 us)
Async XLA Ops:
  7.2 85.5 %all-gather.8.cloned.1.call-start = ((), (), s32[]{:S(2)}) async-start(), calls=%async_computation.1 | async-start | bytes 1327104 | tf_op jit(solution)/shard_map/all_gather | solution.py:788
  9.1 100.5 %all-gather.10.cloned.1.call-start = ((), (), s32[]{:S(2)}) async-start(), calls=%async_computation.2 | async-start | bytes 1327104 | tf_op jit(solution)/shard_map/all_gather | solution.py:788
  9.9 122.5 %all-gather.6.cloned.1.call-start = ((), (), s32[]{:S(2)}) async-start(), calls=%async_computation | async-start | bytes 1843200 | tf_op jit(solution)/shard_map/all_gather | solution.py:793
  49.6 57.4 %copy-start.88 = (s32[66]{0:T(128)}, s32[66]{0:T(128)S(1)}, u32[]{:S(2)}) copy-start(s32[66]{0:T(128)S(1)} %slice.512) | copy-start | bytes 796
  49.6 49.6 %copy-start.51 = (pred[66,5]{0,1:T(8,128)(4,1)}, pred[66,5]{0,1:T(8,128)(4,1)S(1)}, u32[]{:S(2)}) copy-start(pred[66,5]{0,1:T(8,128)(4,1)S(1)} %iota_compare_fusion.6) | copy-start | bytes 994
  57.7 73.5 %copy-start.33 = (bf16[1024,256]{1,0:T(8,128)(2,1)}, bf16[1024,256]{1,0:T(8,128)(2,1)S(1)}, u32[]{:S(2)}) copy-start(bf16[1024,256]{1,0:T(8,128)(2,1)S(1)} %get-tuple-element.332) | copy-start | bytes 1572868
  58.4 48.6 %copy-start.89 = (f32[5]{0:T(128)}, f32[5]{0:T(128)S(1)}, u32[]{:S(2)}) copy-start(f32[5]{0:T(128)S(1)} %multiply_maximum_fusion) | copy-start | bytes 64
  76.8 35.5 %copy-start.77 = (f32[256]{0:T(256)}, f32[256]{0:T(256)S(1)}, u32[]{:S(2)}) copy-start(f32[256]{0:T(256)S(1)} %get-tuple-element.255) | copy-start | bytes 3076
  131.8 26.2 %copy-start.55 = (f32[1024]{0:T(1024)}, f32[1024]{0:T(1024)S(1)}, u32[]{:S(2)}) copy-start(f32[1024]{0:T(1024)S(1)} %broadcast_multiply_fusion.6) | copy-start | bytes 12292
  132.3 25.6 %copy-start.59 = (f32[1024]{0:T(1024)}, f32[1024]{0:T(1024)S(1)}, u32[]{:S(2)}) copy-start(f32[1024]{0:T(1024)S(1)} %add_rsqrt_fusion.1) | copy-start | bytes 12292
  136.5 69.3 %copy-start.13 = (bf16[3,256,256]{2,1,0:T(8,128)(2,1)}, bf16[3,256,256]{2,1,0:T(8,128)(2,1)S(1)}, u32[]{:S(2)}) copy-start(bf16[3,256,256]{2,1,0:T(8,128)(2,1)S(1)} %slice.681) | copy-start | bytes 1179652
  260.9 116.2 %copy-start.14 = (bf16[3,256,256]{2,1,0:T(8,128)(2,1)S(1)}, bf16[3,256,256]{2,1,0:T(8,128)(2,1)}, u32[]{:S(2)}) copy-start(bf16[3,256,256]{2,1,0:T(8,128)(2,1)} %copy-done.13) | copy-start | bytes 1179652
  260.9 116.2 %copy-start.56 = (f32[1024]{0:T(1024)S(1)}, f32[1024]{0:T(1024)}, u32[]{:S(2)}) copy-start(f32[1024]{0:T(1024)} %copy-done.55) | copy-start | bytes 12292
  260.9 116.2 %copy-start.60 = (f32[1024]{0:T(1024)S(1)}, f32[1024]{0:T(1024)}, u32[]{:S(2)}) copy-start(f32[1024]{0:T(1024)} %copy-done.59) | copy-start | bytes 12292
  260.9 116.3 %copy-start.72 = (f32[256]{0:T(256)S(1)}, f32[256]{0:T(256)}, u32[]{:S(2)}) copy-start(f32[256]{0:T(256)} %get-tuple-element.253) | copy-start | bytes 3076
  357.4 23.1 %copy-start.76 = (f32[256]{0:T(256)S(1)}, f32[256]{0:T(256)}, u32[]{:S(2)}) copy-start(f32[256]{0:T(256)} %get-tuple-element.252) | copy-start | bytes 3076
  394.2 22.9 %copy-start.4 = (f32[16,66,256]{2,0,1:T(8,128)S(1)}, f32[16,66,256]{2,0,1:T(8,128)}, u32[]{:S(2)}) copy-start(f32[16,66,256]{2,0,1:T(8,128)} %get-tuple-element.290) | copy-start | bytes 3244036
  421.1 18.2 %copy-start.42 = (f32[16,66,8]{1,2,0:T(8,128)S(1)}, f32[16,66,8]{1,2,0:T(8,128)}, u32[]{:S(2)}) copy-start(f32[16,66,8]{1,2,0:T(8,128)} %get-tuple-element.284) | copy-start | bytes 101380
  454.0 17.3 %copy-start.44 = (f32[64,256]{1,0:T(8,128)S(1)}, f32[64,256]{1,0:T(8,128)}, u32[]{:S(2)}) copy-start(f32[64,256]{1,0:T(8,128)} %copy.434) | copy-start | bytes 196612
  484.7 91.9 %copy-start.25 = (f32[256,256]{0,1:T(8,128)S(1)}, f32[256,256]{0,1:T(8,128)}, u32[]{:S(2)}) copy-start(f32[256,256]{0,1:T(8,128)} %copy.445) | copy-start | bytes 786436
  484.7 91.9 %copy-start.26 = (f32[256,256]{0,1:T(8,128)S(1)}, f32[256,256]{0,1:T(8,128)}, u32[]{:S(2)}) copy-start(f32[256,256]{0,1:T(8,128)} %copy.446) | copy-start | bytes 786436
  568.9 23.5 %copy-start.8 = (f32[2,288,256]{2,1,0:T(8,128)S(1)}, f32[2,288,256]{2,1,0:T(8,128)}, u32[]{:S(2)}) copy-start(f32[2,288,256]{2,1,0:T(8,128)} %param.36) | copy-start | bytes 1769476
  568.9 23.5 %copy-start.31 = (f32[2,288,256]{2,1,0:T(8,128)S(1)}, f32[2,288,256]{2,1,0:T(8,128)}, u32[]{:S(2)}) copy-start(f32[2,288,256]{2,1,0:T(8,128)} %param.44) | copy-start | bytes 1769476
  568.9 23.5 %copy-start.32 = (f32[2,288,256]{2,1,0:T(8,128)S(1)}, f32[2,288,256]{2,1,0:T(8,128)}, u32[]{:S(2)}) copy-start(f32[2,288,256]{2,1,0:T(8,128)} %param.52) | copy-start | bytes 1769476
  (72 other events, 388.6 us)
Sparse Core Ops, SparseCore 0:
  10.5 30.9 all-gather.7
  43.9 26.3 all-gather.9
  72.8 25.9 all-gather.5
